TPU v7x, 1024 devices: a whole 4x4x32 slice. The times are simulated.
1024 devices in a mesh: blk: 256 (over y_lo, z, x), rep: 4 (over y_hi, core).
Axes of the slice: x: 4, y: 4 (y_hi: 2, y_lo: 2; y = y_hi * 2 + y_lo), z: 32, core: 2. Of those that a mesh axis runs over, the one named last changes fastest.
Arguments:
- images: bfloat16 [131072, 1152], P(('blk', 'rep')), may hold values from -0.5 to 0.5
- texts: bfloat16 [131072, 1152], P('blk'), may hold values from -0.5 to 0.5
- positive: int32 [131072], P(('blk', 'rep')), may hold values from 0 to 131071, as said below
- temp_log: float32 [1], replicated, may hold values from 2 to 2.7
- bias_arg: float32 [1], replicated, may hold values from -5 to -2.5
Outputs:
- loss: float32 [1], replicated
- image_grad: float32 [131072, 1152], P(('blk', 'rep'))
- text_grad: float32 [131072, 1152], P(('blk', 'rep'))
- temp_grad: float32 [1], replicated
- bias_grad: float32 [1], replicated
Inputs may be any that keep to these rules, and one draw needn't show every extreme that they name: `positive`: positive_i lies in a text shard whose index differs from i // 512 by at most 2 around the cycle of 256 shards.
All inputs are finite; a program needn't handle non-finite values.
Results may differ from a plain program's by a relative error of at most 0.0009.
Values may be sent and summed in bfloat16 or wider, within the bound.
No kernel may reach another device: no remote copies, remote signals or barrier semaphores. Data moves between devices by JAX's collectives and lax.ppermute only.
A program may use at most 32 MiB of HBM per device.

v0:
```python
import jax
import jax.numpy as jnp
from jax import lax
from jax.sharding import PartitionSpec as P

HALF = 2


EPS = 1e-06


def as_sent(value):

    def short(part):
        return part.astype(jnp.bfloat16) if part.dtype == jnp.float32 else part

    return jax.tree.map(short, value)


def shifted(value, axis, by):
    count = lax.axis_size(axis)
    return lax.ppermute(value, axis, [(i, (i + by) % count) for i in range(count)])


def normalize(values):
    full = values.astype(jnp.float32)
    factor = lax.rsqrt(jnp.sum(full * full, axis=-1, keepdims=True) + EPS)
    return (full * factor, factor)


def back_normal(unit_f, factor, dunit):
    return factor * (dunit - unit_f * jnp.sum(unit_f * dunit, axis=-1, keepdims=True))


def block_terms(image_unit, text_unit, positive_rows, leading_shard, logit_scale, logit_bias):
    similarity = jnp.dot(image_unit, text_unit.T, preferred_element_type=jnp.float32)
    logit = logit_scale * similarity + logit_bias
    cols = leading_shard + jnp.arange(text_unit.shape[0], dtype=jnp.int32)
    sign = jnp.where(positive_rows[:, None] == cols[None, :], 1.0, -1.0).astype(jnp.float32)
    summed = jnp.sum(jax.nn.softplus(-sign * logit))
    grads = -sign * jax.nn.sigmoid(-sign * logit)
    global_batch = grads.astype(jnp.bfloat16)
    dx = jnp.dot(global_batch, text_unit, preferred_element_type=jnp.float32)
    text_grad_rows = jnp.dot(global_batch.T, image_unit, preferred_element_type=jnp.float32)
    return (summed, jnp.sum(grads), jnp.sum(grads * similarity), dx, text_grad_rows)


def per_device(images, texts, positive, temp_log, bias_arg):
    my_shard = lax.axis_index("blk")
    shard_rows = texts.shape[0]
    logit_scale = jnp.exp(temp_log[0])
    logit_bias = bias_arg[0]
    image_float, xfac = normalize(images)
    yf, yfac = normalize(texts)
    image_unit = image_float.astype(jnp.bfloat16)
    text_unit = yf.astype(jnp.bfloat16)
    first_col = my_shard * shard_rows

    def send_images(carried_bundle, by):
        moved = shifted((carried_bundle[0], as_sent(carried_bundle[1])), "blk", by)
        return (moved[0], moved[1])

    carried_bundle = (image_unit, positive)
    zero = jnp.zeros((), jnp.float32)
    totals = (zero, zero, zero, jnp.zeros(texts.shape, jnp.float32))
    start = send_images(carried_bundle, -HALF)
    carried_bundle = start
    offset = HALF
    count = 2 * HALF + 1
    visit_totals = totals
    carried = None
    for turn in range(count):
        if turn > 0:
            carried_bundle = send_images(carried_bundle, 1)
            offset = offset - 1
            carried = shifted(carried, "blk", 1)
        loss_part, g_part, t_part, dx_part, dy_part = block_terms(
            carried_bundle[0], text_unit, carried_bundle[1], first_col, logit_scale, logit_bias
        )
        visit_totals = (
            visit_totals[0] + loss_part,
            visit_totals[1] + g_part,
            visit_totals[2] + t_part,
            visit_totals[3] + dy_part,
        )
        carried = dx_part if carried is None else carried + dx_part
    returned = shifted(carried, "blk", offset)
    returned, totals = (returned, visit_totals)
    share = lax.psum_scatter(totals[3], "rep", scatter_dimension=0, tiled=True)
    share_rows = share.shape[0]
    rep_pos = lax.axis_index("rep")
    mine_f = lax.dynamic_slice_in_dim(yf, rep_pos * share_rows, share_rows, 0)
    mine_fac = lax.dynamic_slice_in_dim(yfac, rep_pos * share_rows, share_rows, 0)
    text_grad = back_normal(mine_f, mine_fac, logit_scale * share)
    summed, gsum, tsum = lax.psum((totals[0], totals[1], totals[2]), ("blk", "rep"))
    image_grad = back_normal(image_float, xfac, logit_scale * returned)
    batch = images.shape[0] * lax.axis_size("blk") * lax.axis_size("rep")
    loss = (summed / batch).reshape(1)
    return (loss, image_grad, text_grad, (logit_scale * tsum).reshape(1), gsum.reshape(1))


def solution(mesh):
    placed = (P(("blk", "rep"), None), P("blk", None), P(("blk", "rep")), P(), P())
    return jax.shard_map(
        per_device,
        mesh=mesh,
        in_specs=placed,
        out_specs=(P(), P(("blk", "rep"), None), P(("blk", "rep"), None), P(), P()),
        check_vma=False,
    )
```

profile of v0, /device:TPU:1, one launch (start us, length us, event | category | flops | bytes accessed | tf_op | source)
XLA Modules:
  0.0 373.0 jit_solution(15660135532552019873)
XLA Ops:
  7.2 22.8 %collective-permute-start = (s32[128]{0:T(128)}, s32[128]{0:T(128)S(1)}, u32[]{:S(2)}, u32[]{:S(2)}) collective-permute-start(s32[128]{0:T(128)} %param.7), channel_id=1, source_target_pairs={{0,1016},{4,1020},{8,0},{12,4},{16,8},{20,12},{24,16},{28,20},{32,... | collective-permute-start | bytes 1544 | tf_op jit(solution)/shard_map/ppermute | solution.py:22
  32.3 2.1 collective-permute-start.1
  34.4 3.1 collective-permute-start.2
  37.5 1.6 fusion
  39.1 3.8 %collective-permute-done.2 = s32[128]{0:T(128)S(1)} collective-permute-done((s32[128]{0:T(128)S(1)}, s32[128]{0:T(128)S(1)}, u32[]{:S(2)}, u32[]{:S(2)}) %collective-permute-start.2) | collective-permute-done | bytes 544 | tf_op jit(solution)/shard_map/ppermute | solution.py:22
  42.9 1.9 collective-permute-start.4
  44.9 6.6 %collective-permute-done.4 = s32[128]{0:T(128)S(1)} collective-permute-done((s32[128]{0:T(128)S(1)}, s32[128]{0:T(128)S(1)}, u32[]{:S(2)}, u32[]{:S(2)}) %collective-permute-start.4) | collective-permute-done | bytes 544 | tf_op jit(solution)/shard_map/ppermute | solution.py:22
  51.4 1.9 collective-permute-start.6
  54.7 5.2 %collective-permute-done.6 = s32[128]{0:T(128)S(1)} collective-permute-done((s32[128]{0:T(128)S(1)}, s32[128]{0:T(128)S(1)}, u32[]{:S(2)}, u32[]{:S(2)}) %collective-permute-start.6) | collective-permute-done | bytes 544 | tf_op jit(solution)/shard_map/ppermute | solution.py:22
  59.9 1.9 collective-permute-start.8
  61.8 1.9 fusion.56
  64.3 1.9 collective-permute-start.10
  66.2 1.9 collective-permute-start.3
  68.8 18.1 %collective-permute-done.3 = bf16[128,1152]{1,0:T(8,128)(2,1)S(1)} collective-permute-done((bf16[128,1152]{1,0:T(8,128)(2,1)S(1)}, bf16[128,1152]{1,0:T(8,128)(2,1)S(1)}, u32[]{:S(2)}, u32[]{:S(2)}) %collective-permute-start.3) | collective-permute-done | bytes 294944 | tf_op jit(solution)/shard_map/ppermute | solution.py:22
  87.5 1.9 collective-permute-start.5
  90.0 9.1 %collective-permute-done.5 = bf16[128,1152]{1,0:T(8,128)(2,1)S(1)} collective-permute-done((bf16[128,1152]{1,0:T(8,128)(2,1)S(1)}, bf16[128,1152]{1,0:T(8,128)(2,1)S(1)}, u32[]{:S(2)}, u32[]{:S(2)}) %collective-permute-start.5) | collective-permute-done | bytes 294944 | tf_op jit(solution)/shard_map/ppermute | solution.py:22
  99.8 1.9 collective-permute-start.7
  102.3 9.1 %collective-permute-done.7 = bf16[128,1152]{1,0:T(8,128)(2,1)S(1)} collective-permute-done((bf16[128,1152]{1,0:T(8,128)(2,1)S(1)}, bf16[128,1152]{1,0:T(8,128)(2,1)S(1)}, u32[]{:S(2)}, u32[]{:S(2)}) %collective-permute-start.7) | collective-permute-done | bytes 294944 | tf_op jit(solution)/shard_map/ppermute | solution.py:22
  112.0 1.9 collective-permute-start.9
  114.6 9.1 %collective-permute-done.9 = bf16[128,1152]{1,0:T(8,128)(2,1)S(1)} collective-permute-done((bf16[128,1152]{1,0:T(8,128)(2,1)S(1)}, bf16[128,1152]{1,0:T(8,128)(2,1)S(1)}, u32[]{:S(2)}, u32[]{:S(2)}) %collective-permute-start.9) | collective-permute-done | bytes 294944 | tf_op jit(solution)/shard_map/ppermute | solution.py:22
  123.7 2.4 fusion.42
  126.2 2.0 convolution_add_fusion
  128.8 1.9 collective-permute-start.11
  130.7 12.9 %collective-permute-done.11 = f32[128,1152]{1,0:T(8,128)S(1)} collective-permute-done((f32[128,1152]{1,0:T(8,128)S(1)}, f32[128,1152]{1,0:T(8,128)S(1)}, u32[]{:S(2)}, u32[]{:S(2)}) %collective-permute-start.11) | collective-permute-done | bytes 589856 | tf_op jit(solution)/shard_map/ppermute | solution.py:22
  144.2 1.9 collective-permute-start.12
  146.2 13.3 %collective-permute-done.12 = f32[128,1152]{1,0:T(8,128)S(1)} collective-permute-done((f32[128,1152]{1,0:T(8,128)S(1)}, f32[128,1152]{1,0:T(8,128)S(1)}, u32[]{:S(2)}, u32[]{:S(2)}) %collective-permute-start.12) | collective-permute-done | bytes 589856 | tf_op jit(solution)/shard_map/ppermute | solution.py:22
  160.0 1.9 collective-permute-start.13
  162.1 14.3 %collective-permute-done.13 = f32[128,1152]{1,0:T(8,128)S(1)} collective-permute-done((f32[128,1152]{1,0:T(8,128)S(1)}, f32[128,1152]{1,0:T(8,128)S(1)}, u32[]{:S(2)}, u32[]{:S(2)}) %collective-permute-start.13) | collective-permute-done | bytes 589856 | tf_op jit(solution)/shard_map/ppermute | solution.py:22
  177.8 1.9 collective-permute-start.14
  189.2 166.6 %all-reduce = (f32[]{:T(128)}, f32[]{:T(128)}, f32[1]{0:T(128)}) all-reduce(f32[]{:T(128)S(6)} %add.190, f32[]{:T(128)S(6)} %add.208, f32[1]{0:T(128)} %bitcast.4), channel_id=1, replica_groups=mesh['blk'=256,'rep'=4] {'blk','rep'}, use_global_device_ids=true, to_apply=%region_7.8 | all-reduce | flops 3 | bytes 24 | tf_op jit(solution)/shard_map/psum | solution.py:95
  358.5 2.2 fusion.6
  361.9 2.0 subtract_multiply_fusion
  (31 shorter events, 13.1 us)
Async XLA Ops:
  7.2 56.5 %copy-start = (bf16[512,1152]{1,0:T(8,128)(2,1)S(1)}, bf16[512,1152]{1,0:T(8,128)(2,1)}, u32[]{:S(2)}) copy-start(bf16[512,1152]{1,0:T(8,128)(2,1)} %param.6) | copy-start | bytes 3538948
  7.2 353.5 %reduce-scatter.2.cloned.1.call-start = ((), (), s32[]{:S(2)}) async-start(), calls=%async_computation.1 | async-start | bytes 2949120 | tf_op jit(solution)/shard_map/reduce_scatter | solution.py:89
  7.2 27.2 %collective-permute-start = (s32[128]{0:T(128)}, s32[128]{0:T(128)S(1)}, u32[]{:S(2)}, u32[]{:S(2)}) collective-permute-start(s32[128]{0:T(128)} %param.7), channel_id=1, source_target_pairs={{0,1016},{4,1020},{8,0},{12,4},{16,8},{20,12},{24,16},{28,20},{32,... | collective-permute-start | bytes 1544 | tf_op jit(solution)/shard_map/ppermute | solution.py:22
  32.3 29.6 %collective-permute-start.1 = (bf16[128,1152]{1,0:T(8,128)(2,1)S(1)}, bf16[128,1152]{1,0:T(8,128)(2,1)S(1)}, u32[]{:S(2)}, u32[]{:S(2)}) collective-permute-start(bf16[128,1152]{1,0:T(8,128)(2,1)S(1)} %fusion.3), channel_id=1, source_target_pairs={{0,1016},{4,1020},{8,0},{12,4},{16,8},{20,12},{24,16},{28,20},{32,... | collective-permute-start | bytes 884744 | tf_op jit(solution)/shard_map/ppermute | solution.py:22
  34.4 8.5 %collective-permute-start.2 = (s32[128]{0:T(128)S(1)}, s32[128]{0:T(128)S(1)}, u32[]{:S(2)}, u32[]{:S(2)}) collective-permute-start(s32[128]{0:T(128)S(1)} %collective-permute-done), channel_id=1, source_target_pairs={{0,4},{4,8},{8,12},{12,16},{16,20},{20,24},{24,28},{28,32},{32,36}... | collective-permute-start | bytes 1544 | tf_op jit(solution)/shard_map/ppermute | solution.py:22
  42.9 8.5 %collective-permute-start.4 = (s32[128]{0:T(128)S(1)}, s32[128]{0:T(128)S(1)}, u32[]{:S(2)}, u32[]{:S(2)}) collective-permute-start(s32[128]{0:T(128)S(1)} %collective-permute-done.2), channel_id=1, source_target_pairs={{0,4},{4,8},{8,12},{12,16},{16,20},{20,24},{24,28},{28,32},{32,36}... | collective-permute-start | bytes 1544 | tf_op jit(solution)/shard_map/ppermute | solution.py:22
  51.4 8.5 %collective-permute-start.6 = (s32[128]{0:T(128)S(1)}, s32[128]{0:T(128)S(1)}, u32[]{:S(2)}, u32[]{:S(2)}) collective-permute-start(s32[128]{0:T(128)S(1)} %collective-permute-done.4), channel_id=1, source_target_pairs={{0,4},{4,8},{8,12},{12,16},{16,20},{20,24},{24,28},{28,32},{32,36}... | collective-permute-start | bytes 1544 | tf_op jit(solution)/shard_map/ppermute | solution.py:22
  59.9 54.7 %collective-permute-start.8 = (s32[128]{0:T(128)S(1)}, s32[128]{0:T(128)S(1)}, u32[]{:S(2)}, u32[]{:S(2)}) collective-permute-start(s32[128]{0:T(128)S(1)} %collective-permute-done.6), channel_id=1, source_target_pairs={{0,4},{4,8},{8,12},{12,16},{16,20},{20,24},{24,28},{28,32},{32,36}... | collective-permute-start | bytes 1544 | tf_op jit(solution)/shard_map/ppermute | solution.py:22
  64.3 64.0 %collective-permute-start.10 = (f32[128,1152]{1,0:T(8,128)S(1)}, f32[128,1152]{1,0:T(8,128)S(1)}, u32[]{:S(2)}, u32[]{:S(2)}) collective-permute-start(f32[128,1152]{1,0:T(8,128)S(1)} %fusion.35), channel_id=1, source_target_pairs={{0,4},{4,8},{8,12},{12,16},{16,20},{20,24},{24,28},{28,32},{32,36}... | collective-permute-start | bytes 1769480 | tf_op jit(solution)/shard_map/ppermute | solution.py:22
  66.2 20.7 %collective-permute-start.3 = (bf16[128,1152]{1,0:T(8,128)(2,1)S(1)}, bf16[128,1152]{1,0:T(8,128)(2,1)S(1)}, u32[]{:S(2)}, u32[]{:S(2)}) collective-permute-start(bf16[128,1152]{1,0:T(8,128)(2,1)S(1)} %collective-permute-done.1), channel_id=1, source_target_pairs={{0,4},{4,8},{8,12},{12,16},{16,20},{20,24},{24,28},{28,32},{32,36}... | collective-permute-start | bytes 884744 | tf_op jit(solution)/shard_map/ppermute | solution.py:22
  87.5 11.7 %collective-permute-start.5 = (bf16[128,1152]{1,0:T(8,128)(2,1)S(1)}, bf16[128,1152]{1,0:T(8,128)(2,1)S(1)}, u32[]{:S(2)}, u32[]{:S(2)}) collective-permute-start(bf16[128,1152]{1,0:T(8,128)(2,1)S(1)} %collective-permute-done.3), channel_id=1, source_target_pairs={{0,4},{4,8},{8,12},{12,16},{16,20},{20,24},{24,28},{28,32},{32,36}... | collective-permute-start | bytes 884744 | tf_op jit(solution)/shard_map/ppermute | solution.py:22
  99.8 11.7 %collective-permute-start.7 = (bf16[128,1152]{1,0:T(8,128)(2,1)S(1)}, bf16[128,1152]{1,0:T(8,128)(2,1)S(1)}, u32[]{:S(2)}, u32[]{:S(2)}) collective-permute-start(bf16[128,1152]{1,0:T(8,128)(2,1)S(1)} %collective-permute-done.5), channel_id=1, source_target_pairs={{0,4},{4,8},{8,12},{12,16},{16,20},{20,24},{24,28},{28,32},{32,36}... | collective-permute-start | bytes 884744 | tf_op jit(solution)/shard_map/ppermute | solution.py:22
  112.0 11.7 %collective-permute-start.9 = (bf16[128,1152]{1,0:T(8,128)(2,1)S(1)}, bf16[128,1152]{1,0:T(8,128)(2,1)S(1)}, u32[]{:S(2)}, u32[]{:S(2)}) collective-permute-start(bf16[128,1152]{1,0:T(8,128)(2,1)S(1)} %collective-permute-done.7), channel_id=1, source_target_pairs={{0,4},{4,8},{8,12},{12,16},{16,20},{20,24},{24,28},{28,32},{32,36}... | collective-permute-start | bytes 884744 | tf_op jit(solution)/shard_map/ppermute | solution.py:22
  128.8 14.8 %collective-permute-start.11 = (f32[128,1152]{1,0:T(8,128)S(1)}, f32[128,1152]{1,0:T(8,128)S(1)}, u32[]{:S(2)}, u32[]{:S(2)}) collective-permute-start(f32[128,1152]{1,0:T(8,128)S(1)} %convolution_add_fusion.4), channel_id=1, source_target_pairs={{0,4},{4,8},{8,12},{12,16},{16,20},{20,24},{24,28},{28,32},{32,36}... | collective-permute-start | bytes 1769480 | tf_op jit(solution)/shard_map/ppermute | solution.py:22
  144.2 15.3 %collective-permute-start.12 = (f32[128,1152]{1,0:T(8,128)S(1)}, f32[128,1152]{1,0:T(8,128)S(1)}, u32[]{:S(2)}, u32[]{:S(2)}) collective-permute-start(f32[128,1152]{1,0:T(8,128)S(1)} %fusion.28), channel_id=1, source_target_pairs={{0,4},{4,8},{8,12},{12,16},{16,20},{20,24},{24,28},{28,32},{32,36}... | collective-permute-start | bytes 1769480 | tf_op jit(solution)/shard_map/ppermute | solution.py:22
  160.0 16.4 %collective-permute-start.13 = (f32[128,1152]{1,0:T(8,128)S(1)}, f32[128,1152]{1,0:T(8,128)S(1)}, u32[]{:S(2)}, u32[]{:S(2)}) collective-permute-start(f32[128,1152]{1,0:T(8,128)S(1)} %fusion.22), channel_id=1, source_target_pairs={{0,4},{4,8},{8,12},{12,16},{16,20},{20,24},{24,28},{28,32},{32,36}... | collective-permute-start | bytes 1769480 | tf_op jit(solution)/shard_map/ppermute | solution.py:22
  177.8 179.3 %collective-permute-start.14 = (f32[128,1152]{1,0:T(8,128)}, f32[128,1152]{1,0:T(8,128)}, u32[]{:S(2)}, u32[]{:S(2)}) collective-permute-start(f32[128,1152]{1,0:T(8,128)} %fusion.16), channel_id=1, source_target_pairs={{0,1016},{4,1020},{8,0},{12,4},{16,8},{20,12},{24,16},{28,20},{32,... | collective-permute-start | bytes 1769480 | tf_op jit(solution)/shard_map/ppermute | solution.py:22
Sparse Core Ops, SparseCore 0:
  128.4 71.7 reduce-scatter.1
where the time goes:
time: 374 us; the launch traced here: 373 us
  blocking collectives  167 us (45%)
  waiting for transfers between devices  102 us (27%)
  starting transfers between devices  51.1 us (14%)
  between operations  28.5 us (8%)
  matrix products  14.3 us (4%)
  other arithmetic  10.8 us (3%)
    psum x1, blocking collectives, per_device(): lax.psum((totals[0], totals[1], totals[2]), ('blk', 'rep'))  167 us
    ppermute x15, waiting for transfers between devices, shifted(): lax.ppermute(value, axis, [(i, (i + by) % count) for i in range(count)])  102 us
    ppermute x15, starting transfers between devices, shifted(): lax.ppermute(value, axis, [(i, (i + by) % count) for i in range(count)])  51.1 us
  transfers between devices with their start and end apart: 16, of which 10 were waited for; matrix products, arithmetic and copies ran while one was open for 6% of the time, Pallas kernels for 0%

commit v1 on v0

v1 whole, which is shorter than its diff:
```python
import jax
import jax.numpy as jnp
from jax import lax
from jax.experimental import pallas as pl
from jax.experimental.pallas import tpu as pltpu
from jax.sharding import Mesh, PartitionSpec as P

EPS = 1e-06
BLK = ("y_lo", "z", "x")
PLANE = ("y_lo", "x", "y_hi", "core")
SIZES = (2, 32, 4, 2, 2)
WIDTH = 1152
IMAGES = 128
TEXTS = 512
PAD_ROWS = 16
PACKED = IMAGES + PAD_ROWS
BATCH = 131072
RING = 32
F32 = jnp.float32
BF16 = jnp.bfloat16


def shape(*dims, dtype=F32):
    return jax.ShapeDtypeStruct(dims, dtype)


def call(body, outs, *args, flops=0, smem_in=(), smem_out=()):
    moved = sum(a.size * a.dtype.itemsize for a in args)
    moved += sum(o.size * o.dtype.itemsize for o in outs)
    scalar = pl.BlockSpec(memory_space=pltpu.SMEM)
    vector = pl.BlockSpec(memory_space=pltpu.VMEM)
    return pl.pallas_call(
        body,
        out_shape=outs,
        in_specs=[scalar if k in smem_in else vector for k in range(len(args))],
        out_specs=[scalar if k in smem_out else vector for k in range(len(outs))],
        compiler_params=pltpu.CompilerParams(vmem_limit_bytes=20 * 1024 * 1024),
        cost_estimate=pl.CostEstimate(flops=flops, bytes_accessed=moved, transcendentals=0),
    )(*args)


def shifted(value, by):
    count = lax.axis_size(BLK)
    return lax.ppermute(value, BLK, [(i, (i + by) % count) for i in range(count)])


def swapped(value, axis):
    return lax.ppermute(value, axis, [(0, 1), (1, 0)])


def normalized(values):
    full = values.astype(F32)
    factor = lax.rsqrt(jnp.sum(full * full, axis=-1, keepdims=True) + EPS)
    return full * factor, factor


def back_normal(unit_f, factor, dunit):
    return factor * (dunit - unit_f * jnp.sum(unit_f * dunit, axis=-1, keepdims=True))


def pack_kernel(images_ref, positive_ref, out_ref):
    unit, _ = normalized(images_ref[...])
    out_ref[:IMAGES, :] = unit.astype(BF16)
    pos = positive_ref[...]
    row = lax.broadcasted_iota(jnp.int32, (PAD_ROWS, IMAGES), 0)
    digit = jnp.where(row == 0, pos >> 12, jnp.where(row == 1, (pos >> 6) & 63, pos & 63))
    out_ref[IMAGES:, :] = jnp.zeros((PAD_ROWS, WIDTH), BF16)
    out_ref[IMAGES:, :IMAGES] = digit.astype(F32).astype(BF16)


def pair_block(packed_ref, text_unit, place_ref, temp_ref, bias_ref):
    unit = packed_ref[:IMAGES, :]
    digits = packed_ref[IMAGES:, :IMAGES].astype(F32).astype(jnp.int32)
    row = lax.broadcasted_iota(jnp.int32, (PAD_ROWS, IMAGES), 0)
    weight = jnp.where(row == 0, 4096, jnp.where(row == 1, 64, jnp.where(row == 2, 1, 0)))
    pos = jnp.sum(digits * weight, axis=0, keepdims=True) - place_ref[0]
    sim = lax.dot_general(text_unit, unit, (((1,), (1,)), ((), ())), preferred_element_type=F32)
    scale = jnp.exp(jnp.full((1, IMAGES), temp_ref[0], F32))
    logit = scale * sim + bias_ref[0]
    matching = lax.broadcasted_iota(jnp.int32, (TEXTS, IMAGES), 0) == pos
    against = jnp.where(matching, -logit, logit)
    small = jnp.exp(-jnp.abs(against))
    soft = jnp.maximum(against, 0.0) + jnp.log1p(small)
    sigmoid = jnp.where(against >= 0, 1.0, small) / (1.0 + small)
    grads = jnp.where(matching, -sigmoid, sigmoid)
    rounded = grads.astype(BF16)
    image_part = lax.dot_general(rounded, text_unit, (((0,), (0,)), ((), ())), preferred_element_type=F32)
    sums = [jnp.sum(v, axis=0, keepdims=True) for v in (soft, grads, grads * sim)]
    return image_part, rounded, sums


def sums_tile(sums):
    return jnp.concatenate(sums + [jnp.zeros((5, IMAGES), F32)], axis=0)


def own_kernel(texts_ref, packed_ref, place_ref, temp_ref, bias_ref, text_ref, dx_ref, grads_ref, sums_ref):
    unit, _ = normalized(texts_ref[...])
    text_ref[...] = unit.astype(BF16)
    dx_ref[...], grads_ref[...], sums = pair_block(packed_ref, text_ref[...], place_ref, temp_ref, bias_ref)
    sums_ref[...] = sums_tile(sums)


def near_kernel(text_ref, left_ref, right_ref, place_ref, temp_ref, bias_ref, dxl_ref, dxr_ref, grads_ref, sums_ref):
    text_unit = text_ref[...]
    dxl_ref[...], grads_ref[:, :IMAGES], first = pair_block(left_ref, text_unit, place_ref, temp_ref, bias_ref)
    dxr_ref[...], grads_ref[:, IMAGES:], second = pair_block(right_ref, text_unit, place_ref, temp_ref, bias_ref)
    sums_ref[...] = sums_tile([a + b for a, b in zip(first, second)])


def far_kernel(text_ref, left_ref, right_ref, place_ref, temp_ref, bias_ref, own_ref, near_ref,
               dxl_ref, dxr_ref, grads_ref, row_ref):
    text_unit = text_ref[...]
    dxl_ref[...], grads_ref[:, :IMAGES], first = pair_block(left_ref, text_unit, place_ref, temp_ref, bias_ref)
    dxr_ref[...], grads_ref[:, IMAGES:], second = pair_block(right_ref, text_unit, place_ref, temp_ref, bias_ref)
    tile = sums_tile([a + b for a, b in zip(first, second)]) + own_ref[...] + near_ref[...]
    totals = jnp.sum(tile, axis=1, keepdims=True)
    lane = lax.broadcasted_iota(jnp.int32, (1, IMAGES), 1)
    row = sum(jnp.where(lane == k, totals[k:k + 1], 0.0) for k in range(3))
    row_ref[...] = jnp.broadcast_to(row[None], (RING, 1, IMAGES))


def text_part_kernel(place_ref, g0, g1, g2, x0, x1l, x1r, x2l, x2r, send_ref, keep_ref):
    core = place_ref[2]
    blocks = ((g0, 0, x0), (g1, 0, x1l), (g1, 1, x1r), (g2, 0, x2l), (g2, 1, x2r))
    for out_ref, owner in ((send_ref, 1 - core), (keep_ref, core)):
        for half in range(2):
            first = pl.multiple_of((2 * half + owner) * IMAGES, IMAGES)
            total = None
            for grads, k, unit in blocks:
                part = jnp.dot(
                    grads[pl.ds(first, IMAGES), k * IMAGES:(k + 1) * IMAGES],
                    unit[:IMAGES, :],
                    preferred_element_type=F32,
                )
                total = part if total is None else total + part
            out_ref[half] = total


def halve_kernel(place_ref, keep_ref, got_ref, send_ref, rest_ref):
    mine = place_ref[1]
    send_ref[...] = keep_ref[1 - mine] + got_ref[1 - mine]
    rest_ref[...] = keep_ref[mine] + got_ref[mine]


def text_end_kernel(place_ref, temp_ref, texts_ref, rest_ref, got_ref, out_ref):
    first = pl.multiple_of((2 * place_ref[1] + place_ref[2]) * IMAGES, IMAGES)
    unit, factor = normalized(texts_ref[pl.ds(first, IMAGES), :])
    scale = jnp.exp(jnp.full((1, WIDTH), temp_ref[0], F32))
    out_ref[...] = back_normal(unit, factor, scale * (rest_ref[...] + got_ref[...]))


def image_end_kernel(temp_ref, images_ref, d0, d1, d2, d3, d4, out_ref):
    unit, factor = normalized(images_ref[...])
    scale = jnp.exp(jnp.full((1, WIDTH), temp_ref[0], F32))
    total = (d0[...] + d1[...] + d2[...]) + (d3[...] + d4[...])
    out_ref[...] = back_normal(unit, factor, scale * total)


def again_kernel(row_ref, out_ref):
    total = jnp.sum(row_ref[...], axis=0, keepdims=True)
    out_ref[...] = jnp.broadcast_to(total, out_ref.shape)


def sums_end_kernel(temp_ref, row_ref, loss_ref, temp_grad_ref, bias_grad_ref):
    total = jnp.sum(row_ref[...], axis=0)
    lane = lax.broadcasted_iota(jnp.int32, (1, IMAGES), 1)
    scale = jnp.exp(jnp.full((1, IMAGES), temp_ref[0], F32))
    loss_ref[0] = jnp.sum(jnp.where(lane == 0, total, 0.0)) * (1.0 / BATCH)
    bias_grad_ref[0] = jnp.sum(jnp.where(lane == 1, total, 0.0))
    temp_grad_ref[0] = jnp.sum(jnp.where(lane == 2, total * scale, 0.0))


def per_device(images, texts, positive, temp_log, bias_arg):
    place = jnp.stack([lax.axis_index(BLK) * TEXTS, lax.axis_index("y_hi"), lax.axis_index("core")]).astype(jnp.int32)
    block_flops = 4 * TEXTS * IMAGES * WIDTH
    (mine,) = call(pack_kernel, [shape(PACKED, WIDTH, dtype=BF16)], images, positive.reshape(1, IMAGES))
    left = shifted(mine, 1)
    right = shifted(mine, -1)
    text_unit, dx0, g0, sums0 = call(
        own_kernel,
        [shape(TEXTS, WIDTH, dtype=BF16), shape(IMAGES, WIDTH), shape(TEXTS, IMAGES, dtype=BF16), shape(8, IMAGES)],
        texts, mine, place, temp_log, bias_arg, flops=block_flops, smem_in=(2, 3, 4),
    )
    left, right, text_unit = lax.optimization_barrier((left, right, text_unit))
    left2 = shifted(left, 1)
    right2 = shifted(right, -1)
    pair_outs = [shape(IMAGES, WIDTH), shape(IMAGES, WIDTH), shape(TEXTS, 2 * IMAGES, dtype=BF16)]
    dxl, dxr, g1, sums1 = call(
        near_kernel, pair_outs + [shape(8, IMAGES)],
        text_unit, left, right, place, temp_log, bias_arg, flops=2 * block_flops, smem_in=(3, 4, 5),
    )
    dxl2, dxr2, g2, row = call(
        far_kernel, pair_outs + [shape(RING, 1, IMAGES)],
        text_unit, left2, right2, place, temp_log, bias_arg, sums0, sums1,
        flops=2 * block_flops, smem_in=(3, 4, 5),
    )
    parts = [shifted(dxl, -1), shifted(dxr, 1), shifted(dxl2, -2), shifted(dxr2, 2)]
    row = lax.all_to_all(row, PLANE, 0, 0, tiled=True)
    send, keep = call(
        text_part_kernel, [shape(2, IMAGES, WIDTH), shape(2, IMAGES, WIDTH)],
        place, g0, g1, g2, mine, left, right, left2, right2, flops=10 * TEXTS * IMAGES * WIDTH, smem_in=(0,),
    )
    got = swapped(send, "core")
    (row,) = call(again_kernel, [shape(RING, 1, IMAGES)], row)
    row, got = lax.optimization_barrier((row, got))
    row = lax.all_to_all(row, "z", 0, 0, tiled=True)
    send, rest = call(halve_kernel, [shape(IMAGES, WIDTH)] * 2, place, keep, got, smem_in=(0,))
    got = swapped(send, "y_hi")
    (text_grad,) = call(
        text_end_kernel, [shape(IMAGES, WIDTH)], place, temp_log, texts, rest, got, smem_in=(0, 1)
    )
    (image_grad,) = call(
        image_end_kernel, [shape(IMAGES, WIDTH)], temp_log, images, dx0, *parts, smem_in=(0,)
    )
    row, image_grad, text_grad = lax.optimization_barrier((row, image_grad, text_grad))
    loss, temp_grad, bias_grad = call(
        sums_end_kernel, [shape(1)] * 3, temp_log, row, smem_in=(0,), smem_out=(0, 1, 2)
    )
    return (loss, image_grad, text_grad, temp_grad, bias_grad)


def solution(mesh):
    axes = BLK + ("y_hi", "core")
    fine = Mesh(mesh.devices.reshape(SIZES), axes)
    placed = (P(axes, None), P(BLK, None), P(axes), P(), P())
    return jax.shard_map(
        per_device,
        mesh=fine,
        in_specs=placed,
        out_specs=(P(), P(axes, None), P(axes, None), P(), P()),
        check_vma=False,
    )
```

time: 374 us -> 134 us (0.36)
  blocking collectives: 167 us -> 0 us
  waiting for transfers between devices: 102 us -> 31 us
  between operations: 28.5 us -> 2.12 us
  starting transfers between devices: 51.1 us -> 75.6 us
  Pallas kernels: 0 us -> 18.6 us
  matrix products: 14.3 us -> 0 us
  other arithmetic: 10.8 us -> 0.08 us
  local copies, waits for them, and re-layouts: 0.08 us -> 6.37 us
    psum x1 -> x0, blocking collectives: 167 us -> none  [per_device(): lax.psum((totals[0], totals[1], totals[2]), ('blk', 'rep'))]
    ppermute x15 -> x10, waiting for transfers between devices: 102 us -> 31 us  [the longest x8 28.6 us: shifted(): lax.ppermute(value, BLK, [(i, (i + by) % count) for i in range(count)])]
    pallas_call x0 -> x10, Pallas kernels: none -> 18.6 us  [call(): pl.pallas_call(body, out_shape=outs, in_specs=[scalar if k in smem_in els...]
    dot_general x15 -> x0, matrix products: 14.3 us -> none  [the longest x5 6.07 us: block_terms(): jnp.dot(image_unit, text_unit.T, preferred_element_type=jnp.float32)]
    all_to_all x0 -> x2, starting transfers between devices: none -> 12.9 us  [the longest x1 8.42 us: per_device(): row = lax.all_to_all(row, 'z', 0, 0, tiled=True)]
    ppermute x15 -> x10, starting transfers between devices: 51.1 us -> 62.7 us  [the longest x8 53.5 us: shifted(): lax.ppermute(value, BLK, [(i, (i + by) % count) for i in range(count)])]
    unnamed x2 -> x22, local copies, waits for them, and re-layouts: 0.01 us -> 6.37 us
    reduce_sum x4 -> x0, other arithmetic: 5.27 us -> none  [the longest x2 2.68 us: normalize(): factor = lax.rsqrt(jnp.sum(full * full, axis=-1, keepdims=True) + EPS)]
  transfers between devices with their start and end apart: 16 -> 12, of which waited for: 10 -> 5; matrix products, arithmetic and copies ran while one was open for 6% -> 0% of each run, Pallas kernels for 0% -> 9%
where the time goes in v1:
time: 134 us
  starting transfers between devices  75.6 us (56%)
  waiting for transfers between devices  31 us (23%)
  Pallas kernels  18.6 us (14%)
  local copies, waits for them, and re-layouts  6.37 us (5%)
  between operations  2.12 us (2%)
    ppermute x8, starting transfers between devices, shifted(): lax.ppermute(value, BLK, [(i, (i + by) % count) for i in range(count)])  53.5 us
    ppermute x8, waiting for transfers between devices, shifted(): lax.ppermute(value, BLK, [(i, (i + by) % count) for i in range(count)])  28.6 us
    pallas_call x10, Pallas kernels, call(): pl.pallas_call(body, out_shape=outs, in_specs=[scalar if k in smem_in els...  18.6 us
    ppermute x2, starting transfers between devices, swapped(): return lax.ppermute(value, axis, [(0, 1), (1, 0)])  9.26 us
    all_to_all x1, starting transfers between devices, per_device(): row = lax.all_to_all(row, 'z', 0, 0, tiled=True)  8.42 us
    unnamed x22, local copies, waits for them, and re-layouts  6.37 us
    all_to_all x1, starting transfers between devices, per_device(): row = lax.all_to_all(row, PLANE, 0, 0, tiled=True)  4.46 us
  transfers between devices with their start and end apart: 12, of which 5 were waited for; matrix products, arithmetic and copies ran while one was open for 0% of the time, Pallas kernels for 9%

profile of v1, /device:TPU:1, one launch (start us, length us, event | category | flops | bytes accessed | tf_op | source)
XLA Modules:
  0.0 133.8 jit_solution(14988385016544088917)
XLA Ops:
  0.6 1.0 copy-done.2
  1.6 0.7 copy-done.6
  2.4 22.4 %collective-permute-start.1 = (bf16[144,1152]{1,0:T(8,128)(2,1)S(1)}, bf16[144,1152]{1,0:T(8,128)(2,1)S(1)}, u32[]{:S(2)}, u32[]{:S(2)}) collective-permute-start(bf16[144,1152]{1,0:T(8,128)(2,1)S(1)} %shard_map.92.packed_ref.x0), channel_id=1, source_target_pairs={{0,1020},{4,0},{8,4},{12,8},{16,12},{20,16},{24,20},{28,24},{32,28... | collective-permute-start | bytes 995336 | tf_op jit(solution)/shard_map/ppermute | solution.py:44
  24.8 1.9 %collective-permute-start = (bf16[144,1152]{1,0:T(8,128)(2,1)S(1)}, bf16[144,1152]{1,0:T(8,128)(2,1)S(1)}, u32[]{:S(2)}, u32[]{:S(2)}) collective-permute-start(bf16[144,1152]{1,0:T(8,128)(2,1)S(1)} %shard_map.92.packed_ref.x0), channel_id=1, source_target_pairs={{0,4},{4,8},{8,12},{12,16},{16,20},{20,24},{24,28},{28,32},{32,36}... | collective-permute-start | bytes 995336 | tf_op jit(solution)/shard_map/ppermute | solution.py:44
  28.2 1.3 copy-done
  29.4 2.0 %shard_map.93 = (bf16[512,1152]{1,0:T(8,128)(2,1)S(1)}, f32[128,1152]{1,0:T(8,128)S(1)}, bf16[512,128]{1,0:T(8,128)(2,1)S(1)}, f32[8,128]{1,0:T(8,128)S(1)}) custom-call(bf16[512,1152]{1,0:T(8,128)(2,1)S(1)} %copy-done, bf16[144,1152]{1,0:T(8,128)(2,1)S(1)} %shard_map.92.packed_ref.x0, s32[3]{0:T(128)S(1)} %pad_add_fusion.place_ref, f32[1]{0:T(128)S(6)} %copy.10.temp_ref, ...), custom_call_target="tpu_custom_call" | custom-call | flops 301989888 | bytes 3416084 | tf_op jit(solution)/shard_map/pallas_call | solution.py:32
  31.4 7.9 %collective-permute-done.left_ref.x1l = bf16[144,1152]{1,0:T(8,128)(2,1)S(1)} collective-permute-done((bf16[144,1152]{1,0:T(8,128)(2,1)S(1)}, bf16[144,1152]{1,0:T(8,128)(2,1)S(1)}, u32[]{:S(2)}, u32[]{:S(2)}) %collective-permute-start) | collective-permute-done | bytes 331808 | tf_op jit(solution)/shard_map/ppermute | solution.py:44
  39.3 1.9 %collective-permute-start.2 = (bf16[144,1152]{1,0:T(8,128)(2,1)S(1)}, bf16[144,1152]{1,0:T(8,128)(2,1)S(1)}, u32[]{:S(2)}, u32[]{:S(2)}) collective-permute-start(bf16[144,1152]{1,0:T(8,128)(2,1)S(1)} %collective-permute-done.left_ref.x1l), channel_id=1, source_target_pairs={{0,4},{4,8},{8,12},{12,16},{16,20},{20,24},{24,28},{28,32},{32,36}... | collective-permute-start | bytes 995336 | tf_op jit(solution)/shard_map/ppermute | solution.py:44
  41.2 7.6 %collective-permute-start.3 = (bf16[144,1152]{1,0:T(8,128)(2,1)S(1)}, bf16[144,1152]{1,0:T(8,128)(2,1)S(1)}, u32[]{:S(2)}, u32[]{:S(2)}) collective-permute-start(bf16[144,1152]{1,0:T(8,128)(2,1)S(1)} %collective-permute-done.1.right_ref.x1r), channel_id=1, source_target_pairs={{0,1020},{4,0},{8,4},{12,8},{16,12},{20,16},{24,20},{28,24},{32,28... | collective-permute-start | bytes 995336 | tf_op jit(solution)/shard_map/ppermute | solution.py:44
  48.8 3.0 %shard_map.94 = (f32[128,1152]{1,0:T(8,128)S(1)}, f32[128,1152]{1,0:T(8,128)S(1)}, bf16[512,256]{1,0:T(8,128)(2,1)S(1)}, f32[8,128]{1,0:T(8,128)S(1)}) custom-call(bf16[512,1152]{1,0:T(8,128)(2,1)S(1)} %get-tuple-element.33.text_ref, bf16[144,1152]{1,0:T(8,128)(2,1)S(1)} %collective-permute-done.left_ref.x1l, ...), custom_call_target="tpu_custom_call" | custom-call | flops 603979776 | bytes 3289108 | tf_op jit(solution)/shard_map/pallas_call | solution.py:32
  51.9 0.8 copy-done.7
  52.7 0.8 copy-done.8
  53.7 3.3 %shard_map.95 = (f32[128,1152]{1,0:T(8,128)S(1)}, f32[128,1152]{1,0:T(8,128)S(1)}, bf16[512,256]{1,0:T(8,128)(2,1)S(1)}, f32[32,1,128]{2,1,0:T(1,128)}) custom-call(bf16[512,1152]{1,0:T(8,128)(2,1)S(1)} %get-tuple-element.33.text_ref, bf16[144,1152]{1,0:T(8,128)(2,1)S(1)} %collective-permute-done.2.left_ref.x2l, ...), custom_call_target="tpu_custom_call" | custom-call | flops 603979776 | bytes 3309588 | tf_op jit(solution)/shard_map/pallas_call | solution.py:32
  57.0 0.8 copy-done.9
  58.0 2.8 %shard_map.97 = (f32[2,128,1152]{2,1,0:T(8,128)}, f32[2,128,1152]{2,1,0:T(8,128)S(1)}) custom-call(s32[3]{0:T(128)S(1)} %pad_add_fusion.place_ref, bf16[512,128]{1,0:T(8,128)(2,1)S(1)} %get-tuple-element.39.g0, bf16[512,256]{1,0:T(8,128)(2,1)S(1)} %get-tuple-element.40.g1, bf16[512,256]{1,0:T(8,128)(2,1)S(1)} %get-tuple-element.41.g2, ...), custom_call_target="tpu_custom_call" | custom-call | flops 754974720 | bytes 4673548 | tf_op jit(solution)/shard_map/pallas_call | solution.py:32
  60.9 5.0 %collective-permute-start.4 = (f32[2,128,1152]{2,1,0:T(8,128)}, f32[2,128,1152]{2,1,0:T(8,128)S(1)}, u32[]{:S(2)}, u32[]{:S(2)}) collective-permute-start(f32[2,128,1152]{2,1,0:T(8,128)} %get-tuple-element.42), channel_id=1, source_target_pairs={{0,1},{1,0},{2,3},{3,2},{4,5},{5,4},{6,7},{7,6},{8,9},{9,8},{10,11... | collective-permute-start | bytes 3538952 | tf_op jit(solution)/shard_map/ppermute | solution.py:48
  65.9 4.5 %all-to-all-start = ((f32[32,1,128]{2,1,0:T(1,128)}), f32[32,1,128]{2,1,0:T(1,128)S(1)}, u32[]{:S(2)}, u32[]{:S(2)}) async-start(f32[32,1,128]{2,1,0:T(1,128)} %get-tuple-element.38), calls=%async_computation | async-start | bytes 32768 | tf_op jit(solution)/shard_map/all_to_all | solution.py:198
  70.3 10.9 %collective-permute-start.5 = (f32[128,1152]{1,0:T(8,128)}, f32[128,1152]{1,0:T(8,128)}, u32[]{:S(2)}, u32[]{:S(2)}) collective-permute-start(f32[128,1152]{1,0:T(8,128)} %copy-done.8), channel_id=1, source_target_pairs={{0,1020},{4,0},{8,4},{12,8},{16,12},{20,16},{24,20},{28,24},{32,28... | collective-permute-start | bytes 1769480 | tf_op jit(solution)/shard_map/ppermute | solution.py:44
  81.2 1.9 %collective-permute-start.6 = (f32[128,1152]{1,0:T(8,128)}, f32[128,1152]{1,0:T(8,128)}, u32[]{:S(2)}, u32[]{:S(2)}) collective-permute-start(f32[128,1152]{1,0:T(8,128)} %copy-done.7), channel_id=1, source_target_pairs={{0,4},{4,8},{8,12},{12,16},{16,20},{20,24},{24,28},{28,32},{32,36}... | collective-permute-start | bytes 1769480 | tf_op jit(solution)/shard_map/ppermute | solution.py:44
  83.2 3.6 %collective-permute-start.7 = (f32[128,1152]{1,0:T(8,128)}, f32[128,1152]{1,0:T(8,128)}, u32[]{:S(2)}, u32[]{:S(2)}) collective-permute-start(f32[128,1152]{1,0:T(8,128)} %copy-done.10), channel_id=1, source_target_pairs={{0,1016},{4,1020},{8,0},{12,4},{16,8},{20,12},{24,16},{28,20},{32,... | collective-permute-start | bytes 1769480 | tf_op jit(solution)/shard_map/ppermute | solution.py:44
  86.8 3.2 %collective-permute-start.8 = (f32[128,1152]{1,0:T(8,128)}, f32[128,1152]{1,0:T(8,128)}, u32[]{:S(2)}, u32[]{:S(2)}) collective-permute-start(f32[128,1152]{1,0:T(8,128)} %copy-done.9), channel_id=1, source_target_pairs={{0,8},{4,12},{8,16},{12,20},{16,24},{20,28},{24,32},{28,36},{32,40... | collective-permute-start | bytes 1769480 | tf_op jit(solution)/shard_map/ppermute | solution.py:44
  90.0 0.6 shard_map.96
  90.6 1.5 %shard_map.99 = (f32[128,1152]{1,0:T(8,128)}, f32[128,1152]{1,0:T(8,128)S(1)}) custom-call(s32[3]{0:T(128)S(1)} %pad_add_fusion.place_ref, f32[2,128,1152]{2,1,0:T(8,128)S(1)} %get-tuple-element.49.keep_ref, f32[2,128,1152]{2,1,0:T(8,128)S(1)} %collective-permute-done.4.got_ref), custom_call_target="tpu_custom_call" | custom-call | bytes 3538956 | tf_op jit(solution)/shard_map/pallas_call | solution.py:32
  92.1 0.8 copy-done.4
  92.9 4.3 %collective-permute-start.9 = (f32[128,1152]{1,0:T(8,128)}, f32[128,1152]{1,0:T(8,128)S(1)}, u32[]{:S(2)}, u32[]{:S(2)}) collective-permute-start(f32[128,1152]{1,0:T(8,128)} %get-tuple-element.52), channel_id=1, source_target_pairs={{0,2},{2,0},{1,3},{3,1},{4,6},{6,4},{5,7},{7,5},{8,10},{10,8},{9,1... | collective-permute-start | bytes 1769480 | tf_op jit(solution)/shard_map/ppermute | solution.py:48
  97.2 8.4 %all-to-all-start.1 = ((f32[32,1,128]{2,1,0:T(1,128)}), f32[32,1,128]{2,1,0:T(1,128)S(1)}, u32[]{:S(2)}, u32[]{:S(2)}) async-start(f32[32,1,128]{2,1,0:T(1,128)} %shard_map.96), calls=%async_computation.1 | async-start | bytes 32768 | tf_op jit(solution)/shard_map/all_to_all | solution.py:206
  105.7 3.9 %collective-permute-done.6.d2 = f32[128,1152]{1,0:T(8,128)} collective-permute-done((f32[128,1152]{1,0:T(8,128)}, f32[128,1152]{1,0:T(8,128)}, u32[]{:S(2)}, u32[]{:S(2)}) %collective-permute-start.6) | collective-permute-done | bytes 589856 | tf_op jit(solution)/shard_map/ppermute | solution.py:44
  109.6 16.6 %collective-permute-done.7.d3 = f32[128,1152]{1,0:T(8,128)} collective-permute-done((f32[128,1152]{1,0:T(8,128)}, f32[128,1152]{1,0:T(8,128)}, u32[]{:S(2)}, u32[]{:S(2)}) %collective-permute-start.7) | collective-permute-done | bytes 589856 | tf_op jit(solution)/shard_map/ppermute | solution.py:44
  126.2 2.9 %shard_map.98 = f32[128,1152]{1,0:T(8,128)} custom-call(f32[1]{0:T(128)S(6)} %copy.10.temp_ref, bf16[128,1152]{1,0:T(8,128)(2,1)S(1)} %copy-done.3, f32[128,1152]{1,0:T(8,128)S(1)} %get-tuple-element.44.d0, f32[128,1152]{1,0:T(8,128)} %collective-permute-done.5.d1, f32[128,1152]{1,0:T(8,128)} %collective-permute-done.6.d2, ...), custom_call_target="tpu_custom_call" | custom-call | bytes 3833860 | tf_op jit(solution)/shard_map/pallas_call | solution.py:32
  129.1 2.4 %collective-permute-done.9.got_ref = f32[128,1152]{1,0:T(8,128)S(1)} collective-permute-done((f32[128,1152]{1,0:T(8,128)}, f32[128,1152]{1,0:T(8,128)S(1)}, u32[]{:S(2)}, u32[]{:S(2)}) %collective-permute-start.9) | collective-permute-done | bytes 589856 | tf_op jit(solution)/shard_map/ppermute | solution.py:48
  131.5 1.6 %shard_map.100 = f32[128,1152]{1,0:T(8,128)} custom-call(s32[3]{0:T(128)S(1)} %pad_add_fusion.place_ref, f32[1]{0:T(128)S(6)} %copy.10.temp_ref, bf16[512,1152]{1,0:T(8,128)(2,1)S(1)} %copy-done.1, f32[128,1152]{1,0:T(8,128)S(1)} %copy-done.5, f32[128,1152]{1,0:T(8,128)S(1)} %collective-permute-done.9.got_ref), custom_call_target="tpu_custom_call" | custom-call | bytes 2949136 | tf_op jit(solution)/shard_map/pallas_call | solution.py:32
  133.1 0.7 shard_map.101
  (25 shorter events, 0.7 us)
Async XLA Ops:
  0.6 1.0 copy-start.2
  1.6 0.7 copy-start.6
  2.4 29.0 %collective-permute-start.1 = (bf16[144,1152]{1,0:T(8,128)(2,1)S(1)}, bf16[144,1152]{1,0:T(8,128)(2,1)S(1)}, u32[]{:S(2)}, u32[]{:S(2)}) collective-permute-start(bf16[144,1152]{1,0:T(8,128)(2,1)S(1)} %shard_map.92.packed_ref.x0), channel_id=1, source_target_pairs={{0,1020},{4,0},{8,4},{12,8},{16,12},{20,16},{24,20},{28,24},{32,28... | collective-permute-start | bytes 995336 | tf_op jit(solution)/shard_map/ppermute | solution.py:44
  24.8 14.5 %collective-permute-start = (bf16[144,1152]{1,0:T(8,128)(2,1)S(1)}, bf16[144,1152]{1,0:T(8,128)(2,1)S(1)}, u32[]{:S(2)}, u32[]{:S(2)}) collective-permute-start(bf16[144,1152]{1,0:T(8,128)(2,1)S(1)} %shard_map.92.packed_ref.x0), channel_id=1, source_target_pairs={{0,4},{4,8},{8,12},{12,16},{16,20},{20,24},{24,28},{28,32},{32,36}... | collective-permute-start | bytes 995336 | tf_op jit(solution)/shard_map/ppermute | solution.py:44
  28.2 1.3 copy-start
  39.3 14.2 %collective-permute-start.2 = (bf16[144,1152]{1,0:T(8,128)(2,1)S(1)}, bf16[144,1152]{1,0:T(8,128)(2,1)S(1)}, u32[]{:S(2)}, u32[]{:S(2)}) collective-permute-start(bf16[144,1152]{1,0:T(8,128)(2,1)S(1)} %collective-permute-done.left_ref.x1l), channel_id=1, source_target_pairs={{0,4},{4,8},{8,12},{12,16},{16,20},{20,24},{24,28},{28,32},{32,36}... | collective-permute-start | bytes 995336 | tf_op jit(solution)/shard_map/ppermute | solution.py:44
  41.2 12.5 %collective-permute-start.3 = (bf16[144,1152]{1,0:T(8,128)(2,1)S(1)}, bf16[144,1152]{1,0:T(8,128)(2,1)S(1)}, u32[]{:S(2)}, u32[]{:S(2)}) collective-permute-start(bf16[144,1152]{1,0:T(8,128)(2,1)S(1)} %collective-permute-done.1.right_ref.x1r), channel_id=1, source_target_pairs={{0,1020},{4,0},{8,4},{12,8},{16,12},{20,16},{24,20},{28,24},{32,28... | collective-permute-start | bytes 995336 | tf_op jit(solution)/shard_map/ppermute | solution.py:44
  51.9 0.8 copy-start.7
  52.7 0.8 copy-start.8
  57.0 0.8 copy-start.9
  57.0 1.0 copy-start.10
  60.9 29.7 %collective-permute-start.4 = (f32[2,128,1152]{2,1,0:T(8,128)}, f32[2,128,1152]{2,1,0:T(8,128)S(1)}, u32[]{:S(2)}, u32[]{:S(2)}) collective-permute-start(f32[2,128,1152]{2,1,0:T(8,128)} %get-tuple-element.42), channel_id=1, source_target_pairs={{0,1},{1,0},{2,3},{3,2},{4,5},{5,4},{6,7},{7,6},{8,9},{9,8},{10,11... | collective-permute-start | bytes 3538952 | tf_op jit(solution)/shard_map/ppermute | solution.py:48
  65.9 24.1 %all-to-all-start = ((f32[32,1,128]{2,1,0:T(1,128)}), f32[32,1,128]{2,1,0:T(1,128)S(1)}, u32[]{:S(2)}, u32[]{:S(2)}) async-start(f32[32,1,128]{2,1,0:T(1,128)} %get-tuple-element.38), calls=%async_computation | async-start | bytes 32768 | tf_op jit(solution)/shard_map/all_to_all | solution.py:198
  70.3 35.3 %collective-permute-start.5 = (f32[128,1152]{1,0:T(8,128)}, f32[128,1152]{1,0:T(8,128)}, u32[]{:S(2)}, u32[]{:S(2)}) collective-permute-start(f32[128,1152]{1,0:T(8,128)} %copy-done.8), channel_id=1, source_target_pairs={{0,1020},{4,0},{8,4},{12,8},{16,12},{20,16},{24,20},{28,24},{32,28... | collective-permute-start | bytes 1769480 | tf_op jit(solution)/shard_map/ppermute | solution.py:44
  81.2 28.4 %collective-permute-start.6 = (f32[128,1152]{1,0:T(8,128)}, f32[128,1152]{1,0:T(8,128)}, u32[]{:S(2)}, u32[]{:S(2)}) collective-permute-start(f32[128,1152]{1,0:T(8,128)} %copy-done.7), channel_id=1, source_target_pairs={{0,4},{4,8},{8,12},{12,16},{16,20},{20,24},{24,28},{28,32},{32,36}... | collective-permute-start | bytes 1769480 | tf_op jit(solution)/shard_map/ppermute | solution.py:44
  83.2 43.0 %collective-permute-start.7 = (f32[128,1152]{1,0:T(8,128)}, f32[128,1152]{1,0:T(8,128)}, u32[]{:S(2)}, u32[]{:S(2)}) collective-permute-start(f32[128,1152]{1,0:T(8,128)} %copy-done.10), channel_id=1, source_target_pairs={{0,1016},{4,1020},{8,0},{12,4},{16,8},{20,12},{24,16},{28,20},{32,... | collective-permute-start | bytes 1769480 | tf_op jit(solution)/shard_map/ppermute | solution.py:44
  86.8 39.4 %collective-permute-start.8 = (f32[128,1152]{1,0:T(8,128)}, f32[128,1152]{1,0:T(8,128)}, u32[]{:S(2)}, u32[]{:S(2)}) collective-permute-start(f32[128,1152]{1,0:T(8,128)} %copy-done.9), channel_id=1, source_target_pairs={{0,8},{4,12},{8,16},{12,20},{16,24},{20,28},{24,32},{28,36},{32,40... | collective-permute-start | bytes 1769480 | tf_op jit(solution)/shard_map/ppermute | solution.py:44
  90.6 35.6 %copy-start.3 = (bf16[128,1152]{1,0:T(8,128)(2,1)S(1)}, bf16[128,1152]{1,0:T(8,128)(2,1)}, u32[]{:S(2)}) copy-start(bf16[128,1152]{1,0:T(8,128)(2,1)} %images_ref.3) | copy-start | bytes 884740
  92.1 0.8 copy-start.4
  92.9 38.6 %collective-permute-start.9 = (f32[128,1152]{1,0:T(8,128)}, f32[128,1152]{1,0:T(8,128)S(1)}, u32[]{:S(2)}, u32[]{:S(2)}) collective-permute-start(f32[128,1152]{1,0:T(8,128)} %get-tuple-element.52), channel_id=1, source_target_pairs={{0,2},{2,0},{1,3},{3,1},{4,6},{6,4},{5,7},{7,5},{8,10},{10,8},{9,1... | collective-permute-start | bytes 1769480 | tf_op jit(solution)/shard_map/ppermute | solution.py:48
  97.2 35.9 %all-to-all-start.1 = ((f32[32,1,128]{2,1,0:T(1,128)}), f32[32,1,128]{2,1,0:T(1,128)S(1)}, u32[]{:S(2)}, u32[]{:S(2)}) async-start(f32[32,1,128]{2,1,0:T(1,128)} %shard_map.96), calls=%async_computation.1 | async-start | bytes 32768 | tf_op jit(solution)/shard_map/all_to_all | solution.py:206
  126.2 5.3 %copy-start.1 = (bf16[512,1152]{1,0:T(8,128)(2,1)S(1)}, bf16[512,1152]{1,0:T(8,128)(2,1)}, u32[]{:S(2)}) copy-start(bf16[512,1152]{1,0:T(8,128)(2,1)} %texts_ref.3) | copy-start | bytes 3538948
  126.2 5.3 %copy-start.5 = (f32[128,1152]{1,0:T(8,128)S(1)}, f32[128,1152]{1,0:T(8,128)}, u32[]{:S(2)}) copy-start(f32[128,1152]{1,0:T(8,128)} %copy-done.4) | copy-start | bytes 1769476

commit v2 on v1

v2 whole, which is shorter than its diff:
```python
import jax
import jax.numpy as jnp
from jax import lax
from jax.experimental import pallas as pl
from jax.experimental.pallas import tpu as pltpu
from jax.sharding import Mesh, PartitionSpec as P

EPS = 1e-06
BLK = ("y_lo", "z", "x")
PLANE = ("y_lo", "x", "y_hi", "core")
SIZES = (2, 32, 4, 2, 2)
WIDTH = 1152
IMAGES = 128
TEXTS = 512
PAD_ROWS = 16
PACKED = IMAGES + PAD_ROWS
BATCH = 131072
RING = 32
F32 = jnp.float32
BF16 = jnp.bfloat16


def shape(*dims, dtype=F32):
    return jax.ShapeDtypeStruct(dims, dtype)


def call(body, outs, *args, flops=0, smem_in=(), smem_out=(), any_out=(), scratch=()):
    moved = sum(a.size * a.dtype.itemsize for a in args)
    moved += sum(o.size * o.dtype.itemsize for o in outs)
    scalar = pl.BlockSpec(memory_space=pltpu.SMEM)
    vector = pl.BlockSpec(memory_space=pltpu.VMEM)
    placed = pl.BlockSpec(memory_space=pl.ANY)
    return pl.pallas_call(
        body,
        out_shape=outs,
        in_specs=[scalar if k in smem_in else vector for k in range(len(args))],
        out_specs=[scalar if k in smem_out else placed if k in any_out else vector for k in range(len(outs))],
        scratch_shapes=list(scratch),
        compiler_params=pltpu.CompilerParams(vmem_limit_bytes=20 * 1024 * 1024),
        cost_estimate=pl.CostEstimate(flops=flops, bytes_accessed=moved, transcendentals=0),
    )(*args)


def to_side(value, by):
    count = lax.axis_size(BLK)
    pairs = []
    for shard in range(count):
        pairs.append((2 * shard, 2 * ((shard + by) % count)))
        pairs.append((2 * shard + 1, 2 * ((shard - by) % count) + 1))
    return lax.ppermute(value, BLK + ("core",), pairs)


def swapped(value, axis):
    return lax.ppermute(value, axis, [(0, 1), (1, 0)])


def normalized(values):
    full = values.astype(F32)
    factor = lax.rsqrt(jnp.sum(full * full, axis=-1, keepdims=True) + EPS)
    return full * factor, factor


def back_normal(unit_f, factor, dunit):
    return factor * (dunit - unit_f * jnp.sum(unit_f * dunit, axis=-1, keepdims=True))


def pack_kernel(mine_ref, other_ref, my_positive_ref, other_positive_ref, out_ref):
    row = lax.broadcasted_iota(jnp.int32, (PAD_ROWS, IMAGES), 0)
    for k, (images_ref, positive_ref) in enumerate(((mine_ref, my_positive_ref), (other_ref, other_positive_ref))):
        unit, _ = normalized(images_ref[...])
        out_ref[k, :IMAGES, :] = unit.astype(BF16)
        pos = positive_ref[...]
        digit = jnp.where(row == 0, pos >> 12, jnp.where(row == 1, (pos >> 6) & 63, pos & 63))
        out_ref[k, IMAGES:, :] = jnp.zeros((PAD_ROWS, WIDTH), BF16)
        out_ref[k, IMAGES:, :IMAGES] = digit.astype(F32).astype(BF16)


def pair_block(packed_ref, k, text_unit, place_ref, temp_ref, bias_ref):
    unit = packed_ref[k, :IMAGES, :]
    digits = packed_ref[k, IMAGES:, :IMAGES].astype(F32).astype(jnp.int32)
    row = lax.broadcasted_iota(jnp.int32, (PAD_ROWS, IMAGES), 0)
    weight = jnp.where(row == 0, 4096, jnp.where(row == 1, 64, jnp.where(row == 2, 1, 0)))
    pos = jnp.sum(digits * weight, axis=0, keepdims=True) - place_ref[0]
    sim = lax.dot_general(text_unit, unit, (((1,), (1,)), ((), ())), preferred_element_type=F32)
    scale = jnp.exp(jnp.full((1, IMAGES), temp_ref[0], F32))
    logit = scale * sim + bias_ref[0]
    matching = lax.broadcasted_iota(jnp.int32, (TEXTS, IMAGES), 0) == pos
    against = jnp.where(matching, -logit, logit)
    small = jnp.exp(-jnp.abs(against))
    soft = jnp.maximum(against, 0.0) + jnp.log1p(small)
    sigmoid = jnp.where(against >= 0, 1.0, small) / (1.0 + small)
    grads = jnp.where(matching, -sigmoid, sigmoid)
    rounded = grads.astype(BF16)
    image_part = lax.dot_general(rounded, text_unit, (((0,), (0,)), ((), ())), preferred_element_type=F32)
    sums = [jnp.sum(v, axis=0, keepdims=True) for v in (soft, grads, grads * sim)]
    return image_part, rounded, sums


def text_part(grads, packed_ref, k):
    return jnp.dot(grads, packed_ref[k, :IMAGES, :], preferred_element_type=F32)


def sums_tile(sums):
    return jnp.concatenate(sums + [jnp.zeros((5, IMAGES), F32)], axis=0)


def own_kernel(texts_ref, packed_ref, place_ref, temp_ref, bias_ref, text_ref, dx_ref, dy_ref, sums_ref):
    unit, _ = normalized(texts_ref[...])
    text_ref[...] = unit.astype(BF16)
    dx_ref[...], grads, sums = pair_block(packed_ref, 0, text_ref[...], place_ref, temp_ref, bias_ref)
    dy_ref[...] = text_part(grads, packed_ref, 0)
    sums_ref[...] = sums_tile(sums)


def both_blocks(text_ref, packed_ref, place_ref, temp_ref, bias_ref, dx_ref, staged, sems):
    text_unit = text_ref[...]
    grads, sums, copies = [], [], []
    for k in range(2):
        staged[k], rounded, part = pair_block(packed_ref, k, text_unit, place_ref, temp_ref, bias_ref)
        copy = pltpu.make_async_copy(staged.at[k], dx_ref.at[k], sems.at[k])
        copy.start()
        grads.append(rounded)
        sums.append(part)
        copies.append(copy)
    return grads, sums_tile([a + b for a, b in zip(*sums)]), copies


def near_kernel(text_ref, packed_ref, place_ref, temp_ref, bias_ref, old_dy_ref, old_sums_ref,
                dx_ref, dy_ref, sums_ref, staged, sems):
    grads, tile, copies = both_blocks(text_ref, packed_ref, place_ref, temp_ref, bias_ref, dx_ref, staged, sems)
    dy_ref[...] = old_dy_ref[...] + text_part(grads[0], packed_ref, 0) + text_part(grads[1], packed_ref, 1)
    sums_ref[...] = old_sums_ref[...] + tile
    for copy in copies:
        copy.wait()


def far_kernel(text_ref, packed_ref, place_ref, temp_ref, bias_ref, old_dy_ref, old_sums_ref,
               dx_ref, send_ref, keep_ref, row_ref, staged, sems, total):
    grads, tile, copies = both_blocks(text_ref, packed_ref, place_ref, temp_ref, bias_ref, dx_ref, staged, sems)
    total[...] = old_dy_ref[...] + text_part(grads[0], packed_ref, 0) + text_part(grads[1], packed_ref, 1)
    core = place_ref[2]
    for out_ref, owner in ((send_ref, 1 - core), (keep_ref, core)):
        for half in range(2):
            first = pl.multiple_of((2 * half + owner) * IMAGES, IMAGES)
            out_ref[half] = total[pl.ds(first, IMAGES), :]
    totals = jnp.sum(old_sums_ref[...] + tile, axis=1, keepdims=True)
    lane = lax.broadcasted_iota(jnp.int32, (1, IMAGES), 1)
    row = sum(jnp.where(lane == k, totals[k:k + 1], 0.0) for k in range(3))
    row_ref[...] = jnp.broadcast_to(row[None], row_ref.shape)
    for copy in copies:
        copy.wait()


def halve_kernel(place_ref, keep_ref, got_ref, send_ref, rest_ref):
    mine = place_ref[1]
    send_ref[...] = keep_ref[1 - mine] + got_ref[1 - mine]
    rest_ref[...] = keep_ref[mine] + got_ref[mine]


def prepare_kernel(place_ref, texts_ref, unit_ref, factor_ref):
    first = pl.multiple_of((2 * place_ref[1] + place_ref[2]) * IMAGES, IMAGES)
    unit_ref[...], factor = normalized(texts_ref[pl.ds(first, IMAGES), :])
    factor_ref[...] = jnp.broadcast_to(factor, factor_ref.shape)


def text_end_kernel(temp_ref, unit_ref, factor_ref, rest_ref, got_ref, out_ref):
    scale = jnp.exp(jnp.full((1, WIDTH), temp_ref[0], F32))
    out_ref[...] = back_normal(unit_ref[...], factor_ref[:, :1], scale * (rest_ref[...] + got_ref[...]))


def near_join_kernel(own_ref, near_ref, mine_ref):
    mine_ref[...] = own_ref[...] + near_ref[0]


def join_kernel(partial_ref, near_ref, far_ref, mine_ref, other_ref):
    mine_ref[...] = partial_ref[...] + far_ref[0]
    other_ref[...] = near_ref[1] + far_ref[1]


def image_end_kernel(temp_ref, images_ref, mine_ref, got_ref, out_ref):
    unit, factor = normalized(images_ref[...])
    scale = jnp.exp(jnp.full((1, WIDTH), temp_ref[0], F32))
    out_ref[...] = back_normal(unit, factor, scale * (mine_ref[...] + got_ref[...]))


def again_kernel(row_ref, out_ref):
    total = jnp.sum(row_ref[...], axis=0, keepdims=True)
    out_ref[...] = jnp.broadcast_to(total, out_ref.shape)


def sums_end_kernel(temp_ref, row_ref, loss_ref, temp_grad_ref, bias_grad_ref):
    total = jnp.sum(row_ref[...], axis=0)
    lane = lax.broadcasted_iota(jnp.int32, (1, IMAGES), 1)
    scale = jnp.exp(jnp.full((1, IMAGES), temp_ref[0], F32))
    loss_ref[0] = jnp.sum(jnp.where(lane == 0, total, 0.0)) * (1.0 / BATCH)
    bias_grad_ref[0] = jnp.sum(jnp.where(lane == 1, total, 0.0))
    temp_grad_ref[0] = jnp.sum(jnp.where(lane == 2, total * scale, 0.0))


def per_device(images, texts, positive, temp_log, bias_arg):
    place = jnp.stack([lax.axis_index(BLK) * TEXTS, lax.axis_index("y_hi"), lax.axis_index("core")]).astype(jnp.int32)
    block_flops = 6 * TEXTS * IMAGES * WIDTH
    positive = positive.reshape(1, IMAGES)
    (packed,) = call(
        pack_kernel, [shape(2, PACKED, WIDTH, dtype=BF16)],
        images, swapped(images, "core"), positive, swapped(positive, "core"),
    )
    near = to_side(packed, 1)
    text_unit, dx0, dy, sums = call(
        own_kernel,
        [shape(TEXTS, WIDTH, dtype=BF16), shape(IMAGES, WIDTH), shape(TEXTS, WIDTH), shape(8, IMAGES)],
        texts, packed, place, temp_log, bias_arg, flops=block_flops, smem_in=(2, 3, 4),
    )
    near, text_unit = lax.optimization_barrier((near, text_unit))
    far = to_side(near, 1)
    staging = [pltpu.VMEM((2, IMAGES, WIDTH), F32), pltpu.SemaphoreType.DMA((2,))]
    near_dx, dy, sums = call(
        near_kernel, [shape(2, IMAGES, WIDTH), shape(TEXTS, WIDTH), shape(8, IMAGES)],
        text_unit, near, place, temp_log, bias_arg, dy, sums,
        flops=2 * block_flops, smem_in=(2, 3, 4), any_out=(0,), scratch=staging,
    )
    near_dx = to_side(near_dx, -1)
    far_dx, send, keep, row = call(
        far_kernel, [shape(2, IMAGES, WIDTH)] * 3 + [shape(RING, 1, IMAGES)],
        text_unit, far, place, temp_log, bias_arg, dy, sums,
        flops=2 * block_flops, smem_in=(2, 3, 4), any_out=(0,),
        scratch=staging + [pltpu.VMEM((TEXTS, WIDTH), F32)],
    )
    far_dx = to_side(far_dx, -2)
    got = swapped(send, "core")
    row = lax.all_to_all(row, "z", 0, 0, tiled=True)
    (mine,) = call(near_join_kernel, [shape(IMAGES, WIDTH)], dx0, near_dx, flops=2 * 10**9)
    mine, got = lax.optimization_barrier((mine, got))
    send, rest = call(halve_kernel, [shape(IMAGES, WIDTH)] * 2, place, keep, got, smem_in=(0,))
    got = swapped(send, "y_hi")
    unit, factor = call(
        prepare_kernel, [shape(IMAGES, WIDTH), shape(IMAGES, IMAGES)], place, texts, smem_in=(0,)
    )
    row, unit = lax.optimization_barrier((row, unit))
    (row,) = call(again_kernel, [shape(RING, 1, IMAGES)], row, flops=6 * 10**9)
    row = lax.all_to_all(row, PLANE, 0, 0, tiled=True)
    mine, other = call(join_kernel, [shape(IMAGES, WIDTH)] * 2, mine, near_dx, far_dx)
    other = swapped(other, "core")
    (text_grad,) = call(
        text_end_kernel, [shape(IMAGES, WIDTH)], temp_log, unit, factor, rest, got,
        smem_in=(0,),
    )
    mine, text_grad = lax.optimization_barrier((mine, text_grad))
    (image_grad,) = call(
        image_end_kernel, [shape(IMAGES, WIDTH)], temp_log, images, mine, other, smem_in=(0,)
    )
    row, image_grad, text_grad = lax.optimization_barrier((row, image_grad, text_grad))
    loss, temp_grad, bias_grad = call(
        sums_end_kernel, [shape(1)] * 3, temp_log, row, smem_in=(0,), smem_out=(0, 1, 2)
    )
    return (loss, image_grad, text_grad, temp_grad, bias_grad)


def solution(mesh):
    axes = BLK + ("y_hi", "core")
    fine = Mesh(mesh.devices.reshape(SIZES), axes)
    placed = (P(axes, None), P(BLK, None), P(axes), P(), P())
    return jax.shard_map(
        per_device,
        mesh=fine,
        in_specs=placed,
        out_specs=(P(), P(axes, None), P(axes, None), P(), P()),
        check_vma=False,
    )
```

time: 134 us -> 119 us (0.89)
  waiting for transfers between devices: 31 us -> 13.6 us
  Pallas kernels: 18.6 us -> 21.6 us
  local copies, waits for them, and re-layouts: 6.37 us -> 4.14 us
    ppermute x8 -> x4, starting transfers between devices: 53.5 us -> 20.8 us  [to_side(): return lax.ppermute(value, BLK + ('core',), pairs)]
    ppermute x2 -> x5, starting transfers between devices: 9.26 us -> 36.3 us  [swapped(): return lax.ppermute(value, axis, [(0, 1), (1, 0)])]
    ppermute x8 -> x4, waiting for transfers between devices: 28.6 us -> 7.66 us  [to_side(): return lax.ppermute(value, BLK + ('core',), pairs)]
    all_to_all x1, starting transfers between devices: 8.42 us -> 13.9 us  [per_device(): row = lax.all_to_all(row, 'z', 0, 0, tiled=True)]
    all_to_all x1, waiting for transfers between devices: 0.01 us -> 4.73 us  [per_device(): row = lax.all_to_all(row, PLANE, 0, 0, tiled=True)]
    pallas_call x10 -> x12, Pallas kernels: 18.6 us -> 21.6 us  [call(): pl.pallas_call(body, out_shape=outs, in_specs=[scalar if k in smem_in els...]
    unnamed x22, local copies, waits for them, and re-layouts: 6.37 us -> 4.14 us
    all_to_all x1, starting transfers between devices: 4.46 us -> 5.82 us  [per_device(): row = lax.all_to_all(row, PLANE, 0, 0, tiled=True)]
  transfers between devices with their start and end apart: 12 -> 11, of which waited for: 5 -> 5; matrix products, arithmetic and copies ran while one was open for 0% -> 0% of each run, Pallas kernels for 9% -> 17%
where the time goes in v2:
time: 119 us; the launch traced here: 118 us
  starting transfers between devices  76.8 us (65%)
  Pallas kernels  21.6 us (18%)
  waiting for transfers between devices  13.6 us (11%)
  local copies, waits for them, and re-layouts  4.14 us (3%)
  between operations  2.17 us (2%)
    ppermute x5, starting transfers between devices, swapped(): return lax.ppermute(value, axis, [(0, 1), (1, 0)])  36.3 us
    pallas_call x12, Pallas kernels, call(): pl.pallas_call(body, out_shape=outs, in_specs=[scalar if k in smem_in els...  21.6 us
    ppermute x4, starting transfers between devices, to_side(): return lax.ppermute(value, BLK + ('core',), pairs)  20.8 us
    all_to_all x1, starting transfers between devices, per_device(): row = lax.all_to_all(row, 'z', 0, 0, tiled=True)  13.9 us
    ppermute x4, waiting for transfers between devices, to_side(): return lax.ppermute(value, BLK + ('core',), pairs)  7.66 us
    all_to_all x1, starting transfers between devices, per_device(): row = lax.all_to_all(row, PLANE, 0, 0, tiled=True)  5.82 us
    all_to_all x1, waiting for transfers between devices, per_device(): row = lax.all_to_all(row, PLANE, 0, 0, tiled=True)  4.73 us
    unnamed x22, local copies, waits for them, and re-layouts  4.14 us
  transfers between devices with their start and end apart: 11, of which 5 were waited for; matrix products, arithmetic and copies ran while one was open for 0% of the time, Pallas kernels for 17%

profile of v2, /device:TPU:1, one launch (start us, length us, event | category | flops | bytes accessed | tf_op | source)
XLA Modules:
  0.0 118.4 jit_solution(16438295222995173657)
XLA Ops:
  0.6 16.2 %collective-permute-start = (bf16[128,1152]{1,0:T(8,128)(2,1)}, bf16[128,1152]{1,0:T(8,128)(2,1)S(1)}, u32[]{:S(2)}, u32[]{:S(2)}) collective-permute-start(bf16[128,1152]{1,0:T(8,128)(2,1)} %images_ref.1), channel_id=1, source_target_pairs={{0,1},{1,0},{2,3},{3,2},{4,5},{5,4},{6,7},{7,6},{8,9},{9,8},{10,11... | collective-permute-start | bytes 884744 | tf_op jit(solution)/shard_map/ppermute | solution.py:54
  16.8 1.9 %collective-permute-start.1 = (s32[1,128]{1,0:T(1,128)}, s32[1,128]{1,0:T(1,128)S(1)}, u32[]{:S(2)}, u32[]{:S(2)}) collective-permute-start(s32[1,128]{1,0:T(1,128)} %bitcast.4), channel_id=1, source_target_pairs={{0,1},{1,0},{2,3},{3,2},{4,5},{5,4},{6,7},{7,6},{8,9},{9,8},{10,11... | collective-permute-start | bytes 1544 | tf_op jit(solution)/shard_map/ppermute | solution.py:54
  18.8 1.2 %collective-permute-done.1.other_positive_ref = s32[1,128]{1,0:T(1,128)S(1)} collective-permute-done((s32[1,128]{1,0:T(1,128)}, s32[1,128]{1,0:T(1,128)S(1)}, u32[]{:S(2)}, u32[]{:S(2)}) %collective-permute-start.1) | collective-permute-done | bytes 544 | tf_op jit(solution)/shard_map/ppermute | solution.py:54
  20.0 1.0 copy-done.1
  21.0 0.7 copy-done.8
  21.8 9.0 %collective-permute-start.2 = (bf16[2,144,1152]{2,1,0:T(8,128)(2,1)S(1)}, bf16[2,144,1152]{2,1,0:T(8,128)(2,1)S(1)}, u32[]{:S(2)}, u32[]{:S(2)}) collective-permute-start(bf16[2,144,1152]{2,1,0:T(8,128)(2,1)S(1)} %shard_map.92.packed_ref), channel_id=1, source_target_pairs={{0,4},{1,1021},{4,8},{5,1},{8,12},{9,5},{12,16},{13,9},{16,20},{17... | collective-permute-start | bytes 1990664 | tf_op jit(solution)/shard_map/ppermute | solution.py:50
  32.2 2.4 %shard_map.93 = (bf16[512,1152]{1,0:T(8,128)(2,1)S(1)}, f32[128,1152]{1,0:T(8,128)S(1)}, f32[512,1152]{1,0:T(8,128)S(1)}, f32[8,128]{1,0:T(8,128)S(1)}) custom-call(bf16[512,1152]{1,0:T(8,128)(2,1)S(1)} %copy-done, bf16[2,144,1152]{2,1,0:T(8,128)(2,1)S(1)} %shard_map.92.packed_ref, s32[3]{0:T(128)S(1)} %pad_add_fusion.place_ref, f32[1]{0:T(128)S(6)} %copy.10.temp_ref, ...), custom_call_target="tpu_custom_call" | custom-call | flops 452984832 | bytes 5976084 | tf_op jit(solution)/shard_map/pallas_call | solution.py:33
  34.6 3.8 %collective-permute-done.2.packed_ref = bf16[2,144,1152]{2,1,0:T(8,128)(2,1)S(1)} collective-permute-done((bf16[2,144,1152]{2,1,0:T(8,128)(2,1)S(1)}, bf16[2,144,1152]{2,1,0:T(8,128)(2,1)S(1)}, u32[]{:S(2)}, u32[]{:S(2)}) %collective-permute-start.2) | collective-permute-done | bytes 663584 | tf_op jit(solution)/shard_map/ppermute | solution.py:50
  38.4 8.0 %collective-permute-start.3 = (bf16[2,144,1152]{2,1,0:T(8,128)(2,1)S(1)}, bf16[2,144,1152]{2,1,0:T(8,128)(2,1)S(1)}, u32[]{:S(2)}, u32[]{:S(2)}) collective-permute-start(bf16[2,144,1152]{2,1,0:T(8,128)(2,1)S(1)} %collective-permute-done.2.packed_ref), channel_id=1, source_target_pairs={{0,4},{1,1021},{4,8},{5,1},{8,12},{9,5},{12,16},{13,9},{16,20},{17... | collective-permute-start | bytes 1990664 | tf_op jit(solution)/shard_map/ppermute | solution.py:50
  46.4 3.8 %shard_map.94 = (f32[2,128,1152]{2,1,0:T(8,128)}, f32[512,1152]{1,0:T(8,128)S(1)}, f32[8,128]{1,0:T(8,128)S(1)}) custom-call(bf16[512,1152]{1,0:T(8,128)(2,1)S(1)} %get-tuple-element.37.text_ref, bf16[2,144,1152]{2,1,0:T(8,128)(2,1)S(1)} %collective-permute-done.2.packed_ref, s32[3]{0:T(128)S(1)} %pad_add_fusion.place_ref, f32[1]{0:T(128)S(6)} %copy.10.temp_ref, ...), custom_call_target="tpu_custom_call" | custom-call | flops 905969664 | bytes 7749652 | tf_op jit(solution)/shard_map/pallas_call | solution.py:33
  50.2 1.9 %collective-permute-start.4 = (f32[2,128,1152]{2,1,0:T(8,128)}, f32[2,128,1152]{2,1,0:T(8,128)}, u32[]{:S(2)}, u32[]{:S(2)}) collective-permute-start(f32[2,128,1152]{2,1,0:T(8,128)} %get-tuple-element.47), channel_id=1, source_target_pairs={{0,1020},{1,5},{4,0},{5,9},{8,4},{9,13},{12,8},{13,17},{16,12},{17... | collective-permute-start | bytes 3538952 | tf_op jit(solution)/shard_map/ppermute | solution.py:50
  52.2 1.8 %collective-permute-done.3.packed_ref = bf16[2,144,1152]{2,1,0:T(8,128)(2,1)S(1)} collective-permute-done((bf16[2,144,1152]{2,1,0:T(8,128)(2,1)S(1)}, bf16[2,144,1152]{2,1,0:T(8,128)(2,1)S(1)}, u32[]{:S(2)}, u32[]{:S(2)}) %collective-permute-start.3) | collective-permute-done | bytes 663584 | tf_op jit(solution)/shard_map/ppermute | solution.py:50
  54.0 4.9 %shard_map.95 = (f32[2,128,1152]{2,1,0:T(8,128)}, f32[2,128,1152]{2,1,0:T(8,128)}, f32[2,128,1152]{2,1,0:T(8,128)S(1)}, f32[32,1,128]{2,1,0:T(1,128)S(1)}) custom-call(bf16[512,1152]{1,0:T(8,128)(2,1)S(1)} %get-tuple-element.37.text_ref, bf16[2,144,1152]{2,1,0:T(8,128)(2,1)S(1)} %collective-permute-done.3.packed_ref, s32[3]{0:T(128)S(1)} %pad_add_fusion.place_ref, ...), custom_call_target="tpu_custom_call" | custom-call | flops 905969664 | bytes 7761940 | tf_op jit(solution)/shard_map/pallas_call | solution.py:33
  58.9 4.6 %collective-permute-start.5 = (f32[2,128,1152]{2,1,0:T(8,128)}, f32[2,128,1152]{2,1,0:T(8,128)S(1)}, u32[]{:S(2)}, u32[]{:S(2)}) collective-permute-start(f32[2,128,1152]{2,1,0:T(8,128)} %get-tuple-element.48), channel_id=1, source_target_pairs={{0,1},{1,0},{2,3},{3,2},{4,5},{5,4},{6,7},{7,6},{8,9},{9,8},{10,11... | collective-permute-start | bytes 3538952 | tf_op jit(solution)/shard_map/ppermute | solution.py:54
  63.5 1.9 %collective-permute-start.6 = (f32[2,128,1152]{2,1,0:T(8,128)}, f32[2,128,1152]{2,1,0:T(8,128)}, u32[]{:S(2)}, u32[]{:S(2)}) collective-permute-start(f32[2,128,1152]{2,1,0:T(8,128)} %get-tuple-element.50), channel_id=1, source_target_pairs={{0,1016},{1,9},{4,1020},{5,13},{8,0},{9,17},{12,4},{13,21},{16,8},... | collective-permute-start | bytes 3538952 | tf_op jit(solution)/shard_map/ppermute | solution.py:50
  65.4 13.9 %all-to-all-start = ((f32[32,1,128]{2,1,0:T(1,128)}), f32[32,1,128]{2,1,0:T(1,128)}, u32[]{:S(2)}, u32[]{:S(2)}) async-start(f32[32,1,128]{2,1,0:T(1,128)} %copy-done.7), calls=%async_computation | async-start | bytes 32768 | tf_op jit(solution)/shard_map/all_to_all | solution.py:231
  79.4 1.1 copy-done.10
  80.4 1.3 %shard_map.98.partial_ref = f32[128,1152]{1,0:T(8,128)S(1)} custom-call(f32[128,1152]{1,0:T(8,128)S(1)} %copy-done.10, f32[2,128,1152]{2,1,0:T(8,128)} %collective-permute-done.4.near_ref), custom_call_target="tpu_custom_call" | custom-call | flops 2000000000 | bytes 2359296 | tf_op jit(solution)/shard_map/pallas_call | solution.py:33
  81.8 1.5 %shard_map.100 = (f32[128,1152]{1,0:T(8,128)}, f32[128,1152]{1,0:T(8,128)S(1)}) custom-call(s32[3]{0:T(128)S(1)} %pad_add_fusion.place_ref, f32[2,128,1152]{2,1,0:T(8,128)S(1)} %get-tuple-element.54.keep_ref, f32[2,128,1152]{2,1,0:T(8,128)S(1)} %collective-permute-done.5.got_ref), custom_call_target="tpu_custom_call" | custom-call | bytes 3538956 | tf_op jit(solution)/shard_map/pallas_call | solution.py:33
  83.2 0.8 copy-done.3
  84.1 4.8 %collective-permute-start.7 = (f32[128,1152]{1,0:T(8,128)}, f32[128,1152]{1,0:T(8,128)S(1)}, u32[]{:S(2)}, u32[]{:S(2)}) collective-permute-start(f32[128,1152]{1,0:T(8,128)} %get-tuple-element.57), channel_id=1, source_target_pairs={{0,2},{2,0},{1,3},{3,1},{4,6},{6,4},{5,7},{7,5},{8,10},{10,8},{9,1... | collective-permute-start | bytes 1769480 | tf_op jit(solution)/shard_map/ppermute | solution.py:54
  88.9 2.0 %collective-permute-done.6.far_ref = f32[2,128,1152]{2,1,0:T(8,128)} collective-permute-done((f32[2,128,1152]{2,1,0:T(8,128)}, f32[2,128,1152]{2,1,0:T(8,128)}, u32[]{:S(2)}, u32[]{:S(2)}) %collective-permute-start.6) | collective-permute-done | bytes 1179680 | tf_op jit(solution)/shard_map/ppermute | solution.py:50
  90.9 2.6 %shard_map.99 = (f32[128,1152]{1,0:T(8,128)S(1)}, f32[128,1152]{1,0:T(8,128)}) custom-call(f32[128,1152]{1,0:T(8,128)S(1)} %shard_map.98.partial_ref, f32[2,128,1152]{2,1,0:T(8,128)} %collective-permute-done.4.near_ref, f32[2,128,1152]{2,1,0:T(8,128)} %collective-permute-done.6.far_ref), custom_call_target="tpu_custom_call" | custom-call | bytes 4128768 | tf_op jit(solution)/shard_map/pallas_call | solution.py:33
  93.5 8.8 %collective-permute-start.8 = (f32[128,1152]{1,0:T(8,128)}, f32[128,1152]{1,0:T(8,128)S(1)}, u32[]{:S(2)}, u32[]{:S(2)}) collective-permute-start(f32[128,1152]{1,0:T(8,128)} %get-tuple-element.59), channel_id=1, source_target_pairs={{0,1},{1,0},{2,3},{3,2},{4,5},{5,4},{6,7},{7,6},{8,9},{9,8},{10,11... | collective-permute-start | bytes 1769480 | tf_op jit(solution)/shard_map/ppermute | solution.py:54
  102.2 0.7 shard_map.96
  102.9 0.6 copy-done.5
  103.6 1.4 %shard_map.97 = f32[32,1,128]{2,1,0:T(1,128)} custom-call(f32[32,1,128]{2,1,0:T(1,128)} %all-to-all-done.row_ref), custom_call_target="tpu_custom_call" | custom-call | flops 6000000000 | bytes 32768 | tf_op jit(solution)/shard_map/pallas_call | solution.py:33
  105.0 5.8 %all-to-all-start.1 = ((f32[32,1,128]{2,1,0:T(1,128)}), f32[32,1,128]{2,1,0:T(1,128)S(1)}, u32[]{:S(2)}, u32[]{:S(2)}) async-start(f32[32,1,128]{2,1,0:T(1,128)} %shard_map.97), calls=%async_computation.1 | async-start | bytes 32768 | tf_op jit(solution)/shard_map/all_to_all | solution.py:241
  110.9 1.1 shard_map.101
  111.9 1.1 shard_map.102
  113.0 4.7 %all-to-all-done.1.row_ref = f32[32,1,128]{2,1,0:T(1,128)S(1)} async-done(((f32[32,1,128]{2,1,0:T(1,128)}), f32[32,1,128]{2,1,0:T(1,128)S(1)}, u32[]{:S(2)}, u32[]{:S(2)}) %all-to-all-start.1) | async-done | bytes 16416 | tf_op jit(solution)/shard_map/all_to_all | solution.py:241
  117.7 0.7 shard_map.103
  (25 shorter events, 0.3 us)
Async XLA Ops:
  0.6 31.5 %copy-start = (bf16[512,1152]{1,0:T(8,128)(2,1)S(1)}, bf16[512,1152]{1,0:T(8,128)(2,1)}, u32[]{:S(2)}) copy-start(bf16[512,1152]{1,0:T(8,128)(2,1)} %texts_ref.3) | copy-start | bytes 3538948
  0.6 19.4 %collective-permute-start = (bf16[128,1152]{1,0:T(8,128)(2,1)}, bf16[128,1152]{1,0:T(8,128)(2,1)S(1)}, u32[]{:S(2)}, u32[]{:S(2)}) collective-permute-start(bf16[128,1152]{1,0:T(8,128)(2,1)} %images_ref.1), channel_id=1, source_target_pairs={{0,1},{1,0},{2,3},{3,2},{4,5},{5,4},{6,7},{7,6},{8,9},{9,8},{10,11... | collective-permute-start | bytes 884744 | tf_op jit(solution)/shard_map/ppermute | solution.py:54
  16.8 3.1 %collective-permute-start.1 = (s32[1,128]{1,0:T(1,128)}, s32[1,128]{1,0:T(1,128)S(1)}, u32[]{:S(2)}, u32[]{:S(2)}) collective-permute-start(s32[1,128]{1,0:T(1,128)} %bitcast.4), channel_id=1, source_target_pairs={{0,1},{1,0},{2,3},{3,2},{4,5},{5,4},{6,7},{7,6},{8,9},{9,8},{10,11... | collective-permute-start | bytes 1544 | tf_op jit(solution)/shard_map/ppermute | solution.py:54
  20.0 1.0 copy-start.1
  21.0 0.7 copy-start.8
  21.8 16.6 %collective-permute-start.2 = (bf16[2,144,1152]{2,1,0:T(8,128)(2,1)S(1)}, bf16[2,144,1152]{2,1,0:T(8,128)(2,1)S(1)}, u32[]{:S(2)}, u32[]{:S(2)}) collective-permute-start(bf16[2,144,1152]{2,1,0:T(8,128)(2,1)S(1)} %shard_map.92.packed_ref), channel_id=1, source_target_pairs={{0,4},{1,1021},{4,8},{5,1},{8,12},{9,5},{12,16},{13,9},{16,20},{17... | collective-permute-start | bytes 1990664 | tf_op jit(solution)/shard_map/ppermute | solution.py:50
  34.6 15.7 %copy-start.9 = (f32[128,1152]{1,0:T(8,128)}, f32[128,1152]{1,0:T(8,128)S(1)}, u32[]{:S(2)}) copy-start(f32[128,1152]{1,0:T(8,128)S(1)} %get-tuple-element.46.own_ref) | copy-start | bytes 1769476
  38.4 15.6 %collective-permute-start.3 = (bf16[2,144,1152]{2,1,0:T(8,128)(2,1)S(1)}, bf16[2,144,1152]{2,1,0:T(8,128)(2,1)S(1)}, u32[]{:S(2)}, u32[]{:S(2)}) collective-permute-start(bf16[2,144,1152]{2,1,0:T(8,128)(2,1)S(1)} %collective-permute-done.2.packed_ref), channel_id=1, source_target_pairs={{0,4},{1,1021},{4,8},{5,1},{8,12},{9,5},{12,16},{13,9},{16,20},{17... | collective-permute-start | bytes 1990664 | tf_op jit(solution)/shard_map/ppermute | solution.py:50
  50.2 29.1 %collective-permute-start.4 = (f32[2,128,1152]{2,1,0:T(8,128)}, f32[2,128,1152]{2,1,0:T(8,128)}, u32[]{:S(2)}, u32[]{:S(2)}) collective-permute-start(f32[2,128,1152]{2,1,0:T(8,128)} %get-tuple-element.47), channel_id=1, source_target_pairs={{0,1020},{1,5},{4,0},{5,9},{8,4},{9,13},{12,8},{13,17},{16,12},{17... | collective-permute-start | bytes 3538952 | tf_op jit(solution)/shard_map/ppermute | solution.py:50
  58.9 6.5 %copy-start.7 = (f32[32,1,128]{2,1,0:T(1,128)}, f32[32,1,128]{2,1,0:T(1,128)S(1)}, u32[]{:S(2)}) copy-start(f32[32,1,128]{2,1,0:T(1,128)S(1)} %get-tuple-element.43) | copy-start | bytes 49156
  58.9 22.9 %collective-permute-start.5 = (f32[2,128,1152]{2,1,0:T(8,128)}, f32[2,128,1152]{2,1,0:T(8,128)S(1)}, u32[]{:S(2)}, u32[]{:S(2)}) collective-permute-start(f32[2,128,1152]{2,1,0:T(8,128)} %get-tuple-element.48), channel_id=1, source_target_pairs={{0,1},{1,0},{2,3},{3,2},{4,5},{5,4},{6,7},{7,6},{8,9},{9,8},{10,11... | collective-permute-start | bytes 3538952 | tf_op jit(solution)/shard_map/ppermute | solution.py:54
  63.5 27.4 %collective-permute-start.6 = (f32[2,128,1152]{2,1,0:T(8,128)}, f32[2,128,1152]{2,1,0:T(8,128)}, u32[]{:S(2)}, u32[]{:S(2)}) collective-permute-start(f32[2,128,1152]{2,1,0:T(8,128)} %get-tuple-element.50), channel_id=1, source_target_pairs={{0,1016},{1,9},{4,1020},{5,13},{8,0},{9,17},{12,4},{13,21},{16,8},... | collective-permute-start | bytes 3538952 | tf_op jit(solution)/shard_map/ppermute | solution.py:50
  65.4 38.1 %all-to-all-start = ((f32[32,1,128]{2,1,0:T(1,128)}), f32[32,1,128]{2,1,0:T(1,128)}, u32[]{:S(2)}, u32[]{:S(2)}) async-start(f32[32,1,128]{2,1,0:T(1,128)} %copy-done.7), calls=%async_computation | async-start | bytes 32768 | tf_op jit(solution)/shard_map/all_to_all | solution.py:231
  79.4 1.1 copy-start.10
  83.2 0.8 copy-start.3
  84.1 26.8 %collective-permute-start.7 = (f32[128,1152]{1,0:T(8,128)}, f32[128,1152]{1,0:T(8,128)S(1)}, u32[]{:S(2)}, u32[]{:S(2)}) collective-permute-start(f32[128,1152]{1,0:T(8,128)} %get-tuple-element.57), channel_id=1, source_target_pairs={{0,2},{2,0},{1,3},{3,1},{4,6},{6,4},{5,7},{7,5},{8,10},{10,8},{9,1... | collective-permute-start | bytes 1769480 | tf_op jit(solution)/shard_map/ppermute | solution.py:54
  93.5 18.5 %collective-permute-start.8 = (f32[128,1152]{1,0:T(8,128)}, f32[128,1152]{1,0:T(8,128)S(1)}, u32[]{:S(2)}, u32[]{:S(2)}) collective-permute-start(f32[128,1152]{1,0:T(8,128)} %get-tuple-element.59), channel_id=1, source_target_pairs={{0,1},{1,0},{2,3},{3,2},{4,5},{5,4},{6,7},{7,6},{8,9},{9,8},{10,11... | collective-permute-start | bytes 1769480 | tf_op jit(solution)/shard_map/ppermute | solution.py:54
  102.9 0.6 copy-start.5
  103.6 7.3 %copy-start.4 = (f32[128,1152]{1,0:T(8,128)S(1)}, f32[128,1152]{1,0:T(8,128)}, u32[]{:S(2)}) copy-start(f32[128,1152]{1,0:T(8,128)} %copy-done.3) | copy-start | bytes 1769476
  103.6 7.3 %copy-start.6 = (f32[128,128]{1,0:T(8,128)S(1)}, f32[128,128]{1,0:T(8,128)}, u32[]{:S(2)}) copy-start(f32[128,128]{1,0:T(8,128)} %copy-done.5) | copy-start | bytes 196612
  105.0 12.7 %all-to-all-start.1 = ((f32[32,1,128]{2,1,0:T(1,128)}), f32[32,1,128]{2,1,0:T(1,128)S(1)}, u32[]{:S(2)}, u32[]{:S(2)}) async-start(f32[32,1,128]{2,1,0:T(1,128)} %shard_map.97), calls=%async_computation.1 | async-start | bytes 32768 | tf_op jit(solution)/shard_map/all_to_all | solution.py:241
  110.8 1.1 copy-start.2

commit v3 on v2

v3 whole, which is shorter than its diff:
```python
import jax
import jax.numpy as jnp
from jax import lax
from jax.experimental import pallas as pl
from jax.experimental.pallas import tpu as pltpu
from jax.sharding import Mesh, PartitionSpec as P

EPS = 1e-06
BLK = ("y_lo", "z", "x")
PLANE = ("y_lo", "x", "y_hi", "core")
SIZES = (2, 32, 4, 2, 2)
WIDTH = 1152
IMAGES = 128
TEXTS = 512
PAD_ROWS = 16
PAIR = 2 * IMAGES
BATCH = 131072
RING = 32
F32 = jnp.float32
BF16 = jnp.bfloat16


def shape(*dims, dtype=F32):
    return jax.ShapeDtypeStruct(dims, dtype)


def call(body, outs, *args, flops=0, smem_in=(), smem_out=(), any_out=(), scratch=()):
    moved = sum(a.size * a.dtype.itemsize for a in args)
    moved += sum(o.size * o.dtype.itemsize for o in outs)
    scalar = pl.BlockSpec(memory_space=pltpu.SMEM)
    vector = pl.BlockSpec(memory_space=pltpu.VMEM)
    placed = pl.BlockSpec(memory_space=pl.ANY)
    return pl.pallas_call(
        body,
        out_shape=outs,
        in_specs=[scalar if k in smem_in else vector for k in range(len(args))],
        out_specs=[scalar if k in smem_out else placed if k in any_out else vector for k in range(len(outs))],
        scratch_shapes=list(scratch),
        compiler_params=pltpu.CompilerParams(vmem_limit_bytes=20 * 1024 * 1024),
        cost_estimate=pl.CostEstimate(flops=flops, bytes_accessed=moved, transcendentals=0),
    )(*args)


def to_side(value, by):
    count = lax.axis_size(BLK)
    pairs = []
    for shard in range(count):
        pairs.append((2 * shard, 2 * ((shard + by) % count)))
        pairs.append((2 * shard + 1, 2 * ((shard - by) % count) + 1))
    return lax.ppermute(value, BLK + ("core",), pairs)


def swapped(value, axis):
    return lax.ppermute(value, axis, [(0, 1), (1, 0)])


def normalized(values):
    full = values.astype(F32)
    factor = lax.rsqrt(jnp.sum(full * full, axis=-1, keepdims=True) + EPS)
    return full * factor, factor


def back_normal(unit_f, factor, dunit):
    return factor * (dunit - unit_f * jnp.sum(unit_f * dunit, axis=-1, keepdims=True))


def pack_kernel(images_ref, positive_ref, out_ref):
    unit, _ = normalized(images_ref[...])
    out_ref[:IMAGES, :] = unit.astype(BF16)
    pos = positive_ref[...]
    row = lax.broadcasted_iota(jnp.int32, (PAD_ROWS, IMAGES), 0)
    digit = jnp.where(row == 0, pos >> 12, jnp.where(row == 1, (pos >> 6) & 63, pos & 63))
    out_ref[IMAGES:, :] = jnp.zeros((PAD_ROWS, WIDTH), BF16)
    out_ref[IMAGES:, :IMAGES] = digit.astype(F32).astype(BF16)


def stack_kernel(mine_ref, other_ref, out_ref):
    out_ref[:IMAGES, :] = mine_ref[:IMAGES, :]
    out_ref[IMAGES:PAIR, :] = other_ref[:IMAGES, :]
    out_ref[PAIR:, :] = mine_ref[IMAGES:, :]
    out_ref[PAIR:, IMAGES:PAIR] = other_ref[IMAGES:, :IMAGES]


def pair_block(packed_ref, text_unit, place_ref, temp_ref, bias_ref):
    count = packed_ref.shape[0] - PAD_ROWS
    unit = packed_ref[:count, :]
    digits = packed_ref[count:, :count].astype(F32).astype(jnp.int32)
    row = lax.broadcasted_iota(jnp.int32, (PAD_ROWS, count), 0)
    weight = jnp.where(row == 0, 4096, jnp.where(row == 1, 64, jnp.where(row == 2, 1, 0)))
    pos = jnp.sum(digits * weight, axis=0, keepdims=True) - place_ref[0]
    sim = lax.dot_general(text_unit, unit, (((1,), (1,)), ((), ())), preferred_element_type=F32)
    scale = jnp.exp(jnp.full((1, count), temp_ref[0], F32))
    logit = scale * sim + bias_ref[0]
    matching = lax.broadcasted_iota(jnp.int32, (TEXTS, count), 0) == pos
    against = jnp.where(matching, -logit, logit)
    small = jnp.exp(-jnp.abs(against))
    soft = jnp.maximum(against, 0.0) + jnp.log1p(small)
    sigmoid = jnp.where(against >= 0, 1.0, small) / (1.0 + small)
    grads = jnp.where(matching, -sigmoid, sigmoid)
    sums = [jnp.sum(v, axis=0, keepdims=True) for v in (soft, grads, grads * sim)]
    tile = jnp.concatenate(sums + [jnp.zeros((5, count), F32)], axis=0)
    for first in range(IMAGES, count, IMAGES):
        tile = tile[:, :IMAGES] + tile[:, first:first + IMAGES]
    return unit, grads.astype(BF16), tile


def image_part(grads, text_unit):
    return lax.dot_general(grads, text_unit, (((0,), (0,)), ((), ())), preferred_element_type=F32)


def text_part(grads, unit):
    return jnp.dot(grads, unit, preferred_element_type=F32)


def own_kernel(texts_ref, packed_ref, place_ref, temp_ref, bias_ref, text_ref, dx_ref, dy_ref, sums_ref):
    unit, _ = normalized(texts_ref[...])
    text_ref[...] = unit.astype(BF16)
    text_unit = text_ref[...]
    unit, grads, sums_ref[...] = pair_block(packed_ref, text_unit, place_ref, temp_ref, bias_ref)
    dx_ref[...] = image_part(grads, text_unit)
    dy_ref[...] = text_part(grads, unit)


def near_kernel(text_ref, packed_ref, place_ref, temp_ref, bias_ref, old_dy_ref, old_sums_ref,
                dx_ref, dy_ref, sums_ref, staged, sem):
    text_unit = text_ref[...]
    unit, grads, tile = pair_block(packed_ref, text_unit, place_ref, temp_ref, bias_ref)
    staged[...] = image_part(grads, text_unit)
    copy = pltpu.make_async_copy(staged, dx_ref, sem)
    copy.start()
    dy_ref[...] = old_dy_ref[...] + text_part(grads, unit)
    sums_ref[...] = old_sums_ref[...] + tile
    copy.wait()


def far_kernel(text_ref, packed_ref, place_ref, temp_ref, bias_ref, old_dy_ref, old_sums_ref,
               dx_ref, send_ref, keep_ref, row_ref, staged, sem, total):
    text_unit = text_ref[...]
    unit, grads, tile = pair_block(packed_ref, text_unit, place_ref, temp_ref, bias_ref)
    staged[...] = image_part(grads, text_unit)
    copy = pltpu.make_async_copy(staged, dx_ref, sem)
    copy.start()
    total[...] = old_dy_ref[...] + text_part(grads, unit)
    core = place_ref[2]
    for out_ref, owner in ((send_ref, 1 - core), (keep_ref, core)):
        for half in range(2):
            first = pl.multiple_of((2 * half + owner) * IMAGES, IMAGES)
            out_ref[half] = total[pl.ds(first, IMAGES), :]
    totals = jnp.sum(old_sums_ref[...] + tile, axis=1, keepdims=True)
    lane = lax.broadcasted_iota(jnp.int32, (1, IMAGES), 1)
    row = sum(jnp.where(lane == k, totals[k:k + 1], 0.0) for k in range(3))
    row_ref[...] = jnp.broadcast_to(row[None], row_ref.shape)
    copy.wait()


def halve_kernel(place_ref, keep_ref, got_ref, send_ref, rest_ref):
    mine = place_ref[1]
    send_ref[...] = keep_ref[1 - mine] + got_ref[1 - mine]
    rest_ref[...] = keep_ref[mine] + got_ref[mine]


def prepare_kernel(place_ref, texts_ref, unit_ref, factor_ref):
    first = pl.multiple_of((2 * place_ref[1] + place_ref[2]) * IMAGES, IMAGES)
    unit_ref[...], factor = normalized(texts_ref[pl.ds(first, IMAGES), :])
    factor_ref[...] = jnp.broadcast_to(factor, factor_ref.shape)


def text_end_kernel(temp_ref, unit_ref, factor_ref, rest_ref, got_ref, out_ref):
    scale = jnp.exp(jnp.full((1, WIDTH), temp_ref[0], F32))
    out_ref[...] = back_normal(unit_ref[...], factor_ref[:, :1], scale * (rest_ref[...] + got_ref[...]))


def join_kernel(own_ref, near_ref, far_ref, mine_ref, other_ref):
    mine_ref[...] = own_ref[...] + near_ref[:IMAGES, :] + far_ref[:IMAGES, :]
    other_ref[...] = near_ref[IMAGES:, :] + far_ref[IMAGES:, :]


def image_end_kernel(temp_ref, images_ref, mine_ref, got_ref, out_ref):
    unit, factor = normalized(images_ref[...])
    scale = jnp.exp(jnp.full((1, WIDTH), temp_ref[0], F32))
    out_ref[...] = back_normal(unit, factor, scale * (mine_ref[...] + got_ref[...]))


def again_kernel(row_ref, out_ref):
    total = jnp.sum(row_ref[...], axis=0, keepdims=True)
    out_ref[...] = jnp.broadcast_to(total, out_ref.shape)


def sums_end_kernel(temp_ref, row_ref, loss_ref, temp_grad_ref, bias_grad_ref):
    total = jnp.sum(row_ref[...], axis=0)
    lane = lax.broadcasted_iota(jnp.int32, (1, IMAGES), 1)
    scale = jnp.exp(jnp.full((1, IMAGES), temp_ref[0], F32))
    loss_ref[0] = jnp.sum(jnp.where(lane == 0, total, 0.0)) * (1.0 / BATCH)
    bias_grad_ref[0] = jnp.sum(jnp.where(lane == 1, total, 0.0))
    temp_grad_ref[0] = jnp.sum(jnp.where(lane == 2, total * scale, 0.0))


def per_device(images, texts, positive, temp_log, bias_arg):
    place = jnp.stack([lax.axis_index(BLK) * TEXTS, lax.axis_index("y_hi"), lax.axis_index("core")]).astype(jnp.int32)
    block_flops = 6 * TEXTS * IMAGES * WIDTH
    positive = positive.reshape(1, IMAGES)
    (mine,) = call(pack_kernel, [shape(IMAGES + PAD_ROWS, WIDTH, dtype=BF16)], images, positive)
    (packed,) = call(stack_kernel, [shape(PAIR + PAD_ROWS, WIDTH, dtype=BF16)], mine, swapped(mine, "core"))
    near = to_side(packed, 1)
    text_unit, dx0, dy, sums = call(
        own_kernel,
        [shape(TEXTS, WIDTH, dtype=BF16), shape(IMAGES, WIDTH), shape(TEXTS, WIDTH), shape(8, IMAGES)],
        texts, mine, place, temp_log, bias_arg, flops=block_flops, smem_in=(2, 3, 4),
    )
    near, text_unit = lax.optimization_barrier((near, text_unit))
    far = to_side(near, 1)
    staging = [pltpu.VMEM((PAIR, WIDTH), F32), pltpu.SemaphoreType.DMA(())]
    near_dx, dy, sums = call(
        near_kernel, [shape(PAIR, WIDTH), shape(TEXTS, WIDTH), shape(8, IMAGES)],
        text_unit, near, place, temp_log, bias_arg, dy, sums,
        flops=2 * block_flops, smem_in=(2, 3, 4), any_out=(0,), scratch=staging,
    )
    near_dx = to_side(near_dx, -1)
    far_dx, send, keep, row = call(
        far_kernel, [shape(PAIR, WIDTH)] + [shape(2, IMAGES, WIDTH)] * 2 + [shape(RING, 1, IMAGES)],
        text_unit, far, place, temp_log, bias_arg, dy, sums,
        flops=2 * block_flops, smem_in=(2, 3, 4), any_out=(0,),
        scratch=staging + [pltpu.VMEM((TEXTS, WIDTH), F32)],
    )
    far_dx = to_side(far_dx, -2)
    got = swapped(send, "core")
    row = lax.all_to_all(row, "z", 0, 0, tiled=True)
    near_dx, got = lax.optimization_barrier((near_dx, got))
    send, rest = call(halve_kernel, [shape(IMAGES, WIDTH)] * 2, place, keep, got, smem_in=(0,))
    got = swapped(send, "y_hi")
    unit, factor = call(
        prepare_kernel, [shape(IMAGES, WIDTH), shape(IMAGES, IMAGES)], place, texts, smem_in=(0,)
    )
    row, unit = lax.optimization_barrier((row, unit))
    (row,) = call(again_kernel, [shape(RING, 1, IMAGES)], row, flops=5 * 10**9)
    row = lax.all_to_all(row, PLANE, 0, 0, tiled=True)
    mine, other = call(join_kernel, [shape(IMAGES, WIDTH)] * 2, dx0, near_dx, far_dx)
    other = swapped(other, "core")
    (text_grad,) = call(
        text_end_kernel, [shape(IMAGES, WIDTH)], temp_log, unit, factor, rest, got,
        smem_in=(0,), flops=8 * 10**9,
    )
    mine, text_grad = lax.optimization_barrier((mine, text_grad))
    (image_grad,) = call(
        image_end_kernel, [shape(IMAGES, WIDTH)], temp_log, images, mine, other, smem_in=(0,)
    )
    row, image_grad, text_grad = lax.optimization_barrier((row, image_grad, text_grad))
    loss, temp_grad, bias_grad = call(
        sums_end_kernel, [shape(1)] * 3, temp_log, row, smem_in=(0,), smem_out=(0, 1, 2)
    )
    return (loss, image_grad, text_grad, temp_grad, bias_grad)


def solution(mesh):
    axes = BLK + ("y_hi", "core")
    fine = Mesh(mesh.devices.reshape(SIZES), axes)
    placed = (P(axes, None), P(BLK, None), P(axes), P(), P())
    return jax.shard_map(
        per_device,
        mesh=fine,
        in_specs=placed,
        out_specs=(P(), P(axes, None), P(axes, None), P(), P()),
        check_vma=False,
    )
```

time: 119 us -> 115 us (0.966)
  waiting for transfers between devices: 13.6 us -> 18.9 us
  starting transfers between devices: 76.8 us -> 71.6 us
  Pallas kernels: 21.6 us -> 18.3 us
    all_to_all x1, waiting for transfers between devices: 0.01 us -> 12.7 us  [per_device(): row = lax.all_to_all(row, 'z', 0, 0, tiled=True)]
    ppermute x5 -> x4, starting transfers between devices: 36.3 us -> 27.9 us  [swapped(): return lax.ppermute(value, axis, [(0, 1), (1, 0)])]
    all_to_all x1, waiting for transfers between devices: 4.73 us -> 0.07 us  [per_device(): row = lax.all_to_all(row, PLANE, 0, 0, tiled=True)]
    ppermute x4, waiting for transfers between devices: 7.66 us -> 4.27 us  [to_side(): return lax.ppermute(value, BLK + ('core',), pairs)]
    pallas_call x12, Pallas kernels: 21.6 us -> 18.3 us  [call(): pl.pallas_call(body, out_shape=outs, in_specs=[scalar if k in smem_in els...]
    all_to_all x1, starting transfers between devices: 5.82 us -> 9.09 us  [per_device(): row = lax.all_to_all(row, PLANE, 0, 0, tiled=True)]
    unnamed x22 -> x20, local copies, waits for them, and re-layouts: 4.14 us -> 3.91 us
  transfers between devices with their start and end apart: 11 -> 10, of which waited for: 5 -> 6; matrix products, arithmetic and copies ran while one was open for 0% -> 0% of each run, Pallas kernels for 17% -> 15%
where the time goes in v3:
time: 115 us
  starting transfers between devices  71.6 us (62%)
  waiting for transfers between devices  18.9 us (16%)
  Pallas kernels  18.3 us (16%)
  local copies, waits for them, and re-layouts  3.91 us (3%)
  between operations  2.15 us (2%)
    ppermute x4, starting transfers between devices, swapped(): return lax.ppermute(value, axis, [(0, 1), (1, 0)])  27.9 us
    ppermute x4, starting transfers between devices, to_side(): return lax.ppermute(value, BLK + ('core',), pairs)  20.8 us
    pallas_call x12, Pallas kernels, call(): pl.pallas_call(body, out_shape=outs, in_specs=[scalar if k in smem_in els...  18.3 us
    all_to_all x1, starting transfers between devices, per_device(): row = lax.all_to_all(row, 'z', 0, 0, tiled=True)  13.8 us
    all_to_all x1, waiting for transfers between devices, per_device(): row = lax.all_to_all(row, 'z', 0, 0, tiled=True)  12.7 us
    all_to_all x1, starting transfers between devices, per_device(): row = lax.all_to_all(row, PLANE, 0, 0, tiled=True)  9.09 us
    ppermute x4, waiting for transfers between devices, to_side(): return lax.ppermute(value, BLK + ('core',), pairs)  4.27 us
    unnamed x20, local copies, waits for them, and re-layouts  3.91 us
  transfers between devices with their start and end apart: 10, of which 6 were waited for; matrix products, arithmetic and copies ran while one was open for 0% of the time, Pallas kernels for 15%

profile of v3, /device:TPU:1, one launch (start us, length us, event | category | flops | bytes accessed | tf_op | source)
XLA Modules:
  0.0 114.9 jit_solution(14657161263159243930)
XLA Ops:
  0.6 1.0 copy-done
  1.6 0.7 copy-done.7
  2.3 0.1 shard_map.92.mine_ref.packed_ref
  2.4 16.2 %collective-permute-start = (bf16[144,1152]{1,0:T(8,128)(2,1)S(1)}, bf16[144,1152]{1,0:T(8,128)(2,1)S(1)}, u32[]{:S(2)}, u32[]{:S(2)}) collective-permute-start(bf16[144,1152]{1,0:T(8,128)(2,1)S(1)} %shard_map.92.mine_ref.packed_ref), channel_id=1, source_target_pairs={{0,1},{1,0},{2,3},{3,2},{4,5},{5,4},{6,7},{7,6},{8,9},{9,8},{10,11... | collective-permute-start | bytes 995336 | tf_op jit(solution)/shard_map/ppermute | solution.py:54
  18.6 1.2 %collective-permute-done.other_ref = bf16[144,1152]{1,0:T(8,128)(2,1)S(1)} collective-permute-done((bf16[144,1152]{1,0:T(8,128)(2,1)S(1)}, bf16[144,1152]{1,0:T(8,128)(2,1)S(1)}, u32[]{:S(2)}, u32[]{:S(2)}) %collective-permute-start) | collective-permute-done | bytes 331808 | tf_op jit(solution)/shard_map/ppermute | solution.py:54
  19.9 9.0 %collective-permute-start.1 = (bf16[272,1152]{1,0:T(8,128)(2,1)S(1)}, bf16[272,1152]{1,0:T(8,128)(2,1)S(1)}, u32[]{:S(2)}, u32[]{:S(2)}) collective-permute-start(bf16[272,1152]{1,0:T(8,128)(2,1)S(1)} %shard_map.93), channel_id=1, source_target_pairs={{0,4},{1,1021},{4,8},{5,1},{8,12},{9,5},{12,16},{13,9},{16,20},{17... | collective-permute-start | bytes 1880072 | tf_op jit(solution)/shard_map/ppermute | solution.py:50
  30.2 0.1 pad_add_fusion.place_ref
  30.2 2.4 %shard_map.94 = (bf16[512,1152]{1,0:T(8,128)(2,1)S(1)}, f32[128,1152]{1,0:T(8,128)S(1)}, f32[512,1152]{1,0:T(8,128)S(1)}, f32[8,128]{1,0:T(8,128)S(1)}) custom-call(bf16[512,1152]{1,0:T(8,128)(2,1)S(1)} %copy-done.2, bf16[144,1152]{1,0:T(8,128)(2,1)S(1)} %shard_map.92.mine_ref.packed_ref, s32[3]{0:T(128)S(1)} %pad_add_fusion.place_ref, f32[1]{0:T(128)S(6)} %copy.10.temp_ref, ...), custom_call_target="tpu_custom_call" | custom-call | flops 452984832 | bytes 5644308 | tf_op jit(solution)/shard_map/pallas_call | solution.py:33
  32.7 0.8 copy-done.3
  33.5 2.6 %collective-permute-done.1.packed_ref = bf16[272,1152]{1,0:T(8,128)(2,1)S(1)} collective-permute-done((bf16[272,1152]{1,0:T(8,128)(2,1)S(1)}, bf16[272,1152]{1,0:T(8,128)(2,1)S(1)}, u32[]{:S(2)}, u32[]{:S(2)}) %collective-permute-start.1) | collective-permute-done | bytes 626720 | tf_op jit(solution)/shard_map/ppermute | solution.py:50
  36.1 8.0 %collective-permute-start.2 = (bf16[272,1152]{1,0:T(8,128)(2,1)S(1)}, bf16[272,1152]{1,0:T(8,128)(2,1)S(1)}, u32[]{:S(2)}, u32[]{:S(2)}) collective-permute-start(bf16[272,1152]{1,0:T(8,128)(2,1)S(1)} %collective-permute-done.1.packed_ref), channel_id=1, source_target_pairs={{0,4},{1,1021},{4,8},{5,1},{8,12},{9,5},{12,16},{13,9},{16,20},{17... | collective-permute-start | bytes 1880072 | tf_op jit(solution)/shard_map/ppermute | solution.py:50
  44.1 3.6 %shard_map.95 = (f32[256,1152]{1,0:T(8,128)}, f32[512,1152]{1,0:T(8,128)S(1)}, f32[8,128]{1,0:T(8,128)S(1)}) custom-call(bf16[512,1152]{1,0:T(8,128)(2,1)S(1)} %get-tuple-element.37.text_ref, bf16[272,1152]{1,0:T(8,128)(2,1)S(1)} %collective-permute-done.1.packed_ref, s32[3]{0:T(128)S(1)} %pad_add_fusion.place_ref, f32[1]{0:T(128)S(6)} %copy.10.temp_ref, ...), custom_call_target="tpu_custom_call" | custom-call | flops 905969664 | bytes 7712788 | tf_op jit(solution)/shard_map/pallas_call | solution.py:33
  47.7 1.9 %collective-permute-start.3 = (f32[256,1152]{1,0:T(8,128)}, f32[256,1152]{1,0:T(8,128)}, u32[]{:S(2)}, u32[]{:S(2)}) collective-permute-start(f32[256,1152]{1,0:T(8,128)} %get-tuple-element.47), channel_id=1, source_target_pairs={{0,1020},{1,5},{4,0},{5,9},{8,4},{9,13},{12,8},{13,17},{16,12},{17... | collective-permute-start | bytes 3538952 | tf_op jit(solution)/shard_map/ppermute | solution.py:50
  49.6 1.7 %collective-permute-done.2.packed_ref = bf16[272,1152]{1,0:T(8,128)(2,1)S(1)} collective-permute-done((bf16[272,1152]{1,0:T(8,128)(2,1)S(1)}, bf16[272,1152]{1,0:T(8,128)(2,1)S(1)}, u32[]{:S(2)}, u32[]{:S(2)}) %collective-permute-start.2) | collective-permute-done | bytes 626720 | tf_op jit(solution)/shard_map/ppermute | solution.py:50
  51.3 4.6 %shard_map.96 = (f32[256,1152]{1,0:T(8,128)}, f32[2,128,1152]{2,1,0:T(8,128)}, f32[2,128,1152]{2,1,0:T(8,128)S(1)}, f32[32,1,128]{2,1,0:T(1,128)}) custom-call(bf16[512,1152]{1,0:T(8,128)(2,1)S(1)} %get-tuple-element.37.text_ref, bf16[272,1152]{1,0:T(8,128)(2,1)S(1)} %collective-permute-done.2.packed_ref, s32[3]{0:T(128)S(1)} %pad_add_fusion.place_ref, ...), custom_call_target="tpu_custom_call" | custom-call | flops 905969664 | bytes 7725076 | tf_op jit(solution)/shard_map/pallas_call | solution.py:33
  55.9 4.8 %collective-permute-start.4 = (f32[2,128,1152]{2,1,0:T(8,128)}, f32[2,128,1152]{2,1,0:T(8,128)S(1)}, u32[]{:S(2)}, u32[]{:S(2)}) collective-permute-start(f32[2,128,1152]{2,1,0:T(8,128)} %get-tuple-element.48), channel_id=1, source_target_pairs={{0,1},{1,0},{2,3},{3,2},{4,5},{5,4},{6,7},{7,6},{8,9},{9,8},{10,11... | collective-permute-start | bytes 3538952 | tf_op jit(solution)/shard_map/ppermute | solution.py:54
  60.7 1.9 %collective-permute-start.5 = (f32[256,1152]{1,0:T(8,128)}, f32[256,1152]{1,0:T(8,128)}, u32[]{:S(2)}, u32[]{:S(2)}) collective-permute-start(f32[256,1152]{1,0:T(8,128)} %get-tuple-element.50), channel_id=1, source_target_pairs={{0,1016},{1,9},{4,1020},{5,13},{8,0},{9,17},{12,4},{13,21},{16,8},... | collective-permute-start | bytes 3538952 | tf_op jit(solution)/shard_map/ppermute | solution.py:50
  62.6 13.8 %all-to-all-start = ((f32[32,1,128]{2,1,0:T(1,128)}), f32[32,1,128]{2,1,0:T(1,128)S(1)}, u32[]{:S(2)}, u32[]{:S(2)}) async-start(f32[32,1,128]{2,1,0:T(1,128)} %get-tuple-element.43), calls=%async_computation | async-start | bytes 32768 | tf_op jit(solution)/shard_map/all_to_all | solution.py:227
  76.4 0.6 copy-done.6
  77.1 1.5 %shard_map.100 = (f32[128,1152]{1,0:T(8,128)}, f32[128,1152]{1,0:T(8,128)S(1)}) custom-call(s32[3]{0:T(128)S(1)} %copy-done.6, f32[2,128,1152]{2,1,0:T(8,128)S(1)} %get-tuple-element.54.keep_ref, f32[2,128,1152]{2,1,0:T(8,128)S(1)} %collective-permute-done.4.got_ref), custom_call_target="tpu_custom_call" | custom-call | bytes 3538956 | tf_op jit(solution)/shard_map/pallas_call | solution.py:33
  78.6 0.8 copy-done.8
  79.4 4.8 %collective-permute-start.6 = (f32[128,1152]{1,0:T(8,128)}, f32[128,1152]{1,0:T(8,128)S(1)}, u32[]{:S(2)}, u32[]{:S(2)}) collective-permute-start(f32[128,1152]{1,0:T(8,128)} %get-tuple-element.57), channel_id=1, source_target_pairs={{0,2},{2,0},{1,3},{3,1},{4,6},{6,4},{5,7},{7,5},{8,10},{10,8},{9,1... | collective-permute-start | bytes 1769480 | tf_op jit(solution)/shard_map/ppermute | solution.py:54
  84.2 0.7 shard_map.97
  84.9 12.7 %all-to-all-done.row_ref = f32[32,1,128]{2,1,0:T(1,128)S(1)} async-done(((f32[32,1,128]{2,1,0:T(1,128)}), f32[32,1,128]{2,1,0:T(1,128)S(1)}, u32[]{:S(2)}, u32[]{:S(2)}) %all-to-all-start) | async-done | bytes 16416 | tf_op jit(solution)/shard_map/all_to_all | solution.py:227
  97.6 0.6 shard_map.98
  98.2 9.1 %all-to-all-start.1 = ((f32[32,1,128]{2,1,0:T(1,128)}), f32[32,1,128]{2,1,0:T(1,128)S(1)}, u32[]{:S(2)}, u32[]{:S(2)}) async-start(f32[32,1,128]{2,1,0:T(1,128)} %shard_map.98), calls=%async_computation.1 | async-start | bytes 32768 | tf_op jit(solution)/shard_map/all_to_all | solution.py:236
  107.3 1.8 %shard_map.99 = (f32[128,1152]{1,0:T(8,128)S(1)}, f32[128,1152]{1,0:T(8,128)S(1)}) custom-call(f32[128,1152]{1,0:T(8,128)S(1)} %copy-done.4, f32[256,1152]{1,0:T(8,128)} %collective-permute-done.3.near_ref, f32[256,1152]{1,0:T(8,128)} %collective-permute-done.5.far_ref), custom_call_target="tpu_custom_call" | custom-call | bytes 4128768 | tf_op jit(solution)/shard_map/pallas_call | solution.py:33
  109.2 2.1 %collective-permute-start.7 = (f32[128,1152]{1,0:T(8,128)S(1)}, f32[128,1152]{1,0:T(8,128)S(1)}, u32[]{:S(2)}, u32[]{:S(2)}) collective-permute-start(f32[128,1152]{1,0:T(8,128)S(1)} %get-tuple-element.59), channel_id=1, source_target_pairs={{0,1},{1,0},{2,3},{3,2},{4,5},{5,4},{6,7},{7,6},{8,9},{9,8},{10,11... | collective-permute-start | bytes 1769480 | tf_op jit(solution)/shard_map/ppermute | solution.py:54
  111.4 1.1 shard_map.101
  112.4 0.7 collective-permute-done.7.got_ref
  113.1 1.1 shard_map.102
  114.2 0.7 shard_map.103
  (21 shorter events, 0.2 us)
Async XLA Ops:
  0.6 1.0 copy-start
  1.6 0.7 copy-start.7
  2.3 28.0 %copy-start.2 = (bf16[512,1152]{1,0:T(8,128)(2,1)S(1)}, bf16[512,1152]{1,0:T(8,128)(2,1)}, u32[]{:S(2)}) copy-start(bf16[512,1152]{1,0:T(8,128)(2,1)} %texts_ref.3) | copy-start | bytes 3538948
  2.4 17.4 %collective-permute-start = (bf16[144,1152]{1,0:T(8,128)(2,1)S(1)}, bf16[144,1152]{1,0:T(8,128)(2,1)S(1)}, u32[]{:S(2)}, u32[]{:S(2)}) collective-permute-start(bf16[144,1152]{1,0:T(8,128)(2,1)S(1)} %shard_map.92.mine_ref.packed_ref), channel_id=1, source_target_pairs={{0,1},{1,0},{2,3},{3,2},{4,5},{5,4},{6,7},{7,6},{8,9},{9,8},{10,11... | collective-permute-start | bytes 995336 | tf_op jit(solution)/shard_map/ppermute | solution.py:54
  19.9 16.2 %collective-permute-start.1 = (bf16[272,1152]{1,0:T(8,128)(2,1)S(1)}, bf16[272,1152]{1,0:T(8,128)(2,1)S(1)}, u32[]{:S(2)}, u32[]{:S(2)}) collective-permute-start(bf16[272,1152]{1,0:T(8,128)(2,1)S(1)} %shard_map.93), channel_id=1, source_target_pairs={{0,4},{1,1021},{4,8},{5,1},{8,12},{9,5},{12,16},{13,9},{16,20},{17... | collective-permute-start | bytes 1880072 | tf_op jit(solution)/shard_map/ppermute | solution.py:50
  30.2 21.1 %copy-start.5 = (s32[3]{0:T(128)}, s32[3]{0:T(128)S(1)}, u32[]{:S(2)}) copy-start(s32[3]{0:T(128)S(1)} %pad_add_fusion.place_ref) | copy-start | bytes 40
  32.6 0.8 copy-start.3
  36.1 15.2 %collective-permute-start.2 = (bf16[272,1152]{1,0:T(8,128)(2,1)S(1)}, bf16[272,1152]{1,0:T(8,128)(2,1)S(1)}, u32[]{:S(2)}, u32[]{:S(2)}) collective-permute-start(bf16[272,1152]{1,0:T(8,128)(2,1)S(1)} %collective-permute-done.1.packed_ref), channel_id=1, source_target_pairs={{0,4},{1,1021},{4,8},{5,1},{8,12},{9,5},{12,16},{13,9},{16,20},{17... | collective-permute-start | bytes 1880072 | tf_op jit(solution)/shard_map/ppermute | solution.py:50
  47.7 28.7 %collective-permute-start.3 = (f32[256,1152]{1,0:T(8,128)}, f32[256,1152]{1,0:T(8,128)}, u32[]{:S(2)}, u32[]{:S(2)}) collective-permute-start(f32[256,1152]{1,0:T(8,128)} %get-tuple-element.47), channel_id=1, source_target_pairs={{0,1020},{1,5},{4,0},{5,9},{8,4},{9,13},{12,8},{13,17},{16,12},{17... | collective-permute-start | bytes 3538952 | tf_op jit(solution)/shard_map/ppermute | solution.py:50
  55.9 20.5 %collective-permute-start.4 = (f32[2,128,1152]{2,1,0:T(8,128)}, f32[2,128,1152]{2,1,0:T(8,128)S(1)}, u32[]{:S(2)}, u32[]{:S(2)}) collective-permute-start(f32[2,128,1152]{2,1,0:T(8,128)} %get-tuple-element.48), channel_id=1, source_target_pairs={{0,1},{1,0},{2,3},{3,2},{4,5},{5,4},{6,7},{7,6},{8,9},{9,8},{10,11... | collective-permute-start | bytes 3538952 | tf_op jit(solution)/shard_map/ppermute | solution.py:54
  60.7 46.6 %collective-permute-start.5 = (f32[256,1152]{1,0:T(8,128)}, f32[256,1152]{1,0:T(8,128)}, u32[]{:S(2)}, u32[]{:S(2)}) collective-permute-start(f32[256,1152]{1,0:T(8,128)} %get-tuple-element.50), channel_id=1, source_target_pairs={{0,1016},{1,9},{4,1020},{5,13},{8,0},{9,17},{12,4},{13,21},{16,8},... | collective-permute-start | bytes 3538952 | tf_op jit(solution)/shard_map/ppermute | solution.py:50
  62.6 35.0 %all-to-all-start = ((f32[32,1,128]{2,1,0:T(1,128)}), f32[32,1,128]{2,1,0:T(1,128)S(1)}, u32[]{:S(2)}, u32[]{:S(2)}) async-start(f32[32,1,128]{2,1,0:T(1,128)} %get-tuple-element.43), calls=%async_computation | async-start | bytes 32768 | tf_op jit(solution)/shard_map/all_to_all | solution.py:227
  76.4 0.7 copy-start.6
  78.6 0.8 copy-start.8
  79.4 32.0 %collective-permute-start.6 = (f32[128,1152]{1,0:T(8,128)}, f32[128,1152]{1,0:T(8,128)S(1)}, u32[]{:S(2)}, u32[]{:S(2)}) collective-permute-start(f32[128,1152]{1,0:T(8,128)} %get-tuple-element.57), channel_id=1, source_target_pairs={{0,2},{2,0},{1,3},{3,1},{4,6},{6,4},{5,7},{7,5},{8,10},{10,8},{9,1... | collective-permute-start | bytes 1769480 | tf_op jit(solution)/shard_map/ppermute | solution.py:54
  97.6 9.8 %copy-start.4 = (f32[128,1152]{1,0:T(8,128)S(1)}, f32[128,1152]{1,0:T(8,128)}, u32[]{:S(2)}) copy-start(f32[128,1152]{1,0:T(8,128)} %copy-done.3) | copy-start | bytes 1769476
  98.2 16.0 %all-to-all-start.1 = ((f32[32,1,128]{2,1,0:T(1,128)}), f32[32,1,128]{2,1,0:T(1,128)S(1)}, u32[]{:S(2)}, u32[]{:S(2)}) async-start(f32[32,1,128]{2,1,0:T(1,128)} %shard_map.98), calls=%async_computation.1 | async-start | bytes 32768 | tf_op jit(solution)/shard_map/all_to_all | solution.py:236
  107.3 4.0 %copy-start.9 = (f32[128,1152]{1,0:T(8,128)S(1)}, f32[128,1152]{1,0:T(8,128)}, u32[]{:S(2)}) copy-start(f32[128,1152]{1,0:T(8,128)} %copy-done.8) | copy-start | bytes 1769476
  109.2 3.9 %collective-permute-start.7 = (f32[128,1152]{1,0:T(8,128)S(1)}, f32[128,1152]{1,0:T(8,128)S(1)}, u32[]{:S(2)}, u32[]{:S(2)}) collective-permute-start(f32[128,1152]{1,0:T(8,128)S(1)} %get-tuple-element.59), channel_id=1, source_target_pairs={{0,1},{1,0},{2,3},{3,2},{4,5},{5,4},{6,7},{7,6},{8,9},{9,8},{10,11... | collective-permute-start | bytes 1769480 | tf_op jit(solution)/shard_map/ppermute | solution.py:54
  111.3 1.7 %copy-start.1 = (bf16[128,1152]{1,0:T(8,128)(2,1)S(1)}, bf16[128,1152]{1,0:T(8,128)(2,1)}, u32[]{:S(2)}) copy-start(bf16[128,1152]{1,0:T(8,128)(2,1)} %images_ref.3) | copy-start | bytes 884740

commit v4 on v3

--- a/solution.py
+++ b/solution.py
@@ -74,17 +74,10 @@
     out_ref[IMAGES:, :IMAGES] = digit.astype(F32).astype(BF16)
 
 
-def stack_kernel(mine_ref, other_ref, out_ref):
-    out_ref[:IMAGES, :] = mine_ref[:IMAGES, :]
-    out_ref[IMAGES:PAIR, :] = other_ref[:IMAGES, :]
-    out_ref[PAIR:, :] = mine_ref[IMAGES:, :]
-    out_ref[PAIR:, IMAGES:PAIR] = other_ref[IMAGES:, :IMAGES]
-
-
-def pair_block(packed_ref, text_unit, place_ref, temp_ref, bias_ref):
-    count = packed_ref.shape[0] - PAD_ROWS
-    unit = packed_ref[:count, :]
-    digits = packed_ref[count:, :count].astype(F32).astype(jnp.int32)
+def pair_block(packed_refs, text_unit, place_ref, temp_ref, bias_ref):
+    count = len(packed_refs) * IMAGES
+    unit = jnp.concatenate([ref[:IMAGES, :] for ref in packed_refs], axis=0)
+    digits = jnp.concatenate([ref[IMAGES:, :IMAGES] for ref in packed_refs], axis=1).astype(F32).astype(jnp.int32)
     row = lax.broadcasted_iota(jnp.int32, (PAD_ROWS, count), 0)
     weight = jnp.where(row == 0, 4096, jnp.where(row == 1, 64, jnp.where(row == 2, 1, 0)))
     pos = jnp.sum(digits * weight, axis=0, keepdims=True) - place_ref[0]
@@ -116,15 +109,15 @@
     unit, _ = normalized(texts_ref[...])
     text_ref[...] = unit.astype(BF16)
     text_unit = text_ref[...]
-    unit, grads, sums_ref[...] = pair_block(packed_ref, text_unit, place_ref, temp_ref, bias_ref)
+    unit, grads, sums_ref[...] = pair_block([packed_ref], text_unit, place_ref, temp_ref, bias_ref)
     dx_ref[...] = image_part(grads, text_unit)
     dy_ref[...] = text_part(grads, unit)
 
 
-def near_kernel(text_ref, packed_ref, place_ref, temp_ref, bias_ref, old_dy_ref, old_sums_ref,
+def near_kernel(text_ref, first_ref, second_ref, place_ref, temp_ref, bias_ref, old_dy_ref, old_sums_ref,
                 dx_ref, dy_ref, sums_ref, staged, sem):
     text_unit = text_ref[...]
-    unit, grads, tile = pair_block(packed_ref, text_unit, place_ref, temp_ref, bias_ref)
+    unit, grads, tile = pair_block([first_ref, second_ref], text_unit, place_ref, temp_ref, bias_ref)
     staged[...] = image_part(grads, text_unit)
     copy = pltpu.make_async_copy(staged, dx_ref, sem)
     copy.start()
@@ -133,10 +126,10 @@
     copy.wait()
 
 
-def far_kernel(text_ref, packed_ref, place_ref, temp_ref, bias_ref, old_dy_ref, old_sums_ref,
+def far_kernel(text_ref, first_ref, second_ref, place_ref, temp_ref, bias_ref, old_dy_ref, old_sums_ref,
                dx_ref, send_ref, keep_ref, row_ref, staged, sem, total):
     text_unit = text_ref[...]
-    unit, grads, tile = pair_block(packed_ref, text_unit, place_ref, temp_ref, bias_ref)
+    unit, grads, tile = pair_block([first_ref, second_ref], text_unit, place_ref, temp_ref, bias_ref)
     staged[...] = image_part(grads, text_unit)
     copy = pltpu.make_async_copy(staged, dx_ref, sem)
     copy.start()
@@ -200,26 +193,26 @@
     block_flops = 6 * TEXTS * IMAGES * WIDTH
     positive = positive.reshape(1, IMAGES)
     (mine,) = call(pack_kernel, [shape(IMAGES + PAD_ROWS, WIDTH, dtype=BF16)], images, positive)
-    (packed,) = call(stack_kernel, [shape(PAIR + PAD_ROWS, WIDTH, dtype=BF16)], mine, swapped(mine, "core"))
-    near = to_side(packed, 1)
+    other = swapped(mine, "core")
+    near = [to_side(mine, 1), to_side(other, 1)]
     text_unit, dx0, dy, sums = call(
         own_kernel,
         [shape(TEXTS, WIDTH, dtype=BF16), shape(IMAGES, WIDTH), shape(TEXTS, WIDTH), shape(8, IMAGES)],
         texts, mine, place, temp_log, bias_arg, flops=block_flops, smem_in=(2, 3, 4),
     )
-    near, text_unit = lax.optimization_barrier((near, text_unit))
-    far = to_side(near, 1)
+    near[0], text_unit = lax.optimization_barrier((near[0], text_unit))
+    far = [to_side(near[0], 1), to_side(near[1], 1)]
     staging = [pltpu.VMEM((PAIR, WIDTH), F32), pltpu.SemaphoreType.DMA(())]
     near_dx, dy, sums = call(
         near_kernel, [shape(PAIR, WIDTH), shape(TEXTS, WIDTH), shape(8, IMAGES)],
-        text_unit, near, place, temp_log, bias_arg, dy, sums,
-        flops=2 * block_flops, smem_in=(2, 3, 4), any_out=(0,), scratch=staging,
+        text_unit, *near, place, temp_log, bias_arg, dy, sums,
+        flops=2 * block_flops, smem_in=(3, 4, 5), any_out=(0,), scratch=staging,
     )
     near_dx = to_side(near_dx, -1)
     far_dx, send, keep, row = call(
         far_kernel, [shape(PAIR, WIDTH)] + [shape(2, IMAGES, WIDTH)] * 2 + [shape(RING, 1, IMAGES)],
-        text_unit, far, place, temp_log, bias_arg, dy, sums,
-        flops=2 * block_flops, smem_in=(2, 3, 4), any_out=(0,),
+        text_unit, *far, place, temp_log, bias_arg, dy, sums,
+        flops=2 * block_flops, smem_in=(3, 4, 5), any_out=(0,),
         scratch=staging + [pltpu.VMEM((TEXTS, WIDTH), F32)],
     )
     far_dx = to_side(far_dx, -2)

time: 115 us -> 111 us (0.965)
  waiting for transfers between devices: 18.9 us -> 13.7 us
    ppermute x4 -> x6, starting transfers between devices: 20.8 us -> 26.5 us  [to_side(): return lax.ppermute(value, BLK + ('core',), pairs)]
    ppermute x4 -> x6, waiting for transfers between devices: 4.27 us -> 0.02 us  [to_side(): return lax.ppermute(value, BLK + ('core',), pairs)]
    all_to_all x1, starting transfers between devices: 13.8 us -> 9.74 us  [per_device(): row = lax.all_to_all(row, 'z', 0, 0, tiled=True)]
    ppermute x4, starting transfers between devices: 27.9 us -> 26.4 us  [swapped(): return lax.ppermute(value, axis, [(0, 1), (1, 0)])]
    ppermute x4, waiting for transfers between devices: 1.9 us -> 0.66 us  [swapped(): return lax.ppermute(value, axis, [(0, 1), (1, 0)])]
    unnamed x20 -> x22, local copies, waits for them, and re-layouts: 3.91 us -> 4.38 us
    pallas_call x12 -> x11, Pallas kernels: 18.3 us -> 17.8 us  [call(): pl.pallas_call(body, out_shape=outs, in_specs=[scalar if k in smem_in els...]
  transfers between devices with their start and end apart: 10 -> 12, of which waited for: 6 -> 3; matrix products, arithmetic and copies ran while one was open for 0% -> 0% of each run, Pallas kernels for 15% -> 15%
where the time goes in v4:
time: 111 us; the launch traced here: 110 us
  starting transfers between devices  71.8 us (65%)
  Pallas kernels  17.8 us (16%)
  waiting for transfers between devices  13.7 us (12%)
  local copies, waits for them, and re-layouts  4.38 us (4%)
  between operations  2.22 us (2%)
    ppermute x6, starting transfers between devices, to_side(): return lax.ppermute(value, BLK + ('core',), pairs)  26.5 us
    ppermute x4, starting transfers between devices, swapped(): return lax.ppermute(value, axis, [(0, 1), (1, 0)])  26.4 us
    pallas_call x11, Pallas kernels, call(): pl.pallas_call(body, out_shape=outs, in_specs=[scalar if k in smem_in els...  17.8 us
    all_to_all x1, waiting for transfers between devices, per_device(): row = lax.all_to_all(row, 'z', 0, 0, tiled=True)  12.6 us
    all_to_all x1, starting transfers between devices, per_device(): row = lax.all_to_all(row, 'z', 0, 0, tiled=True)  9.74 us
    all_to_all x1, starting transfers between devices, per_device(): row = lax.all_to_all(row, PLANE, 0, 0, tiled=True)  9.2 us
    unnamed x22, local copies, waits for them, and re-layouts  4.38 us
  transfers between devices with their start and end apart: 12, of which 3 were waited for; matrix products, arithmetic and copies ran while one was open for 0% of the time, Pallas kernels for 15%

profile of v4, /device:TPU:1, one launch (start us, length us, event | category | flops | bytes accessed | tf_op | source)
XLA Modules:
  0.0 109.9 jit_solution(895555417821393166)
XLA Ops:
  0.6 1.0 copy-done
  1.6 0.7 copy-done.8
  2.3 0.1 shard_map.92.packed_ref
  2.4 16.1 %collective-permute-start.2 = (bf16[144,1152]{1,0:T(8,128)(2,1)S(1)}, bf16[144,1152]{1,0:T(8,128)(2,1)S(1)}, u32[]{:S(2)}, u32[]{:S(2)}) collective-permute-start(bf16[144,1152]{1,0:T(8,128)(2,1)S(1)} %shard_map.92.packed_ref), channel_id=1, source_target_pairs={{0,1},{1,0},{2,3},{3,2},{4,5},{5,4},{6,7},{7,6},{8,9},{9,8},{10,11... | collective-permute-start | bytes 995336 | tf_op jit(solution)/shard_map/ppermute | solution.py:54
  18.5 9.0 %collective-permute-start = (bf16[144,1152]{1,0:T(8,128)(2,1)S(1)}, bf16[144,1152]{1,0:T(8,128)(2,1)S(1)}, u32[]{:S(2)}, u32[]{:S(2)}) collective-permute-start(bf16[144,1152]{1,0:T(8,128)(2,1)S(1)} %shard_map.92.packed_ref), channel_id=1, source_target_pairs={{0,4},{1,1021},{4,8},{5,1},{8,12},{9,5},{12,16},{13,9},{16,20},{17... | collective-permute-start | bytes 995336 | tf_op jit(solution)/shard_map/ppermute | solution.py:50
  27.4 2.5 %collective-permute-start.3 = (bf16[144,1152]{1,0:T(8,128)(2,1)S(1)}, bf16[144,1152]{1,0:T(8,128)(2,1)S(1)}, u32[]{:S(2)}, u32[]{:S(2)}) collective-permute-start(bf16[144,1152]{1,0:T(8,128)(2,1)S(1)} %collective-permute-done.2), channel_id=1, source_target_pairs={{0,4},{1,1021},{4,8},{5,1},{8,12},{9,5},{12,16},{13,9},{16,20},{17... | collective-permute-start | bytes 995336 | tf_op jit(solution)/shard_map/ppermute | solution.py:50
  31.2 0.1 pad_add_fusion.place_ref
  31.3 1.3 %copy-done.2 = bf16[512,1152]{1,0:T(8,128)(2,1)S(1)} copy-done((bf16[512,1152]{1,0:T(8,128)(2,1)S(1)}, bf16[512,1152]{1,0:T(8,128)(2,1)}, u32[]{:S(2)}) %copy-start.2) | copy-done | bytes 1179672
  32.6 2.4 %shard_map.93 = (bf16[512,1152]{1,0:T(8,128)(2,1)S(1)}, f32[128,1152]{1,0:T(8,128)S(1)}, f32[512,1152]{1,0:T(8,128)S(1)}, f32[8,128]{1,0:T(8,128)S(1)}) custom-call(bf16[512,1152]{1,0:T(8,128)(2,1)S(1)} %copy-done.2, bf16[144,1152]{1,0:T(8,128)(2,1)S(1)} %shard_map.92.packed_ref, s32[3]{0:T(128)S(1)} %pad_add_fusion.place_ref, f32[1]{0:T(128)S(6)} %copy.10.temp_ref, ...), custom_call_target="tpu_custom_call" | custom-call | flops 452984832 | bytes 5644308 | tf_op jit(solution)/shard_map/pallas_call | solution.py:33
  35.0 4.5 %collective-permute-start.1 = (bf16[144,1152]{1,0:T(8,128)(2,1)S(1)}, bf16[144,1152]{1,0:T(8,128)(2,1)S(1)}, u32[]{:S(2)}, u32[]{:S(2)}) collective-permute-start(bf16[144,1152]{1,0:T(8,128)(2,1)S(1)} %collective-permute-done.first_ref), channel_id=1, source_target_pairs={{0,4},{1,1021},{4,8},{5,1},{8,12},{9,5},{12,16},{13,9},{16,20},{17... | collective-permute-start | bytes 995336 | tf_op jit(solution)/shard_map/ppermute | solution.py:50
  39.5 3.5 %collective-permute-start.4 = (bf16[144,1152]{1,0:T(8,128)(2,1)S(1)}, bf16[144,1152]{1,0:T(8,128)(2,1)S(1)}, u32[]{:S(2)}, u32[]{:S(2)}) collective-permute-start(bf16[144,1152]{1,0:T(8,128)(2,1)S(1)} %collective-permute-done.3.second_ref), channel_id=1, source_target_pairs={{0,4},{1,1021},{4,8},{5,1},{8,12},{9,5},{12,16},{13,9},{16,20},{17... | collective-permute-start | bytes 995336 | tf_op jit(solution)/shard_map/ppermute | solution.py:50
  43.1 3.6 %shard_map.94 = (f32[256,1152]{1,0:T(8,128)}, f32[512,1152]{1,0:T(8,128)S(1)}, f32[8,128]{1,0:T(8,128)S(1)}) custom-call(bf16[512,1152]{1,0:T(8,128)(2,1)S(1)} %get-tuple-element.37.text_ref, bf16[144,1152]{1,0:T(8,128)(2,1)S(1)} %collective-permute-done.first_ref, bf16[144,1152]{1,0:T(8,128)(2,1)S(1)} %collective-permute-done.3.second_ref, ...), custom_call_target="tpu_custom_call" | custom-call | flops 905969664 | bytes 7749652 | tf_op jit(solution)/shard_map/pallas_call | solution.py:33
  46.7 1.9 %collective-permute-start.5 = (f32[256,1152]{1,0:T(8,128)}, f32[256,1152]{1,0:T(8,128)S(1)}, u32[]{:S(2)}, u32[]{:S(2)}) collective-permute-start(f32[256,1152]{1,0:T(8,128)} %get-tuple-element.47), channel_id=1, source_target_pairs={{0,1020},{1,5},{4,0},{5,9},{8,4},{9,13},{12,8},{13,17},{16,12},{17... | collective-permute-start | bytes 3538952 | tf_op jit(solution)/shard_map/ppermute | solution.py:50
  48.6 4.6 %shard_map.95 = (f32[256,1152]{1,0:T(8,128)}, f32[2,128,1152]{2,1,0:T(8,128)}, f32[2,128,1152]{2,1,0:T(8,128)S(1)}, f32[32,1,128]{2,1,0:T(1,128)}) custom-call(bf16[512,1152]{1,0:T(8,128)(2,1)S(1)} %get-tuple-element.37.text_ref, bf16[144,1152]{1,0:T(8,128)(2,1)S(1)} %collective-permute-done.1.first_ref, ...), custom_call_target="tpu_custom_call" | custom-call | flops 905969664 | bytes 7761940 | tf_op jit(solution)/shard_map/pallas_call | solution.py:33
  53.2 3.3 %collective-permute-start.6 = (f32[2,128,1152]{2,1,0:T(8,128)}, f32[2,128,1152]{2,1,0:T(8,128)S(1)}, u32[]{:S(2)}, u32[]{:S(2)}) collective-permute-start(f32[2,128,1152]{2,1,0:T(8,128)} %get-tuple-element.48), channel_id=1, source_target_pairs={{0,1},{1,0},{2,3},{3,2},{4,5},{5,4},{6,7},{7,6},{8,9},{9,8},{10,11... | collective-permute-start | bytes 3538952 | tf_op jit(solution)/shard_map/ppermute | solution.py:54
  56.6 5.1 %collective-permute-start.7 = (f32[256,1152]{1,0:T(8,128)}, f32[256,1152]{1,0:T(8,128)}, u32[]{:S(2)}, u32[]{:S(2)}) collective-permute-start(f32[256,1152]{1,0:T(8,128)} %get-tuple-element.50), channel_id=1, source_target_pairs={{0,1016},{1,9},{4,1020},{5,13},{8,0},{9,17},{12,4},{13,21},{16,8},... | collective-permute-start | bytes 3538952 | tf_op jit(solution)/shard_map/ppermute | solution.py:50
  61.7 9.7 %all-to-all-start = ((f32[32,1,128]{2,1,0:T(1,128)}), f32[32,1,128]{2,1,0:T(1,128)S(1)}, u32[]{:S(2)}, u32[]{:S(2)}) async-start(f32[32,1,128]{2,1,0:T(1,128)} %get-tuple-element.43), calls=%async_computation | async-start | bytes 32768 | tf_op jit(solution)/shard_map/all_to_all | solution.py:220
  71.5 0.6 copy-done.7
  72.1 1.5 %shard_map.99 = (f32[128,1152]{1,0:T(8,128)}, f32[128,1152]{1,0:T(8,128)S(1)}) custom-call(s32[3]{0:T(128)S(1)} %copy-done.7, f32[2,128,1152]{2,1,0:T(8,128)S(1)} %get-tuple-element.54.keep_ref, f32[2,128,1152]{2,1,0:T(8,128)S(1)} %collective-permute-done.6.got_ref), custom_call_target="tpu_custom_call" | custom-call | bytes 3538956 | tf_op jit(solution)/shard_map/pallas_call | solution.py:33
  73.6 0.8 copy-done.9
  74.4 4.8 %collective-permute-start.8 = (f32[128,1152]{1,0:T(8,128)}, f32[128,1152]{1,0:T(8,128)S(1)}, u32[]{:S(2)}, u32[]{:S(2)}) collective-permute-start(f32[128,1152]{1,0:T(8,128)} %get-tuple-element.57), channel_id=1, source_target_pairs={{0,2},{2,0},{1,3},{3,1},{4,6},{6,4},{5,7},{7,5},{8,10},{10,8},{9,1... | collective-permute-start | bytes 1769480 | tf_op jit(solution)/shard_map/ppermute | solution.py:54
  79.2 0.7 shard_map.96
  79.9 12.6 %all-to-all-done.row_ref = f32[32,1,128]{2,1,0:T(1,128)S(1)} async-done(((f32[32,1,128]{2,1,0:T(1,128)}), f32[32,1,128]{2,1,0:T(1,128)S(1)}, u32[]{:S(2)}, u32[]{:S(2)}) %all-to-all-start) | async-done | bytes 16416 | tf_op jit(solution)/shard_map/all_to_all | solution.py:220
  92.5 0.6 shard_map.97
  93.2 9.2 %all-to-all-start.1 = ((f32[32,1,128]{2,1,0:T(1,128)}), f32[32,1,128]{2,1,0:T(1,128)S(1)}, u32[]{:S(2)}, u32[]{:S(2)}) async-start(f32[32,1,128]{2,1,0:T(1,128)} %shard_map.97), calls=%async_computation.1 | async-start | bytes 32768 | tf_op jit(solution)/shard_map/all_to_all | solution.py:229
  102.4 1.5 %shard_map.98 = (f32[128,1152]{1,0:T(8,128)S(1)}, f32[128,1152]{1,0:T(8,128)S(1)}) custom-call(f32[128,1152]{1,0:T(8,128)S(1)} %copy-done.5, f32[256,1152]{1,0:T(8,128)S(1)} %collective-permute-done.5.near_ref, f32[256,1152]{1,0:T(8,128)} %collective-permute-done.7.far_ref), custom_call_target="tpu_custom_call" | custom-call | bytes 4128768 | tf_op jit(solution)/shard_map/pallas_call | solution.py:33
  103.9 2.1 %collective-permute-start.9 = (f32[128,1152]{1,0:T(8,128)S(1)}, f32[128,1152]{1,0:T(8,128)S(1)}, u32[]{:S(2)}, u32[]{:S(2)}) collective-permute-start(f32[128,1152]{1,0:T(8,128)S(1)} %get-tuple-element.59), channel_id=1, source_target_pairs={{0,1},{1,0},{2,3},{3,2},{4,5},{5,4},{6,7},{7,6},{8,9},{9,8},{10,11... | collective-permute-start | bytes 1769480 | tf_op jit(solution)/shard_map/ppermute | solution.py:54
  106.1 1.1 shard_map.100
  107.1 0.7 collective-permute-done.9.got_ref
  107.8 1.1 shard_map.101
  108.8 0.4 all-to-all-done.1.row_ref
  109.3 0.7 shard_map.102
  (26 shorter events, 0.1 us)
Async XLA Ops:
  0.6 1.0 copy-start
  1.6 0.7 copy-start.8
  2.4 25.0 %collective-permute-start.2 = (bf16[144,1152]{1,0:T(8,128)(2,1)S(1)}, bf16[144,1152]{1,0:T(8,128)(2,1)S(1)}, u32[]{:S(2)}, u32[]{:S(2)}) collective-permute-start(bf16[144,1152]{1,0:T(8,128)(2,1)S(1)} %shard_map.92.packed_ref), channel_id=1, source_target_pairs={{0,1},{1,0},{2,3},{3,2},{4,5},{5,4},{6,7},{7,6},{8,9},{9,8},{10,11... | collective-permute-start | bytes 995336 | tf_op jit(solution)/shard_map/ppermute | solution.py:54
  18.5 16.5 %collective-permute-start = (bf16[144,1152]{1,0:T(8,128)(2,1)S(1)}, bf16[144,1152]{1,0:T(8,128)(2,1)S(1)}, u32[]{:S(2)}, u32[]{:S(2)}) collective-permute-start(bf16[144,1152]{1,0:T(8,128)(2,1)S(1)} %shard_map.92.packed_ref), channel_id=1, source_target_pairs={{0,4},{1,1021},{4,8},{5,1},{8,12},{9,5},{12,16},{13,9},{16,20},{17... | collective-permute-start | bytes 995336 | tf_op jit(solution)/shard_map/ppermute | solution.py:50
  27.4 12.1 %collective-permute-start.3 = (bf16[144,1152]{1,0:T(8,128)(2,1)S(1)}, bf16[144,1152]{1,0:T(8,128)(2,1)S(1)}, u32[]{:S(2)}, u32[]{:S(2)}) collective-permute-start(bf16[144,1152]{1,0:T(8,128)(2,1)S(1)} %collective-permute-done.2), channel_id=1, source_target_pairs={{0,4},{1,1021},{4,8},{5,1},{8,12},{9,5},{12,16},{13,9},{16,20},{17... | collective-permute-start | bytes 995336 | tf_op jit(solution)/shard_map/ppermute | solution.py:50
  31.3 1.3 %copy-start.2 = (bf16[512,1152]{1,0:T(8,128)(2,1)S(1)}, bf16[512,1152]{1,0:T(8,128)(2,1)}, u32[]{:S(2)}) copy-start(bf16[512,1152]{1,0:T(8,128)(2,1)} %texts_ref.3) | copy-start | bytes 3538948
  32.6 16.0 %copy-start.6 = (s32[3]{0:T(128)}, s32[3]{0:T(128)S(1)}, u32[]{:S(2)}) copy-start(s32[3]{0:T(128)S(1)} %pad_add_fusion.place_ref) | copy-start | bytes 40
  35.0 11.7 %copy-start.4 = (f32[128,1152]{1,0:T(8,128)}, f32[128,1152]{1,0:T(8,128)S(1)}, u32[]{:S(2)}) copy-start(f32[128,1152]{1,0:T(8,128)S(1)} %get-tuple-element.46.own_ref) | copy-start | bytes 1769476
  35.0 13.6 %collective-permute-start.1 = (bf16[144,1152]{1,0:T(8,128)(2,1)S(1)}, bf16[144,1152]{1,0:T(8,128)(2,1)S(1)}, u32[]{:S(2)}, u32[]{:S(2)}) collective-permute-start(bf16[144,1152]{1,0:T(8,128)(2,1)S(1)} %collective-permute-done.first_ref), channel_id=1, source_target_pairs={{0,4},{1,1021},{4,8},{5,1},{8,12},{9,5},{12,16},{13,9},{16,20},{17... | collective-permute-start | bytes 995336 | tf_op jit(solution)/shard_map/ppermute | solution.py:50
  39.5 9.1 %collective-permute-start.4 = (bf16[144,1152]{1,0:T(8,128)(2,1)S(1)}, bf16[144,1152]{1,0:T(8,128)(2,1)S(1)}, u32[]{:S(2)}, u32[]{:S(2)}) collective-permute-start(bf16[144,1152]{1,0:T(8,128)(2,1)S(1)} %collective-permute-done.3.second_ref), channel_id=1, source_target_pairs={{0,4},{1,1021},{4,8},{5,1},{8,12},{9,5},{12,16},{13,9},{16,20},{17... | collective-permute-start | bytes 995336 | tf_op jit(solution)/shard_map/ppermute | solution.py:50
  46.7 24.8 %collective-permute-start.5 = (f32[256,1152]{1,0:T(8,128)}, f32[256,1152]{1,0:T(8,128)S(1)}, u32[]{:S(2)}, u32[]{:S(2)}) collective-permute-start(f32[256,1152]{1,0:T(8,128)} %get-tuple-element.47), channel_id=1, source_target_pairs={{0,1020},{1,5},{4,0},{5,9},{8,4},{9,13},{12,8},{13,17},{16,12},{17... | collective-permute-start | bytes 3538952 | tf_op jit(solution)/shard_map/ppermute | solution.py:50
  53.2 18.2 %collective-permute-start.6 = (f32[2,128,1152]{2,1,0:T(8,128)}, f32[2,128,1152]{2,1,0:T(8,128)S(1)}, u32[]{:S(2)}, u32[]{:S(2)}) collective-permute-start(f32[2,128,1152]{2,1,0:T(8,128)} %get-tuple-element.48), channel_id=1, source_target_pairs={{0,1},{1,0},{2,3},{3,2},{4,5},{5,4},{6,7},{7,6},{8,9},{9,8},{10,11... | collective-permute-start | bytes 3538952 | tf_op jit(solution)/shard_map/ppermute | solution.py:54
  56.6 45.8 %collective-permute-start.7 = (f32[256,1152]{1,0:T(8,128)}, f32[256,1152]{1,0:T(8,128)}, u32[]{:S(2)}, u32[]{:S(2)}) collective-permute-start(f32[256,1152]{1,0:T(8,128)} %get-tuple-element.50), channel_id=1, source_target_pairs={{0,1016},{1,9},{4,1020},{5,13},{8,0},{9,17},{12,4},{13,21},{16,8},... | collective-permute-start | bytes 3538952 | tf_op jit(solution)/shard_map/ppermute | solution.py:50
  61.7 30.8 %all-to-all-start = ((f32[32,1,128]{2,1,0:T(1,128)}), f32[32,1,128]{2,1,0:T(1,128)S(1)}, u32[]{:S(2)}, u32[]{:S(2)}) async-start(f32[32,1,128]{2,1,0:T(1,128)} %get-tuple-element.43), calls=%async_computation | async-start | bytes 32768 | tf_op jit(solution)/shard_map/all_to_all | solution.py:220
  71.5 0.7 copy-start.7
  72.1 7.1 %copy-start.3 = (bf16[512,1152]{1,0:T(8,128)(2,1)S(1)}, bf16[512,1152]{1,0:T(8,128)(2,1)}, u32[]{:S(2)}) copy-start(bf16[512,1152]{1,0:T(8,128)(2,1)} %texts_ref.3) | copy-start | bytes 3538948
  73.6 0.8 copy-start.9
  74.4 31.6 %collective-permute-start.8 = (f32[128,1152]{1,0:T(8,128)}, f32[128,1152]{1,0:T(8,128)S(1)}, u32[]{:S(2)}, u32[]{:S(2)}) collective-permute-start(f32[128,1152]{1,0:T(8,128)} %get-tuple-element.57), channel_id=1, source_target_pairs={{0,2},{2,0},{1,3},{3,1},{4,6},{6,4},{5,7},{7,5},{8,10},{10,8},{9,1... | collective-permute-start | bytes 1769480 | tf_op jit(solution)/shard_map/ppermute | solution.py:54
  92.5 9.9 %copy-start.5 = (f32[128,1152]{1,0:T(8,128)S(1)}, f32[128,1152]{1,0:T(8,128)}, u32[]{:S(2)}) copy-start(f32[128,1152]{1,0:T(8,128)} %copy-done.4) | copy-start | bytes 1769476
  93.2 16.1 %all-to-all-start.1 = ((f32[32,1,128]{2,1,0:T(1,128)}), f32[32,1,128]{2,1,0:T(1,128)S(1)}, u32[]{:S(2)}, u32[]{:S(2)}) async-start(f32[32,1,128]{2,1,0:T(1,128)} %shard_map.97), calls=%async_computation.1 | async-start | bytes 32768 | tf_op jit(solution)/shard_map/all_to_all | solution.py:229
  102.4 3.7 %copy-start.10 = (f32[128,1152]{1,0:T(8,128)S(1)}, f32[128,1152]{1,0:T(8,128)}, u32[]{:S(2)}) copy-start(f32[128,1152]{1,0:T(8,128)} %copy-done.9) | copy-start | bytes 1769476
  103.9 3.9 %collective-permute-start.9 = (f32[128,1152]{1,0:T(8,128)S(1)}, f32[128,1152]{1,0:T(8,128)S(1)}, u32[]{:S(2)}, u32[]{:S(2)}) collective-permute-start(f32[128,1152]{1,0:T(8,128)S(1)} %get-tuple-element.59), channel_id=1, source_target_pairs={{0,1},{1,0},{2,3},{3,2},{4,5},{5,4},{6,7},{7,6},{8,9},{9,8},{10,11... | collective-permute-start | bytes 1769480 | tf_op jit(solution)/shard_map/ppermute | solution.py:54
  106.0 1.7 %copy-start.1 = (bf16[128,1152]{1,0:T(8,128)(2,1)S(1)}, bf16[128,1152]{1,0:T(8,128)(2,1)}, u32[]{:S(2)}) copy-start(bf16[128,1152]{1,0:T(8,128)(2,1)} %images_ref.3) | copy-start | bytes 884740

commit v5 on v4

--- a/solution.py
+++ b/solution.py
@@ -105,23 +105,22 @@
     return jnp.dot(grads, unit, preferred_element_type=F32)
 
 
-def own_kernel(texts_ref, packed_ref, place_ref, temp_ref, bias_ref, text_ref, dx_ref, dy_ref, sums_ref):
+def own_kernel(texts_ref, packed_ref, place_ref, temp_ref, bias_ref, text_ref, dx_ref, grads_ref, sums_ref):
     unit, _ = normalized(texts_ref[...])
     text_ref[...] = unit.astype(BF16)
     text_unit = text_ref[...]
-    unit, grads, sums_ref[...] = pair_block([packed_ref], text_unit, place_ref, temp_ref, bias_ref)
-    dx_ref[...] = image_part(grads, text_unit)
-    dy_ref[...] = text_part(grads, unit)
-
-
-def near_kernel(text_ref, first_ref, second_ref, place_ref, temp_ref, bias_ref, old_dy_ref, old_sums_ref,
+    _, grads_ref[...], sums_ref[...] = pair_block([packed_ref], text_unit, place_ref, temp_ref, bias_ref)
+    dx_ref[...] = image_part(grads_ref[...], text_unit)
+
+
+def near_kernel(text_ref, first_ref, second_ref, place_ref, temp_ref, bias_ref, own_ref, own_grads_ref, old_sums_ref,
                 dx_ref, dy_ref, sums_ref, staged, sem):
     text_unit = text_ref[...]
     unit, grads, tile = pair_block([first_ref, second_ref], text_unit, place_ref, temp_ref, bias_ref)
     staged[...] = image_part(grads, text_unit)
     copy = pltpu.make_async_copy(staged, dx_ref, sem)
     copy.start()
-    dy_ref[...] = old_dy_ref[...] + text_part(grads, unit)
+    dy_ref[...] = text_part(own_grads_ref[...], own_ref[:IMAGES, :]) + text_part(grads, unit)
     sums_ref[...] = old_sums_ref[...] + tile
     copy.wait()
 
@@ -195,9 +194,9 @@
     (mine,) = call(pack_kernel, [shape(IMAGES + PAD_ROWS, WIDTH, dtype=BF16)], images, positive)
     other = swapped(mine, "core")
     near = [to_side(mine, 1), to_side(other, 1)]
-    text_unit, dx0, dy, sums = call(
+    text_unit, dx0, own_grads, sums = call(
         own_kernel,
-        [shape(TEXTS, WIDTH, dtype=BF16), shape(IMAGES, WIDTH), shape(TEXTS, WIDTH), shape(8, IMAGES)],
+        [shape(TEXTS, WIDTH, dtype=BF16), shape(IMAGES, WIDTH), shape(TEXTS, IMAGES, dtype=BF16), shape(8, IMAGES)],
         texts, mine, place, temp_log, bias_arg, flops=block_flops, smem_in=(2, 3, 4),
     )
     near[0], text_unit = lax.optimization_barrier((near[0], text_unit))
@@ -205,7 +204,7 @@
     staging = [pltpu.VMEM((PAIR, WIDTH), F32), pltpu.SemaphoreType.DMA(())]
     near_dx, dy, sums = call(
         near_kernel, [shape(PAIR, WIDTH), shape(TEXTS, WIDTH), shape(8, IMAGES)],
-        text_unit, *near, place, temp_log, bias_arg, dy, sums,
+        text_unit, *near, place, temp_log, bias_arg, mine, own_grads, sums,
         flops=2 * block_flops, smem_in=(3, 4, 5), any_out=(0,), scratch=staging,
     )
     near_dx = to_side(near_dx, -1)

time: 111 us -> 111 us (level)
  no operation moved by 1% of the time
where the time goes in v5:
time: 111 us; the launch traced here: 110 us
  starting transfers between devices  71.3 us (64%)
  Pallas kernels  17.5 us (16%)
  waiting for transfers between devices  13.7 us (12%)
  local copies, waits for them, and re-layouts  5.18 us (5%)
  between operations  2.21 us (2%)
    ppermute x6, starting transfers between devices, to_side(): return lax.ppermute(value, BLK + ('core',), pairs)  26.9 us
    ppermute x4, starting transfers between devices, swapped(): return lax.ppermute(value, axis, [(0, 1), (1, 0)])  26.4 us
    pallas_call x11, Pallas kernels, call(): pl.pallas_call(body, out_shape=outs, in_specs=[scalar if k in smem_in els...  17.5 us
    all_to_all x1, waiting for transfers between devices, per_device(): row = lax.all_to_all(row, 'z', 0, 0, tiled=True)  12.6 us
    all_to_all x1, starting transfers between devices, per_device(): row = lax.all_to_all(row, PLANE, 0, 0, tiled=True)  9.2 us
    all_to_all x1, starting transfers between devices, per_device(): row = lax.all_to_all(row, 'z', 0, 0, tiled=True)  8.81 us
    unnamed x22, local copies, waits for them, and re-layouts  5.18 us
  transfers between devices with their start and end apart: 12, of which 3 were waited for; matrix products, arithmetic and copies ran while one was open for 0% of the time, Pallas kernels for 15%

profile of v5, /device:TPU:1, one launch (start us, length us, event | category | flops | bytes accessed | tf_op | source)
XLA Modules:
  0.0 110.0 jit_solution(16731993663665254888)
XLA Ops:
  0.6 1.0 copy-done
  1.6 0.7 copy-done.8
  2.3 0.1 shard_map.92.packed_ref.own_ref
  2.4 16.1 %collective-permute-start.2 = (bf16[144,1152]{1,0:T(8,128)(2,1)S(1)}, bf16[144,1152]{1,0:T(8,128)(2,1)S(1)}, u32[]{:S(2)}, u32[]{:S(2)}) collective-permute-start(bf16[144,1152]{1,0:T(8,128)(2,1)S(1)} %shard_map.92.packed_ref.own_ref), channel_id=1, source_target_pairs={{0,1},{1,0},{2,3},{3,2},{4,5},{5,4},{6,7},{7,6},{8,9},{9,8},{10,11... | collective-permute-start | bytes 995336 | tf_op jit(solution)/shard_map/ppermute | solution.py:54
  18.5 9.0 %collective-permute-start = (bf16[144,1152]{1,0:T(8,128)(2,1)S(1)}, bf16[144,1152]{1,0:T(8,128)(2,1)S(1)}, u32[]{:S(2)}, u32[]{:S(2)}) collective-permute-start(bf16[144,1152]{1,0:T(8,128)(2,1)S(1)} %shard_map.92.packed_ref.own_ref), channel_id=1, source_target_pairs={{0,4},{1,1021},{4,8},{5,1},{8,12},{9,5},{12,16},{13,9},{16,20},{17... | collective-permute-start | bytes 995336 | tf_op jit(solution)/shard_map/ppermute | solution.py:50
  27.4 2.5 %collective-permute-start.3 = (bf16[144,1152]{1,0:T(8,128)(2,1)S(1)}, bf16[144,1152]{1,0:T(8,128)(2,1)S(1)}, u32[]{:S(2)}, u32[]{:S(2)}) collective-permute-start(bf16[144,1152]{1,0:T(8,128)(2,1)S(1)} %collective-permute-done.2), channel_id=1, source_target_pairs={{0,4},{1,1021},{4,8},{5,1},{8,12},{9,5},{12,16},{13,9},{16,20},{17... | collective-permute-start | bytes 995336 | tf_op jit(solution)/shard_map/ppermute | solution.py:50
  31.3 1.3 %copy-done.2 = bf16[512,1152]{1,0:T(8,128)(2,1)S(1)} copy-done((bf16[512,1152]{1,0:T(8,128)(2,1)S(1)}, bf16[512,1152]{1,0:T(8,128)(2,1)}, u32[]{:S(2)}) %copy-start.2) | copy-done | bytes 1179672
  32.6 2.0 %shard_map.93 = (bf16[512,1152]{1,0:T(8,128)(2,1)S(1)}, f32[128,1152]{1,0:T(8,128)S(1)}, bf16[512,128]{1,0:T(8,128)(2,1)S(1)}, f32[8,128]{1,0:T(8,128)S(1)}) custom-call(bf16[512,1152]{1,0:T(8,128)(2,1)S(1)} %copy-done.2, bf16[144,1152]{1,0:T(8,128)(2,1)S(1)} %shard_map.92.packed_ref.own_ref, s32[3]{0:T(128)S(1)} %pad_add_fusion.place_ref, ...), custom_call_target="tpu_custom_call" | custom-call | flops 452984832 | bytes 3416084 | tf_op jit(solution)/shard_map/pallas_call | solution.py:33
  34.6 0.8 copy-done.4
  35.4 4.1 %collective-permute-start.1 = (bf16[144,1152]{1,0:T(8,128)(2,1)S(1)}, bf16[144,1152]{1,0:T(8,128)(2,1)S(1)}, u32[]{:S(2)}, u32[]{:S(2)}) collective-permute-start(bf16[144,1152]{1,0:T(8,128)(2,1)S(1)} %collective-permute-done.first_ref), channel_id=1, source_target_pairs={{0,4},{1,1021},{4,8},{5,1},{8,12},{9,5},{12,16},{13,9},{16,20},{17... | collective-permute-start | bytes 995336 | tf_op jit(solution)/shard_map/ppermute | solution.py:50
  39.5 3.5 %collective-permute-start.4 = (bf16[144,1152]{1,0:T(8,128)(2,1)S(1)}, bf16[144,1152]{1,0:T(8,128)(2,1)S(1)}, u32[]{:S(2)}, u32[]{:S(2)}) collective-permute-start(bf16[144,1152]{1,0:T(8,128)(2,1)S(1)} %collective-permute-done.3.second_ref), channel_id=1, source_target_pairs={{0,4},{1,1021},{4,8},{5,1},{8,12},{9,5},{12,16},{13,9},{16,20},{17... | collective-permute-start | bytes 995336 | tf_op jit(solution)/shard_map/ppermute | solution.py:50
  43.1 3.6 %shard_map.94 = (f32[256,1152]{1,0:T(8,128)}, f32[512,1152]{1,0:T(8,128)S(1)}, f32[8,128]{1,0:T(8,128)S(1)}) custom-call(bf16[512,1152]{1,0:T(8,128)(2,1)S(1)} %get-tuple-element.37.text_ref, bf16[144,1152]{1,0:T(8,128)(2,1)S(1)} %collective-permute-done.first_ref, bf16[144,1152]{1,0:T(8,128)(2,1)S(1)} %collective-permute-done.3.second_ref, ...), custom_call_target="tpu_custom_call" | custom-call | flops 905969664 | bytes 5853204 | tf_op jit(solution)/shard_map/pallas_call | solution.py:33
  46.7 1.9 %collective-permute-start.5 = (f32[256,1152]{1,0:T(8,128)}, f32[256,1152]{1,0:T(8,128)S(1)}, u32[]{:S(2)}, u32[]{:S(2)}) collective-permute-start(f32[256,1152]{1,0:T(8,128)} %get-tuple-element.47), channel_id=1, source_target_pairs={{0,1020},{1,5},{4,0},{5,9},{8,4},{9,13},{12,8},{13,17},{16,12},{17... | collective-permute-start | bytes 3538952 | tf_op jit(solution)/shard_map/ppermute | solution.py:50
  48.6 4.6 %shard_map.95 = (f32[256,1152]{1,0:T(8,128)}, f32[2,128,1152]{2,1,0:T(8,128)}, f32[2,128,1152]{2,1,0:T(8,128)S(1)}, f32[32,1,128]{2,1,0:T(1,128)}) custom-call(bf16[512,1152]{1,0:T(8,128)(2,1)S(1)} %get-tuple-element.37.text_ref, bf16[144,1152]{1,0:T(8,128)(2,1)S(1)} %collective-permute-done.1.first_ref, ...), custom_call_target="tpu_custom_call" | custom-call | flops 905969664 | bytes 7761940 | tf_op jit(solution)/shard_map/pallas_call | solution.py:33
  53.2 3.3 %collective-permute-start.6 = (f32[2,128,1152]{2,1,0:T(8,128)}, f32[2,128,1152]{2,1,0:T(8,128)S(1)}, u32[]{:S(2)}, u32[]{:S(2)}) collective-permute-start(f32[2,128,1152]{2,1,0:T(8,128)} %get-tuple-element.48), channel_id=1, source_target_pairs={{0,1},{1,0},{2,3},{3,2},{4,5},{5,4},{6,7},{7,6},{8,9},{9,8},{10,11... | collective-permute-start | bytes 3538952 | tf_op jit(solution)/shard_map/ppermute | solution.py:54
  56.6 6.0 %collective-permute-start.7 = (f32[256,1152]{1,0:T(8,128)}, f32[256,1152]{1,0:T(8,128)}, u32[]{:S(2)}, u32[]{:S(2)}) collective-permute-start(f32[256,1152]{1,0:T(8,128)} %get-tuple-element.50), channel_id=1, source_target_pairs={{0,1016},{1,9},{4,1020},{5,13},{8,0},{9,17},{12,4},{13,21},{16,8},... | collective-permute-start | bytes 3538952 | tf_op jit(solution)/shard_map/ppermute | solution.py:50
  62.6 8.8 %all-to-all-start = ((f32[32,1,128]{2,1,0:T(1,128)}), f32[32,1,128]{2,1,0:T(1,128)S(1)}, u32[]{:S(2)}, u32[]{:S(2)}) async-start(f32[32,1,128]{2,1,0:T(1,128)} %get-tuple-element.43), calls=%async_computation | async-start | bytes 32768 | tf_op jit(solution)/shard_map/all_to_all | solution.py:219
  71.5 0.6 copy-done.7
  72.1 1.5 %shard_map.99 = (f32[128,1152]{1,0:T(8,128)}, f32[128,1152]{1,0:T(8,128)S(1)}) custom-call(s32[3]{0:T(128)S(1)} %copy-done.7, f32[2,128,1152]{2,1,0:T(8,128)S(1)} %get-tuple-element.54.keep_ref, f32[2,128,1152]{2,1,0:T(8,128)S(1)} %collective-permute-done.6.got_ref), custom_call_target="tpu_custom_call" | custom-call | bytes 3538956 | tf_op jit(solution)/shard_map/pallas_call | solution.py:33
  73.6 0.8 copy-done.9
  74.4 4.8 %collective-permute-start.8 = (f32[128,1152]{1,0:T(8,128)}, f32[128,1152]{1,0:T(8,128)S(1)}, u32[]{:S(2)}, u32[]{:S(2)}) collective-permute-start(f32[128,1152]{1,0:T(8,128)} %get-tuple-element.57), channel_id=1, source_target_pairs={{0,2},{2,0},{1,3},{3,1},{4,6},{6,4},{5,7},{7,5},{8,10},{10,8},{9,1... | collective-permute-start | bytes 1769480 | tf_op jit(solution)/shard_map/ppermute | solution.py:54
  79.3 0.7 shard_map.96
  80.0 12.6 %all-to-all-done.row_ref = f32[32,1,128]{2,1,0:T(1,128)S(1)} async-done(((f32[32,1,128]{2,1,0:T(1,128)}), f32[32,1,128]{2,1,0:T(1,128)S(1)}, u32[]{:S(2)}, u32[]{:S(2)}) %all-to-all-start) | async-done | bytes 16416 | tf_op jit(solution)/shard_map/all_to_all | solution.py:219
  92.5 0.6 shard_map.97
  93.2 9.2 %all-to-all-start.1 = ((f32[32,1,128]{2,1,0:T(1,128)}), f32[32,1,128]{2,1,0:T(1,128)S(1)}, u32[]{:S(2)}, u32[]{:S(2)}) async-start(f32[32,1,128]{2,1,0:T(1,128)} %shard_map.97), calls=%async_computation.1 | async-start | bytes 32768 | tf_op jit(solution)/shard_map/all_to_all | solution.py:228
  102.4 1.5 %shard_map.98 = (f32[128,1152]{1,0:T(8,128)S(1)}, f32[128,1152]{1,0:T(8,128)S(1)}) custom-call(f32[128,1152]{1,0:T(8,128)S(1)} %copy-done.5, f32[256,1152]{1,0:T(8,128)S(1)} %collective-permute-done.5.near_ref, f32[256,1152]{1,0:T(8,128)} %collective-permute-done.7.far_ref), custom_call_target="tpu_custom_call" | custom-call | bytes 4128768 | tf_op jit(solution)/shard_map/pallas_call | solution.py:33
  103.9 2.1 %collective-permute-start.9 = (f32[128,1152]{1,0:T(8,128)S(1)}, f32[128,1152]{1,0:T(8,128)S(1)}, u32[]{:S(2)}, u32[]{:S(2)}) collective-permute-start(f32[128,1152]{1,0:T(8,128)S(1)} %get-tuple-element.59), channel_id=1, source_target_pairs={{0,1},{1,0},{2,3},{3,2},{4,5},{5,4},{6,7},{7,6},{8,9},{9,8},{10,11... | collective-permute-start | bytes 1769480 | tf_op jit(solution)/shard_map/ppermute | solution.py:54
  106.1 1.1 shard_map.100
  107.1 0.7 collective-permute-done.9.got_ref
  107.8 1.1 shard_map.101
  108.9 0.4 all-to-all-done.1.row_ref
  109.3 0.7 shard_map.102
  (26 shorter events, 0.1 us)
Async XLA Ops:
  0.6 1.0 copy-start
  1.6 0.7 copy-start.8
  2.4 25.0 %collective-permute-start.2 = (bf16[144,1152]{1,0:T(8,128)(2,1)S(1)}, bf16[144,1152]{1,0:T(8,128)(2,1)S(1)}, u32[]{:S(2)}, u32[]{:S(2)}) collective-permute-start(bf16[144,1152]{1,0:T(8,128)(2,1)S(1)} %shard_map.92.packed_ref.own_ref), channel_id=1, source_target_pairs={{0,1},{1,0},{2,3},{3,2},{4,5},{5,4},{6,7},{7,6},{8,9},{9,8},{10,11... | collective-permute-start | bytes 995336 | tf_op jit(solution)/shard_map/ppermute | solution.py:54
  18.5 17.0 %collective-permute-start = (bf16[144,1152]{1,0:T(8,128)(2,1)S(1)}, bf16[144,1152]{1,0:T(8,128)(2,1)S(1)}, u32[]{:S(2)}, u32[]{:S(2)}) collective-permute-start(bf16[144,1152]{1,0:T(8,128)(2,1)S(1)} %shard_map.92.packed_ref.own_ref), channel_id=1, source_target_pairs={{0,4},{1,1021},{4,8},{5,1},{8,12},{9,5},{12,16},{13,9},{16,20},{17... | collective-permute-start | bytes 995336 | tf_op jit(solution)/shard_map/ppermute | solution.py:50
  27.4 12.1 %collective-permute-start.3 = (bf16[144,1152]{1,0:T(8,128)(2,1)S(1)}, bf16[144,1152]{1,0:T(8,128)(2,1)S(1)}, u32[]{:S(2)}, u32[]{:S(2)}) collective-permute-start(bf16[144,1152]{1,0:T(8,128)(2,1)S(1)} %collective-permute-done.2), channel_id=1, source_target_pairs={{0,4},{1,1021},{4,8},{5,1},{8,12},{9,5},{12,16},{13,9},{16,20},{17... | collective-permute-start | bytes 995336 | tf_op jit(solution)/shard_map/ppermute | solution.py:50
  31.3 1.3 %copy-start.2 = (bf16[512,1152]{1,0:T(8,128)(2,1)S(1)}, bf16[512,1152]{1,0:T(8,128)(2,1)}, u32[]{:S(2)}) copy-start(bf16[512,1152]{1,0:T(8,128)(2,1)} %texts_ref.3) | copy-start | bytes 3538948
  32.6 16.1 %copy-start.6 = (s32[3]{0:T(128)}, s32[3]{0:T(128)S(1)}, u32[]{:S(2)}) copy-start(s32[3]{0:T(128)S(1)} %pad_add_fusion.place_ref) | copy-start | bytes 40
  34.6 0.8 copy-start.4
  35.4 13.2 %collective-permute-start.1 = (bf16[144,1152]{1,0:T(8,128)(2,1)S(1)}, bf16[144,1152]{1,0:T(8,128)(2,1)S(1)}, u32[]{:S(2)}, u32[]{:S(2)}) collective-permute-start(bf16[144,1152]{1,0:T(8,128)(2,1)S(1)} %collective-permute-done.first_ref), channel_id=1, source_target_pairs={{0,4},{1,1021},{4,8},{5,1},{8,12},{9,5},{12,16},{13,9},{16,20},{17... | collective-permute-start | bytes 995336 | tf_op jit(solution)/shard_map/ppermute | solution.py:50
  39.5 9.1 %collective-permute-start.4 = (bf16[144,1152]{1,0:T(8,128)(2,1)S(1)}, bf16[144,1152]{1,0:T(8,128)(2,1)S(1)}, u32[]{:S(2)}, u32[]{:S(2)}) collective-permute-start(bf16[144,1152]{1,0:T(8,128)(2,1)S(1)} %collective-permute-done.3.second_ref), channel_id=1, source_target_pairs={{0,4},{1,1021},{4,8},{5,1},{8,12},{9,5},{12,16},{13,9},{16,20},{17... | collective-permute-start | bytes 995336 | tf_op jit(solution)/shard_map/ppermute | solution.py:50
  46.7 24.8 %collective-permute-start.5 = (f32[256,1152]{1,0:T(8,128)}, f32[256,1152]{1,0:T(8,128)S(1)}, u32[]{:S(2)}, u32[]{:S(2)}) collective-permute-start(f32[256,1152]{1,0:T(8,128)} %get-tuple-element.47), channel_id=1, source_target_pairs={{0,1020},{1,5},{4,0},{5,9},{8,4},{9,13},{12,8},{13,17},{16,12},{17... | collective-permute-start | bytes 3538952 | tf_op jit(solution)/shard_map/ppermute | solution.py:50
  53.2 18.2 %collective-permute-start.6 = (f32[2,128,1152]{2,1,0:T(8,128)}, f32[2,128,1152]{2,1,0:T(8,128)S(1)}, u32[]{:S(2)}, u32[]{:S(2)}) collective-permute-start(f32[2,128,1152]{2,1,0:T(8,128)} %get-tuple-element.48), channel_id=1, source_target_pairs={{0,1},{1,0},{2,3},{3,2},{4,5},{5,4},{6,7},{7,6},{8,9},{9,8},{10,11... | collective-permute-start | bytes 3538952 | tf_op jit(solution)/shard_map/ppermute | solution.py:54
  56.6 45.8 %collective-permute-start.7 = (f32[256,1152]{1,0:T(8,128)}, f32[256,1152]{1,0:T(8,128)}, u32[]{:S(2)}, u32[]{:S(2)}) collective-permute-start(f32[256,1152]{1,0:T(8,128)} %get-tuple-element.50), channel_id=1, source_target_pairs={{0,1016},{1,9},{4,1020},{5,13},{8,0},{9,17},{12,4},{13,21},{16,8},... | collective-permute-start | bytes 3538952 | tf_op jit(solution)/shard_map/ppermute | solution.py:50
  62.6 29.9 %all-to-all-start = ((f32[32,1,128]{2,1,0:T(1,128)}), f32[32,1,128]{2,1,0:T(1,128)S(1)}, u32[]{:S(2)}, u32[]{:S(2)}) async-start(f32[32,1,128]{2,1,0:T(1,128)} %get-tuple-element.43), calls=%async_computation | async-start | bytes 32768 | tf_op jit(solution)/shard_map/all_to_all | solution.py:219
  71.5 0.7 copy-start.7
  72.1 7.1 %copy-start.3 = (bf16[512,1152]{1,0:T(8,128)(2,1)S(1)}, bf16[512,1152]{1,0:T(8,128)(2,1)}, u32[]{:S(2)}) copy-start(bf16[512,1152]{1,0:T(8,128)(2,1)} %texts_ref.3) | copy-start | bytes 3538948
  73.6 0.8 copy-start.9
  74.4 31.6 %collective-permute-start.8 = (f32[128,1152]{1,0:T(8,128)}, f32[128,1152]{1,0:T(8,128)S(1)}, u32[]{:S(2)}, u32[]{:S(2)}) collective-permute-start(f32[128,1152]{1,0:T(8,128)} %get-tuple-element.57), channel_id=1, source_target_pairs={{0,2},{2,0},{1,3},{3,1},{4,6},{6,4},{5,7},{7,5},{8,10},{10,8},{9,1... | collective-permute-start | bytes 1769480 | tf_op jit(solution)/shard_map/ppermute | solution.py:54
  92.5 9.9 %copy-start.5 = (f32[128,1152]{1,0:T(8,128)S(1)}, f32[128,1152]{1,0:T(8,128)}, u32[]{:S(2)}) copy-start(f32[128,1152]{1,0:T(8,128)} %copy-done.4) | copy-start | bytes 1769476
  93.2 16.1 %all-to-all-start.1 = ((f32[32,1,128]{2,1,0:T(1,128)}), f32[32,1,128]{2,1,0:T(1,128)S(1)}, u32[]{:S(2)}, u32[]{:S(2)}) async-start(f32[32,1,128]{2,1,0:T(1,128)} %shard_map.97), calls=%async_computation.1 | async-start | bytes 32768 | tf_op jit(solution)/shard_map/all_to_all | solution.py:228
  102.4 3.7 %copy-start.10 = (f32[128,1152]{1,0:T(8,128)S(1)}, f32[128,1152]{1,0:T(8,128)}, u32[]{:S(2)}) copy-start(f32[128,1152]{1,0:T(8,128)} %copy-done.9) | copy-start | bytes 1769476
  103.9 3.9 %collective-permute-start.9 = (f32[128,1152]{1,0:T(8,128)S(1)}, f32[128,1152]{1,0:T(8,128)S(1)}, u32[]{:S(2)}, u32[]{:S(2)}) collective-permute-start(f32[128,1152]{1,0:T(8,128)S(1)} %get-tuple-element.59), channel_id=1, source_target_pairs={{0,1},{1,0},{2,3},{3,2},{4,5},{5,4},{6,7},{7,6},{8,9},{9,8},{10,11... | collective-permute-start | bytes 1769480 | tf_op jit(solution)/shard_map/ppermute | solution.py:54
  106.1 1.7 %copy-start.1 = (bf16[128,1152]{1,0:T(8,128)(2,1)S(1)}, bf16[128,1152]{1,0:T(8,128)(2,1)}, u32[]{:S(2)}) copy-start(bf16[128,1152]{1,0:T(8,128)(2,1)} %images_ref.3) | copy-start | bytes 884740

commit v6 on v4

--- a/solution.py
+++ b/solution.py
@@ -168,24 +168,21 @@
     other_ref[...] = near_ref[IMAGES:, :] + far_ref[IMAGES:, :]
 
 
-def image_end_kernel(temp_ref, images_ref, mine_ref, got_ref, out_ref):
-    unit, factor = normalized(images_ref[...])
-    scale = jnp.exp(jnp.full((1, WIDTH), temp_ref[0], F32))
-    out_ref[...] = back_normal(unit, factor, scale * (mine_ref[...] + got_ref[...]))
-
-
 def again_kernel(row_ref, out_ref):
     total = jnp.sum(row_ref[...], axis=0, keepdims=True)
     out_ref[...] = jnp.broadcast_to(total, out_ref.shape)
 
 
-def sums_end_kernel(temp_ref, row_ref, loss_ref, temp_grad_ref, bias_grad_ref):
+def end_kernel(temp_ref, images_ref, mine_ref, got_ref, row_ref, image_ref, loss_ref, temp_grad_ref, bias_grad_ref):
     total = jnp.sum(row_ref[...], axis=0)
     lane = lax.broadcasted_iota(jnp.int32, (1, IMAGES), 1)
     scale = jnp.exp(jnp.full((1, IMAGES), temp_ref[0], F32))
     loss_ref[0] = jnp.sum(jnp.where(lane == 0, total, 0.0)) * (1.0 / BATCH)
     bias_grad_ref[0] = jnp.sum(jnp.where(lane == 1, total, 0.0))
     temp_grad_ref[0] = jnp.sum(jnp.where(lane == 2, total * scale, 0.0))
+    unit, factor = normalized(images_ref[...])
+    scale = jnp.exp(jnp.full((1, WIDTH), temp_ref[0], F32))
+    image_ref[...] = back_normal(unit, factor, scale * (mine_ref[...] + got_ref[...]))
 
 
 def per_device(images, texts, positive, temp_log, bias_arg):
@@ -234,12 +231,9 @@
         smem_in=(0,), flops=8 * 10**9,
     )
     mine, text_grad = lax.optimization_barrier((mine, text_grad))
-    (image_grad,) = call(
-        image_end_kernel, [shape(IMAGES, WIDTH)], temp_log, images, mine, other, smem_in=(0,)
-    )
-    row, image_grad, text_grad = lax.optimization_barrier((row, image_grad, text_grad))
-    loss, temp_grad, bias_grad = call(
-        sums_end_kernel, [shape(1)] * 3, temp_log, row, smem_in=(0,), smem_out=(0, 1, 2)
+    image_grad, loss, temp_grad, bias_grad = call(
+        end_kernel, [shape(IMAGES, WIDTH)] + [shape(1)] * 3, temp_log, images, mine, other, row,
+        smem_in=(0,), smem_out=(1, 2, 3),
     )
     return (loss, image_grad, text_grad, temp_grad, bias_grad)
 

time: 111 us -> 111 us (level)
    unnamed x22 -> x26, local copies, waits for them, and re-layouts: 4.38 us -> 5.18 us
    pallas_call x11 -> x10, Pallas kernels: 17.8 us -> 18 us  [call(): pl.pallas_call(body, out_shape=outs, in_specs=[scalar if k in smem_in els...]
  transfers between devices with their start and end apart: 12 -> 12, of which waited for: 3 -> 2; matrix products, arithmetic and copies ran while one was open for 0% -> 0% of each run, Pallas kernels for 15% -> 15%
where the time goes in v6:
time: 111 us; the launch traced here: 110 us
  starting transfers between devices  71.6 us (65%)
  Pallas kernels  18 us (16%)
  waiting for transfers between devices  13.2 us (12%)
  local copies, waits for them, and re-layouts  5.18 us (5%)
  between operations  2.24 us (2%)
    ppermute x6, starting transfers between devices, to_side(): return lax.ppermute(value, BLK + ('core',), pairs)  26.5 us
    ppermute x4, starting transfers between devices, swapped(): return lax.ppermute(value, axis, [(0, 1), (1, 0)])  26.4 us
    pallas_call x10, Pallas kernels, call(): pl.pallas_call(body, out_shape=outs, in_specs=[scalar if k in smem_in els...  18 us
    all_to_all x1, waiting for transfers between devices, per_device(): row = lax.all_to_all(row, 'z', 0, 0, tiled=True)  11.9 us
    all_to_all x1, starting transfers between devices, per_device(): row = lax.all_to_all(row, 'z', 0, 0, tiled=True)  9.75 us
    all_to_all x1, starting transfers between devices, per_device(): row = lax.all_to_all(row, PLANE, 0, 0, tiled=True)  9.04 us
    unnamed x26, local copies, waits for them, and re-layouts  5.18 us
  transfers between devices with their start and end apart: 12, of which 2 were waited for; matrix products, arithmetic and copies ran while one was open for 0% of the time, Pallas kernels for 15%

profile of v6, /device:TPU:1, one launch (start us, length us, event | category | flops | bytes accessed | tf_op | source)
XLA Modules:
  0.0 110.3 jit_solution(7976464590892163485)
XLA Ops:
  0.6 1.0 copy-done.2
  1.6 0.7 copy-done.8
  2.3 0.1 shard_map.92.packed_ref
  2.4 16.1 %collective-permute-start.1 = (bf16[144,1152]{1,0:T(8,128)(2,1)S(1)}, bf16[144,1152]{1,0:T(8,128)(2,1)S(1)}, u32[]{:S(2)}, u32[]{:S(2)}) collective-permute-start(bf16[144,1152]{1,0:T(8,128)(2,1)S(1)} %shard_map.92.packed_ref), channel_id=1, source_target_pairs={{0,1},{1,0},{2,3},{3,2},{4,5},{5,4},{6,7},{7,6},{8,9},{9,8},{10,11... | collective-permute-start | bytes 995336 | tf_op jit(solution)/shard_map/ppermute | solution.py:54
  18.5 9.0 %collective-permute-start = (bf16[144,1152]{1,0:T(8,128)(2,1)S(1)}, bf16[144,1152]{1,0:T(8,128)(2,1)S(1)}, u32[]{:S(2)}, u32[]{:S(2)}) collective-permute-start(bf16[144,1152]{1,0:T(8,128)(2,1)S(1)} %shard_map.92.packed_ref), channel_id=1, source_target_pairs={{0,4},{1,1021},{4,8},{5,1},{8,12},{9,5},{12,16},{13,9},{16,20},{17... | collective-permute-start | bytes 995336 | tf_op jit(solution)/shard_map/ppermute | solution.py:50
  27.4 2.5 %collective-permute-start.2 = (bf16[144,1152]{1,0:T(8,128)(2,1)S(1)}, bf16[144,1152]{1,0:T(8,128)(2,1)S(1)}, u32[]{:S(2)}, u32[]{:S(2)}) collective-permute-start(bf16[144,1152]{1,0:T(8,128)(2,1)S(1)} %collective-permute-done.1), channel_id=1, source_target_pairs={{0,4},{1,1021},{4,8},{5,1},{8,12},{9,5},{12,16},{13,9},{16,20},{17... | collective-permute-start | bytes 995336 | tf_op jit(solution)/shard_map/ppermute | solution.py:50
  31.2 0.1 pad_add_fusion.place_ref
  31.3 1.3 %copy-done = bf16[512,1152]{1,0:T(8,128)(2,1)S(1)} copy-done((bf16[512,1152]{1,0:T(8,128)(2,1)S(1)}, bf16[512,1152]{1,0:T(8,128)(2,1)}, u32[]{:S(2)}) %copy-start) | copy-done | bytes 1179672
  32.6 2.4 %shard_map.93 = (bf16[512,1152]{1,0:T(8,128)(2,1)S(1)}, f32[128,1152]{1,0:T(8,128)S(1)}, f32[512,1152]{1,0:T(8,128)S(1)}, f32[8,128]{1,0:T(8,128)S(1)}) custom-call(bf16[512,1152]{1,0:T(8,128)(2,1)S(1)} %copy-done, bf16[144,1152]{1,0:T(8,128)(2,1)S(1)} %shard_map.92.packed_ref, s32[3]{0:T(128)S(1)} %pad_add_fusion.place_ref, f32[1]{0:T(128)S(6)} %copy.10.temp_ref, ...), custom_call_target="tpu_custom_call" | custom-call | flops 452984832 | bytes 5644308 | tf_op jit(solution)/shard_map/pallas_call | solution.py:33
  35.0 0.0 copy-start.4
  35.0 4.5 %collective-permute-start.4 = (bf16[144,1152]{1,0:T(8,128)(2,1)S(1)}, bf16[144,1152]{1,0:T(8,128)(2,1)S(1)}, u32[]{:S(2)}, u32[]{:S(2)}) collective-permute-start(bf16[144,1152]{1,0:T(8,128)(2,1)S(1)} %collective-permute-done.first_ref), channel_id=1, source_target_pairs={{0,4},{1,1021},{4,8},{5,1},{8,12},{9,5},{12,16},{13,9},{16,20},{17... | collective-permute-start | bytes 995336 | tf_op jit(solution)/shard_map/ppermute | solution.py:50
  39.5 3.5 %collective-permute-start.5 = (bf16[144,1152]{1,0:T(8,128)(2,1)S(1)}, bf16[144,1152]{1,0:T(8,128)(2,1)S(1)}, u32[]{:S(2)}, u32[]{:S(2)}) collective-permute-start(bf16[144,1152]{1,0:T(8,128)(2,1)S(1)} %collective-permute-done.2.second_ref), channel_id=1, source_target_pairs={{0,4},{1,1021},{4,8},{5,1},{8,12},{9,5},{12,16},{13,9},{16,20},{17... | collective-permute-start | bytes 995336 | tf_op jit(solution)/shard_map/ppermute | solution.py:50
  43.1 3.6 %shard_map.94 = (f32[256,1152]{1,0:T(8,128)}, f32[512,1152]{1,0:T(8,128)S(1)}, f32[8,128]{1,0:T(8,128)S(1)}) custom-call(bf16[512,1152]{1,0:T(8,128)(2,1)S(1)} %get-tuple-element.36.text_ref, bf16[144,1152]{1,0:T(8,128)(2,1)S(1)} %collective-permute-done.first_ref, bf16[144,1152]{1,0:T(8,128)(2,1)S(1)} %collective-permute-done.2.second_ref, ...), custom_call_target="tpu_custom_call" | custom-call | flops 905969664 | bytes 7749652 | tf_op jit(solution)/shard_map/pallas_call | solution.py:33
  46.7 1.9 %collective-permute-start.3 = (f32[256,1152]{1,0:T(8,128)}, f32[256,1152]{1,0:T(8,128)S(1)}, u32[]{:S(2)}, u32[]{:S(2)}) collective-permute-start(f32[256,1152]{1,0:T(8,128)} %get-tuple-element.40), channel_id=1, source_target_pairs={{0,1020},{1,5},{4,0},{5,9},{8,4},{9,13},{12,8},{13,17},{16,12},{17... | collective-permute-start | bytes 3538952 | tf_op jit(solution)/shard_map/ppermute | solution.py:50
  48.6 4.6 %shard_map.95 = (f32[256,1152]{1,0:T(8,128)}, f32[2,128,1152]{2,1,0:T(8,128)}, f32[2,128,1152]{2,1,0:T(8,128)S(1)}, f32[32,1,128]{2,1,0:T(1,128)}) custom-call(bf16[512,1152]{1,0:T(8,128)(2,1)S(1)} %get-tuple-element.36.text_ref, bf16[144,1152]{1,0:T(8,128)(2,1)S(1)} %collective-permute-done.4.first_ref, ...), custom_call_target="tpu_custom_call" | custom-call | flops 905969664 | bytes 7761940 | tf_op jit(solution)/shard_map/pallas_call | solution.py:33
  53.2 3.3 %collective-permute-start.6 = (f32[2,128,1152]{2,1,0:T(8,128)}, f32[2,128,1152]{2,1,0:T(8,128)S(1)}, u32[]{:S(2)}, u32[]{:S(2)}) collective-permute-start(f32[2,128,1152]{2,1,0:T(8,128)} %get-tuple-element.43), channel_id=1, source_target_pairs={{0,1},{1,0},{2,3},{3,2},{4,5},{5,4},{6,7},{7,6},{8,9},{9,8},{10,11... | collective-permute-start | bytes 3538952 | tf_op jit(solution)/shard_map/ppermute | solution.py:54
  56.6 5.1 %collective-permute-start.7 = (f32[256,1152]{1,0:T(8,128)}, f32[256,1152]{1,0:T(8,128)}, u32[]{:S(2)}, u32[]{:S(2)}) collective-permute-start(f32[256,1152]{1,0:T(8,128)} %get-tuple-element.45), channel_id=1, source_target_pairs={{0,1016},{1,9},{4,1020},{5,13},{8,0},{9,17},{12,4},{13,21},{16,8},... | collective-permute-start | bytes 3538952 | tf_op jit(solution)/shard_map/ppermute | solution.py:50
  61.7 9.8 %all-to-all-start = ((f32[32,1,128]{2,1,0:T(1,128)}), f32[32,1,128]{2,1,0:T(1,128)S(1)}, u32[]{:S(2)}, u32[]{:S(2)}) async-start(f32[32,1,128]{2,1,0:T(1,128)} %get-tuple-element.47), calls=%async_computation | async-start | bytes 32768 | tf_op jit(solution)/shard_map/all_to_all | solution.py:217
  71.5 0.6 copy-done.7
  72.1 1.5 %shard_map.98 = (f32[128,1152]{1,0:T(8,128)}, f32[128,1152]{1,0:T(8,128)S(1)}) custom-call(s32[3]{0:T(128)S(1)} %copy-done.7, f32[2,128,1152]{2,1,0:T(8,128)S(1)} %get-tuple-element.51.keep_ref, f32[2,128,1152]{2,1,0:T(8,128)S(1)} %collective-permute-done.6.got_ref), custom_call_target="tpu_custom_call" | custom-call | bytes 3538956 | tf_op jit(solution)/shard_map/pallas_call | solution.py:33
  73.6 0.8 copy-done.9
  74.4 4.8 %collective-permute-start.8 = (f32[128,1152]{1,0:T(8,128)}, f32[128,1152]{1,0:T(8,128)S(1)}, u32[]{:S(2)}, u32[]{:S(2)}) collective-permute-start(f32[128,1152]{1,0:T(8,128)} %get-tuple-element.54), channel_id=1, source_target_pairs={{0,2},{2,0},{1,3},{3,1},{4,6},{6,4},{5,7},{7,5},{8,10},{10,8},{9,1... | collective-permute-start | bytes 1769480 | tf_op jit(solution)/shard_map/ppermute | solution.py:54
  79.2 0.7 shard_map.97
  79.9 0.8 copy-done.11
  80.7 11.9 %all-to-all-done.row_ref = f32[32,1,128]{2,1,0:T(1,128)S(1)} async-done(((f32[32,1,128]{2,1,0:T(1,128)}), f32[32,1,128]{2,1,0:T(1,128)S(1)}, u32[]{:S(2)}, u32[]{:S(2)}) %all-to-all-start) | async-done | bytes 16416 | tf_op jit(solution)/shard_map/all_to_all | solution.py:217
  92.6 0.6 shard_map.100
  93.3 9.0 %all-to-all-start.1 = ((f32[32,1,128]{2,1,0:T(1,128)}), f32[32,1,128]{2,1,0:T(1,128)S(1)}, u32[]{:S(2)}, u32[]{:S(2)}) async-start(f32[32,1,128]{2,1,0:T(1,128)} %shard_map.100), calls=%async_computation.1 | async-start | bytes 32768 | tf_op jit(solution)/shard_map/all_to_all | solution.py:226
  102.4 2.3 %shard_map.96 = (f32[128,1152]{1,0:T(8,128)S(1)}, f32[128,1152]{1,0:T(8,128)}) custom-call(f32[128,1152]{1,0:T(8,128)S(1)} %copy-done.5, f32[256,1152]{1,0:T(8,128)S(1)} %collective-permute-done.3.near_ref, f32[256,1152]{1,0:T(8,128)} %collective-permute-done.7.far_ref), custom_call_target="tpu_custom_call" | custom-call | bytes 4128768 | tf_op jit(solution)/shard_map/pallas_call | solution.py:33
  104.7 2.1 %collective-permute-start.9 = (f32[128,1152]{1,0:T(8,128)}, f32[128,1152]{1,0:T(8,128)S(1)}, u32[]{:S(2)}, u32[]{:S(2)}) collective-permute-start(f32[128,1152]{1,0:T(8,128)} %get-tuple-element.56), channel_id=1, source_target_pairs={{0,1},{1,0},{2,3},{3,2},{4,5},{5,4},{6,7},{7,6},{8,9},{9,8},{10,11... | collective-permute-start | bytes 1769480 | tf_op jit(solution)/shard_map/ppermute | solution.py:54
  106.9 1.1 shard_map.99
  107.9 1.3 %all-to-all-done.1.row_ref = f32[32,1,128]{2,1,0:T(1,128)S(1)} async-done(((f32[32,1,128]{2,1,0:T(1,128)}), f32[32,1,128]{2,1,0:T(1,128)S(1)}, u32[]{:S(2)}, u32[]{:S(2)}) %all-to-all-start.1) | async-done | bytes 16416 | tf_op jit(solution)/shard_map/all_to_all | solution.py:226
  109.2 1.1 shard_map.101
  (29 shorter events, 0.1 us)
Async XLA Ops:
  0.6 1.0 copy-start.2
  1.6 0.7 copy-start.8
  2.4 25.0 %collective-permute-start.1 = (bf16[144,1152]{1,0:T(8,128)(2,1)S(1)}, bf16[144,1152]{1,0:T(8,128)(2,1)S(1)}, u32[]{:S(2)}, u32[]{:S(2)}) collective-permute-start(bf16[144,1152]{1,0:T(8,128)(2,1)S(1)} %shard_map.92.packed_ref), channel_id=1, source_target_pairs={{0,1},{1,0},{2,3},{3,2},{4,5},{5,4},{6,7},{7,6},{8,9},{9,8},{10,11... | collective-permute-start | bytes 995336 | tf_op jit(solution)/shard_map/ppermute | solution.py:54
  18.5 16.5 %collective-permute-start = (bf16[144,1152]{1,0:T(8,128)(2,1)S(1)}, bf16[144,1152]{1,0:T(8,128)(2,1)S(1)}, u32[]{:S(2)}, u32[]{:S(2)}) collective-permute-start(bf16[144,1152]{1,0:T(8,128)(2,1)S(1)} %shard_map.92.packed_ref), channel_id=1, source_target_pairs={{0,4},{1,1021},{4,8},{5,1},{8,12},{9,5},{12,16},{13,9},{16,20},{17... | collective-permute-start | bytes 995336 | tf_op jit(solution)/shard_map/ppermute | solution.py:50
  27.4 12.1 %collective-permute-start.2 = (bf16[144,1152]{1,0:T(8,128)(2,1)S(1)}, bf16[144,1152]{1,0:T(8,128)(2,1)S(1)}, u32[]{:S(2)}, u32[]{:S(2)}) collective-permute-start(bf16[144,1152]{1,0:T(8,128)(2,1)S(1)} %collective-permute-done.1), channel_id=1, source_target_pairs={{0,4},{1,1021},{4,8},{5,1},{8,12},{9,5},{12,16},{13,9},{16,20},{17... | collective-permute-start | bytes 995336 | tf_op jit(solution)/shard_map/ppermute | solution.py:50
  31.3 1.3 %copy-start = (bf16[512,1152]{1,0:T(8,128)(2,1)S(1)}, bf16[512,1152]{1,0:T(8,128)(2,1)}, u32[]{:S(2)}) copy-start(bf16[512,1152]{1,0:T(8,128)(2,1)} %texts_ref.3) | copy-start | bytes 3538948
  32.6 16.0 %copy-start.6 = (s32[3]{0:T(128)}, s32[3]{0:T(128)S(1)}, u32[]{:S(2)}) copy-start(s32[3]{0:T(128)S(1)} %pad_add_fusion.place_ref) | copy-start | bytes 40
  35.0 11.7 %copy-start.4 = (f32[128,1152]{1,0:T(8,128)}, f32[128,1152]{1,0:T(8,128)S(1)}, u32[]{:S(2)}) copy-start(f32[128,1152]{1,0:T(8,128)S(1)} %get-tuple-element.34.own_ref) | copy-start | bytes 1769476
  35.0 13.6 %collective-permute-start.4 = (bf16[144,1152]{1,0:T(8,128)(2,1)S(1)}, bf16[144,1152]{1,0:T(8,128)(2,1)S(1)}, u32[]{:S(2)}, u32[]{:S(2)}) collective-permute-start(bf16[144,1152]{1,0:T(8,128)(2,1)S(1)} %collective-permute-done.first_ref), channel_id=1, source_target_pairs={{0,4},{1,1021},{4,8},{5,1},{8,12},{9,5},{12,16},{13,9},{16,20},{17... | collective-permute-start | bytes 995336 | tf_op jit(solution)/shard_map/ppermute | solution.py:50
  39.5 9.1 %collective-permute-start.5 = (bf16[144,1152]{1,0:T(8,128)(2,1)S(1)}, bf16[144,1152]{1,0:T(8,128)(2,1)S(1)}, u32[]{:S(2)}, u32[]{:S(2)}) collective-permute-start(bf16[144,1152]{1,0:T(8,128)(2,1)S(1)} %collective-permute-done.2.second_ref), channel_id=1, source_target_pairs={{0,4},{1,1021},{4,8},{5,1},{8,12},{9,5},{12,16},{13,9},{16,20},{17... | collective-permute-start | bytes 995336 | tf_op jit(solution)/shard_map/ppermute | solution.py:50
  46.7 24.8 %collective-permute-start.3 = (f32[256,1152]{1,0:T(8,128)}, f32[256,1152]{1,0:T(8,128)S(1)}, u32[]{:S(2)}, u32[]{:S(2)}) collective-permute-start(f32[256,1152]{1,0:T(8,128)} %get-tuple-element.40), channel_id=1, source_target_pairs={{0,1020},{1,5},{4,0},{5,9},{8,4},{9,13},{12,8},{13,17},{16,12},{17... | collective-permute-start | bytes 3538952 | tf_op jit(solution)/shard_map/ppermute | solution.py:50
  53.2 18.2 %collective-permute-start.6 = (f32[2,128,1152]{2,1,0:T(8,128)}, f32[2,128,1152]{2,1,0:T(8,128)S(1)}, u32[]{:S(2)}, u32[]{:S(2)}) collective-permute-start(f32[2,128,1152]{2,1,0:T(8,128)} %get-tuple-element.43), channel_id=1, source_target_pairs={{0,1},{1,0},{2,3},{3,2},{4,5},{5,4},{6,7},{7,6},{8,9},{9,8},{10,11... | collective-permute-start | bytes 3538952 | tf_op jit(solution)/shard_map/ppermute | solution.py:54
  56.6 45.7 %collective-permute-start.7 = (f32[256,1152]{1,0:T(8,128)}, f32[256,1152]{1,0:T(8,128)}, u32[]{:S(2)}, u32[]{:S(2)}) collective-permute-start(f32[256,1152]{1,0:T(8,128)} %get-tuple-element.45), channel_id=1, source_target_pairs={{0,1016},{1,9},{4,1020},{5,13},{8,0},{9,17},{12,4},{13,21},{16,8},... | collective-permute-start | bytes 3538952 | tf_op jit(solution)/shard_map/ppermute | solution.py:50
  61.7 30.9 %all-to-all-start = ((f32[32,1,128]{2,1,0:T(1,128)}), f32[32,1,128]{2,1,0:T(1,128)S(1)}, u32[]{:S(2)}, u32[]{:S(2)}) async-start(f32[32,1,128]{2,1,0:T(1,128)} %get-tuple-element.47), calls=%async_computation | async-start | bytes 32768 | tf_op jit(solution)/shard_map/all_to_all | solution.py:217
  71.5 0.7 copy-start.7
  72.1 7.1 %copy-start.1 = (bf16[512,1152]{1,0:T(8,128)(2,1)S(1)}, bf16[512,1152]{1,0:T(8,128)(2,1)}, u32[]{:S(2)}) copy-start(bf16[512,1152]{1,0:T(8,128)(2,1)} %texts_ref.3) | copy-start | bytes 3538948
  73.6 0.8 copy-start.9
  74.4 32.4 %collective-permute-start.8 = (f32[128,1152]{1,0:T(8,128)}, f32[128,1152]{1,0:T(8,128)S(1)}, u32[]{:S(2)}, u32[]{:S(2)}) collective-permute-start(f32[128,1152]{1,0:T(8,128)} %get-tuple-element.54), channel_id=1, source_target_pairs={{0,2},{2,0},{1,3},{3,1},{4,6},{6,4},{5,7},{7,5},{8,10},{10,8},{9,1... | collective-permute-start | bytes 1769480 | tf_op jit(solution)/shard_map/ppermute | solution.py:54
  79.9 0.8 copy-start.11
  92.6 9.7 %copy-start.5 = (f32[128,1152]{1,0:T(8,128)S(1)}, f32[128,1152]{1,0:T(8,128)}, u32[]{:S(2)}) copy-start(f32[128,1152]{1,0:T(8,128)} %copy-done.4) | copy-start | bytes 1769476
  93.3 16.0 %all-to-all-start.1 = ((f32[32,1,128]{2,1,0:T(1,128)}), f32[32,1,128]{2,1,0:T(1,128)S(1)}, u32[]{:S(2)}, u32[]{:S(2)}) async-start(f32[32,1,128]{2,1,0:T(1,128)} %shard_map.100), calls=%async_computation.1 | async-start | bytes 32768 | tf_op jit(solution)/shard_map/all_to_all | solution.py:226
  102.3 4.5 %copy-start.10 = (f32[128,1152]{1,0:T(8,128)S(1)}, f32[128,1152]{1,0:T(8,128)}, u32[]{:S(2)}) copy-start(f32[128,1152]{1,0:T(8,128)} %copy-done.9) | copy-start | bytes 1769476
  102.3 4.5 %copy-start.12 = (f32[128,1152]{1,0:T(8,128)S(1)}, f32[128,1152]{1,0:T(8,128)}, u32[]{:S(2)}) copy-start(f32[128,1152]{1,0:T(8,128)} %copy-done.11) | copy-start | bytes 1769476
  104.7 4.6 %collective-permute-start.9 = (f32[128,1152]{1,0:T(8,128)}, f32[128,1152]{1,0:T(8,128)S(1)}, u32[]{:S(2)}, u32[]{:S(2)}) collective-permute-start(f32[128,1152]{1,0:T(8,128)} %get-tuple-element.56), channel_id=1, source_target_pairs={{0,1},{1,0},{2,3},{3,2},{4,5},{5,4},{6,7},{7,6},{8,9},{9,8},{10,11... | collective-permute-start | bytes 1769480 | tf_op jit(solution)/shard_map/ppermute | solution.py:54
  106.8 2.4 %copy-start.3 = (bf16[128,1152]{1,0:T(8,128)(2,1)S(1)}, bf16[128,1152]{1,0:T(8,128)(2,1)}, u32[]{:S(2)}) copy-start(bf16[128,1152]{1,0:T(8,128)(2,1)} %images_ref.3) | copy-start | bytes 884740
